TPU v7x, 256 devices: a whole 4x4x8 slice. The times are simulated.
256 devices in a mesh: prow: 16 (over y, z_hi), pcol: 16 (over x, z_lo, core).
Axes of the slice: x: 4, y: 4, z: 8 (z_hi: 4, z_lo: 2; z = z_hi * 2 + z_lo), core: 2. Of those that a mesh axis runs over, the one named last changes fastest.
Arguments:
- paper_x: bfloat16 [16384, 768], P(('prow', 'pcol')), may hold values from -6 to 6
- author_x: bfloat16 [16384, 768], P(('pcol', 'prow')), may hold values from -6 to 6
- w_self: bfloat16 [768, 768], replicated, may hold values from -0.21875 to 0.21875
- w_rel: bfloat16 [2, 768, 768], replicated, may hold values from -0.0048828125 to 0.0048828125
- w_two: bfloat16 [768, 768], replicated, may hold values from -0.0048828125 to 0.0048828125
- block_rows: int32 [16, 16, 32], P('prow', 'pcol'), may hold values from 0 to 7, as said below
- block_cols: int32 [16, 16, 32], P('prow', 'pcol'), may hold values from 0 to 7, as said below
- block_type: int32 [16, 16, 32], P('prow', 'pcol'), may hold values from 0 to 1
- block_count: int32 [16, 16], P('prow', 'pcol'), may hold values from 8 to 32, as said below
- block_vals: bfloat16 [16, 16, 32, 128, 128], P('prow', 'pcol'), may hold values from 0 to 1, as said below
Outputs:
- paper_hidden: bfloat16 [16384, 768], P(('prow', 'pcol'))
- author_out: bfloat16 [16384, 768], P(('pcol', 'prow'))
Inputs may be any that keep to these rules, and one draw needn't show every extreme that they name: `block_rows`: within one tile the live and dead slots name distinct positions; block rows are below 8. `block_cols`: block columns are below 8; with block_rows, positions of one tile are distinct. `block_count`: slots 0 to count - 1 of a tile are live; some tile holds 32 live slots and some tile 32 // 4 in every draw. `block_vals`: every entry is 0 or 1.
All inputs are finite; a program needn't handle non-finite values.
Results may differ from a plain program's by a relative error of at most 0.0041.
Values may be sent and summed in bfloat16 or wider, within the bound.
No kernel may reach another device: no remote copies, remote signals or barrier semaphores. Data moves between devices by JAX's collectives and lax.ppermute only.
A program may use at most 64 MiB of HBM per device.

v0:
```python
import jax
import jax.numpy as jnp
from jax import lax
from jax.sharding import PartitionSpec as P

GROUP = 16


def per_device(
    paper_x,
    author_x,
    w_self,
    w_rel,
    w_two,
    block_rows,
    block_cols,
    block_type,
    block_count,
    block_vals,
):
    slots = block_rows.shape[2]
    side = block_vals.shape[3]
    width = paper_x.shape[1]
    relations = w_rel.shape[0]
    groups = slots // GROUP
    own_rows = paper_x.shape[0]
    row_ids = block_rows.reshape(groups, GROUP)
    col_ids = block_cols.reshape(groups, GROUP)
    type_ids = block_type.reshape(groups, GROUP)
    live = (
        (jnp.arange(slots, dtype=jnp.int32) < block_count.reshape(()))
        .astype(jnp.float32)
        .reshape(groups, GROUP)
    )
    contents = block_vals.reshape(groups, GROUP, side, side)
    self_term = jnp.dot(paper_x, w_self, preferred_element_type=jnp.float32)
    own_msgs = jnp.stack(
        [
            jnp.dot(author_x, w_rel[index], preferred_element_type=jnp.float32)
            for index in range(relations)
        ]
    ).astype(jnp.bfloat16)
    messages = lax.all_gather(own_msgs, "prow", axis=1, tiled=True)
    col_blocks = messages.shape[1] // side
    row_blocks = own_rows * lax.axis_size("pcol") // side
    table = messages.reshape(relations * col_blocks, side, width)
    row_range = jnp.arange(row_blocks, dtype=jnp.int32)
    col_range = jnp.arange(col_blocks, dtype=jnp.int32)

    def first_hop(total, item):
        rows_now, cols_now, types_now, mask_now, content_now = item
        picked = table[types_now * col_blocks + cols_now]
        product = jnp.einsum(
            "kpa,kaf->kpf", content_now, picked, preferred_element_type=jnp.float32
        )
        placing = (rows_now[:, None] == row_range[None, :]).astype(jnp.float32) * mask_now[:, None]
        return (
            total + jnp.einsum("kr,kpf->rpf", placing, product, precision=lax.Precision.HIGHEST),
            None,
        )

    start = jnp.zeros((row_blocks, side, width), jnp.float32)
    partial_value, _ = lax.scan(first_hop, start, (row_ids, col_ids, type_ids, live, contents))
    partial_value = partial_value.reshape(row_blocks * side, width)
    summed = lax.psum_scatter(partial_value, "pcol", scatter_dimension=0, tiled=True)
    paper_hidden = jnp.maximum(self_term + summed, 0.0).astype(jnp.bfloat16)
    outgoing = jnp.dot(paper_hidden, w_two, preferred_element_type=jnp.float32).astype(jnp.bfloat16)
    paper_rows = lax.all_gather(outgoing, "pcol", axis=0, tiled=True).reshape(
        row_blocks, side, width
    )

    def second_hop(total, item):
        rows_now, cols_now, mask_now, content_now = item
        picked = paper_rows[rows_now]
        product = jnp.einsum(
            "kpa,kpf->kaf", content_now, picked, preferred_element_type=jnp.float32
        )
        placing = (cols_now[:, None] == col_range[None, :]).astype(jnp.float32) * mask_now[:, None]
        return (
            total + jnp.einsum("kc,kaf->caf", placing, product, precision=lax.Precision.HIGHEST),
            None,
        )

    start_two = jnp.zeros((col_blocks, side, width), jnp.float32)
    author_part, _ = lax.scan(second_hop, start_two, (row_ids, col_ids, live, contents))
    author_total = lax.psum_scatter(
        author_part.reshape(col_blocks * side, width), "prow", scatter_dimension=0, tiled=True
    )
    return (paper_hidden, author_total.astype(jnp.bfloat16))


def solution(mesh):
    return jax.shard_map(
        per_device,
        mesh=mesh,
        in_specs=(
            P(("prow", "pcol"), None),
            P(("pcol", "prow"), None),
            P(),
            P(),
            P(),
            P("prow", "pcol", None),
            P("prow", "pcol", None),
            P("prow", "pcol", None),
            P("prow", "pcol"),
            P("prow", "pcol", None, None, None),
        ),
        out_specs=(P(("prow", "pcol"), None), P(("pcol", "prow"), None)),
        check_vma=False,
    )
```

profile of v0, /device:TPU:64, one launch (start us, length us, event | category | flops | bytes accessed | tf_op | source)
XLA Modules:
  0.0 375.9 jit_solution(17906923748152827027)
XLA Ops:
  7.2 0.0 copy-start
  7.2 0.0 copy-start.4
  7.2 0.0 copy-start.5
  7.2 0.0 copy-start.6
  7.2 0.0 copy-start.1
  7.2 0.0 all-gather.3.cloned.1.call-start
  7.3 1.8 fusion.55
  9.1 1.7 fusion.58
  10.7 0.7 pad_maximum_fusion
  11.4 0.0 all-gather.3.cloned.1.call-update
  11.4 0.0 reduce-scatter.3.cloned.1.call-start
  11.5 0.5 broadcast.116
  12.0 0.0 copy-done.4
  12.0 0.7 reduce.9
  12.7 0.1 reshape.103
  12.8 0.0 copy-done.5
  12.8 0.7 reduce.11
  13.4 0.1 reshape.107
  13.5 0.0 copy-done.6
  13.5 0.7 reduce.10
  14.2 0.1 reshape.106
  14.9 66.1 %all-gather.3.cloned.1.call-done = bf16[2,1024,768]{2,1,0:T(8,128)(2,1)} async-done(((bf16[2,64,768]{2,1,0:T(8,128)(2,1)}), bf16[2,1024,768]{2,1,0:T(8,128)(2,1)}) %all-gather.3.cloned.1.call-update) | async-done | bytes 3145744 | tf_op jit(solution)/shard_map/all_gather | solution.py:43
  81.1 0.0 copy-done.1
  81.1 42.0 %while.22 = (s32[]{:T(128)}, f32[8,128,768]{2,0,1:T(8,128)}, s32[2,16]{1,0:T(2,128)S(1)}, f32[2,16]{1,0:T(2,128)S(1)}, bf16[2,16,128,128]{3,2,1,0:T(8,128)(2,1)S...) while((s32[]{:T(128)}, f32[8,128,768]{2,0,1:T(8,128)}, ...), condition=%wide.region_1.2_spmd.clone, body=%wide.region_0.1_spmd.clone.sunk | while | flops 555222400 | bytes 28840768 | solution.py:63
  81.1 4.3 %gather_fusion = bf16[16,128,768]{2,1,0:T(8,128)(2,1)} fusion(bf16[16,128,768]{2,1,0:T(8,128)(2,1)} %get-tuple-element.297, s32[1024]{0:T(1024)S(1)} %pad_clamp_fusion.4), kind=kCustom, calls=%fused_computation.clone.clone.1 | custom fusion | bytes 6291520 | tf_op jit(solution)/shard_map/while/body/eval_jaxpr/gather | solution.py:52
  85.4 5.5 %fusion.90 = f32[16,128,768]{2,1,0:T(8,128)} fusion(bf16[16,128,768]{2,1,0:T(8,128)(2,1)} %gather_fusion, bf16[2,16,128,128]{3,2,1,0:T(8,128)(2,1)S(1)} %get-tuple-element.294, s32[]{:T(128)} %get-tuple-element.280), kind=kOutput, calls=%fused_computation.7.clone.1 | convolution fusion | flops 402653184 | bytes 9961476 | tf_op jit(solution)/shard_map/while/body/eval_jaxpr/kpa,kaf->kpf/dot_general | solution.py:53
  90.9 10.9 %select_add_fusion.4 = f32[8,128,768]{2,0,1:T(8,128)} fusion(f32[8,128,768]{2,0,1:T(8,128)} %get-tuple-element.281, f32[16,128,768]{2,1,0:T(8,128)} %fusion.90, pred[]{:T(512)S(6)} %compare.6, f32[16]{0:T(128)S(1)} %fusion.91, s32[16]{0:T(128)S(1)} %fusion.92), kind=kOutput, calls=%fused_computation.6.clone.1 | convolution fusion | flops 152568064 | bytes 12583041 | tf_op jit(solution)/shard_map/while/body/eval_jaxpr/kr,kpf->rpf/dot_general | solution.py:58
  101.9 4.3 %gather_fusion = bf16[16,128,768]{2,1,0:T(8,128)(2,1)} fusion(bf16[16,128,768]{2,1,0:T(8,128)(2,1)} %get-tuple-element.297, s32[1024]{0:T(1024)S(1)} %pad_clamp_fusion.4), kind=kCustom, calls=%fused_computation.clone.clone.1 | custom fusion | bytes 6291520 | tf_op jit(solution)/shard_map/while/body/eval_jaxpr/gather | solution.py:52
  106.2 5.5 %fusion.90 = f32[16,128,768]{2,1,0:T(8,128)} fusion(bf16[16,128,768]{2,1,0:T(8,128)(2,1)} %gather_fusion, bf16[2,16,128,128]{3,2,1,0:T(8,128)(2,1)S(1)} %get-tuple-element.294, s32[]{:T(128)} %get-tuple-element.280), kind=kOutput, calls=%fused_computation.7.clone.1 | convolution fusion | flops 402653184 | bytes 9961476 | tf_op jit(solution)/shard_map/while/body/eval_jaxpr/kpa,kaf->kpf/dot_general | solution.py:53
  111.7 11.4 %select_add_fusion.4 = f32[8,128,768]{2,0,1:T(8,128)} fusion(f32[8,128,768]{2,0,1:T(8,128)} %get-tuple-element.281, f32[16,128,768]{2,1,0:T(8,128)} %fusion.90, pred[]{:T(512)S(6)} %compare.6, f32[16]{0:T(128)S(1)} %fusion.91, s32[16]{0:T(128)S(1)} %fusion.92), kind=kOutput, calls=%fused_computation.6.clone.1 | convolution fusion | flops 152568064 | bytes 12583041 | tf_op jit(solution)/shard_map/while/body/eval_jaxpr/kr,kpf->rpf/dot_general | solution.py:58
  123.1 4.6 %copy.12 = f32[8,128,768]{2,1,0:T(8,128)} copy(f32[8,128,768]{2,0,1:T(8,128)} %get-tuple-element.91) | data formatting | bytes 6291456 | tf_op jit(solution)/shard_map/while | solution.py:63
  127.6 0.0 copy-start.2
  127.6 0.0 reduce-scatter.3.cloned.1.call-update
  127.7 0.0 all-gather.5.cloned.1.call-start
  127.7 68.1 %reduce-scatter.3.cloned.1.call-done = f32[64,768]{1,0:T(8,128)} async-done(((f32[1024,768]{1,0:T(8,128)}), f32[64,768]{1,0:T(8,128)}) %reduce-scatter.3.cloned.1.call-update) | async-done | bytes 196624 | tf_op jit(solution)/shard_map/reduce_scatter | solution.py:65
  195.8 0.0 copy-done
  195.8 1.3 fusion.54
  197.1 0.0 copy-done.2
  197.1 0.0 copy-start.3
  197.1 1.0 convolution_convert_fusion
  198.1 0.0 all-gather.5.cloned.1.call-update
  198.1 0.2 reduce-scatter.5.cloned.1.call-start
  198.3 33.6 %all-gather.5.cloned.1.call-done = bf16[1024,768]{1,0:T(8,128)(2,1)} async-done(((bf16[64,768]{1,0:T(8,128)(2,1)}), bf16[1024,768]{1,0:T(8,128)(2,1)}) %all-gather.5.cloned.1.call-update) | async-done | bytes 1572880 | tf_op jit(solution)/shard_map/all_gather | solution.py:68
  232.0 0.0 copy-done.3
  232.0 41.3 %while.23 = (s32[]{:T(128)}, f32[8,128,768]{2,0,1:T(8,128)}, s32[2,16]{1,0:T(2,128)S(1)}, f32[2,16]{1,0:T(2,128)S(1)}, bf16[2,16,128,128]{3,2,1,0:T(8,128)(2,1)S...) while((s32[]{:T(128)}, f32[8,128,768]{2,0,1:T(8,128)}, ...), condition=%wide.region_4.5_spmd.clone, body=%wide.region_3.4_spmd.clone.sunk | while | flops 555222336 | bytes 28840696 | solution.py:85
  232.0 3.8 %gather_fusion.1 = bf16[16,128,768]{2,1,0:T(8,128)(2,1)} fusion(bf16[8,128,768]{2,1,0:T(8,128)(2,1)} %get-tuple-element.324, s32[1024]{0:T(1024)S(1)} %pad_clamp_fusion.5), kind=kCustom, calls=%fused_computation.1.clone.clone.1 | custom fusion | bytes 6291520 | tf_op jit(solution)/shard_map/while/body/eval_jaxpr/gather | solution.py:74
  235.8 5.6 %fusion.98 = f32[16,128,768]{2,1,0:T(8,128)} fusion(bf16[16,128,768]{2,1,0:T(8,128)(2,1)} %gather_fusion.1, bf16[2,16,128,128]{3,2,1,0:T(8,128)(2,1)S(1)} %get-tuple-element.322, s32[]{:T(128)} %get-tuple-element.309), kind=kOutput, calls=%fused_computation.32.clone.1 | convolution fusion | flops 402653184 | bytes 9961476 | tf_op jit(solution)/shard_map/while/body/eval_jaxpr/kpa,kpf->kaf/dot_general | solution.py:75
  241.4 11.0 %select_add_fusion.5 = f32[8,128,768]{2,0,1:T(8,128)} fusion(f32[8,128,768]{2,0,1:T(8,128)} %get-tuple-element.310, f32[16,128,768]{2,1,0:T(8,128)} %fusion.98, pred[]{:T(512)S(6)} %compare.7, f32[16]{0:T(128)S(1)} %fusion.99, s32[16]{0:T(128)S(1)} %fusion.100), kind=kOutput, calls=%fused_computation.31.clone.1 | convolution fusion | flops 152568064 | bytes 12583041 | tf_op jit(solution)/shard_map/while/body/eval_jaxpr/kc,kaf->caf/dot_general | solution.py:80
  252.4 3.8 %gather_fusion.1 = bf16[16,128,768]{2,1,0:T(8,128)(2,1)} fusion(bf16[8,128,768]{2,1,0:T(8,128)(2,1)} %get-tuple-element.324, s32[1024]{0:T(1024)S(1)} %pad_clamp_fusion.5), kind=kCustom, calls=%fused_computation.1.clone.clone.1 | custom fusion | bytes 6291520 | tf_op jit(solution)/shard_map/while/body/eval_jaxpr/gather | solution.py:74
  256.2 5.6 %fusion.98 = f32[16,128,768]{2,1,0:T(8,128)} fusion(bf16[16,128,768]{2,1,0:T(8,128)(2,1)} %gather_fusion.1, bf16[2,16,128,128]{3,2,1,0:T(8,128)(2,1)S(1)} %get-tuple-element.322, s32[]{:T(128)} %get-tuple-element.309), kind=kOutput, calls=%fused_computation.32.clone.1 | convolution fusion | flops 402653184 | bytes 9961476 | tf_op jit(solution)/shard_map/while/body/eval_jaxpr/kpa,kpf->kaf/dot_general | solution.py:75
  261.8 11.4 %select_add_fusion.5 = f32[8,128,768]{2,0,1:T(8,128)} fusion(f32[8,128,768]{2,0,1:T(8,128)} %get-tuple-element.310, f32[16,128,768]{2,1,0:T(8,128)} %fusion.98, pred[]{:T(512)S(6)} %compare.7, f32[16]{0:T(128)S(1)} %fusion.99, s32[16]{0:T(128)S(1)} %fusion.100), kind=kOutput, calls=%fused_computation.31.clone.1 | convolution fusion | flops 152568064 | bytes 12583041 | tf_op jit(solution)/shard_map/while/body/eval_jaxpr/kc,kaf->caf/dot_general | solution.py:80
  273.2 4.6 %copy.13 = f32[8,128,768]{2,1,0:T(8,128)} copy(f32[8,128,768]{2,0,1:T(8,128)} %get-tuple-element.92) | data formatting | bytes 6291456 | tf_op jit(solution)/shard_map/while | solution.py:85
  277.8 0.0 reduce-scatter.5.cloned.1.call-update
  277.8 90.0 %reduce-scatter.5.cloned.1.call-done = f32[64,768]{1,0:T(8,128)} async-done(((f32[1024,768]{1,0:T(8,128)}), f32[64,768]{1,0:T(8,128)}) %reduce-scatter.5.cloned.1.call-update) | async-done | bytes 196624 | tf_op jit(solution)/shard_map/reduce_scatter | solution.py:86
  367.8 1.6 convert_element_type.19
  (19 shorter events, 0.1 us)
Async XLA Ops:
  7.2 188.6 %copy-start = (bf16[768,768]{1,0:T(8,128)(2,1)S(1)}, bf16[768,768]{1,0:T(8,128)(2,1)}, u32[]{:S(2)}) copy-start(bf16[768,768]{1,0:T(8,128)(2,1)} %param.16) | copy-start | bytes 3538948
  7.2 4.8 %copy-start.4 = (s32[1,1,32]{2,1,0:T(1,128)S(1)}, s32[1,1,32]{2,1,0:T(1,128)}, u32[]{:S(2)}) copy-start(s32[1,1,32]{2,1,0:T(1,128)} %param.19) | copy-start | bytes 388
  7.2 5.6 %copy-start.5 = (s32[1,1,32]{2,1,0:T(1,128)S(1)}, s32[1,1,32]{2,1,0:T(1,128)}, u32[]{:S(2)}) copy-start(s32[1,1,32]{2,1,0:T(1,128)} %param.20) | copy-start | bytes 388
  7.2 6.3 %copy-start.6 = (s32[1,1,32]{2,1,0:T(1,128)S(1)}, s32[1,1,32]{2,1,0:T(1,128)}, u32[]{:S(2)}) copy-start(s32[1,1,32]{2,1,0:T(1,128)} %param.21) | copy-start | bytes 388
  7.2 73.9 %copy-start.1 = (bf16[1,1,32,128,128]{4,3,2,1,0:T(8,128)(2,1)S(1)}, bf16[1,1,32,128,128]{4,3,2,1,0:T(8,128)(2,1)}, u32[]{:S(2)}) copy-start(bf16[1,1,32,128,128]{4,3,2,1,0:T(8,128)(2,1)} %param.23) | copy-start | bytes 3145732
  7.2 73.8 %all-gather.3.cloned.1.call-start = ((), (), s32[]{:S(2)}) async-start(), calls=%async_computation.2 | async-start | bytes 3342336 | tf_op jit(solution)/shard_map/all_gather | solution.py:43
  11.4 184.3 %reduce-scatter.3.cloned.1.call-start = ((), (), s32[]{:S(2)}) async-start(), calls=%async_computation.3 | async-start | bytes 3342336 | tf_op jit(solution)/shard_map/reduce_scatter | solution.py:65
  127.6 69.5 %copy-start.2 = (bf16[768,768]{1,0:T(8,128)(2,1)S(1)}, bf16[768,768]{1,0:T(8,128)(2,1)}, u32[]{:S(2)}) copy-start(bf16[768,768]{1,0:T(8,128)(2,1)} %param.18) | copy-start | bytes 3538948
  127.7 104.3 %all-gather.5.cloned.1.call-start = ((), (), s32[]{:S(2)}) async-start(), calls=%async_computation.4 | async-start | bytes 1671168 | tf_op jit(solution)/shard_map/all_gather | solution.py:68
  197.1 34.9 %copy-start.3 = (bf16[64,768]{1,0:T(8,128)(2,1)}, bf16[64,768]{1,0:T(8,128)(2,1)S(1)}, u32[]{:S(2)}) copy-start(bf16[64,768]{1,0:T(8,128)(2,1)S(1)} %fusion.54) | copy-start | bytes 294916
  198.1 169.7 %reduce-scatter.5.cloned.1.call-start = ((), (), s32[]{:S(2)}) async-start(), calls=%async_computation.5 | async-start | bytes 3342336 | tf_op jit(solution)/shard_map/reduce_scatter | solution.py:86
Sparse Core Ops, SparseCore 0:
  11.6 69.4 all-gather.2
  127.8 67.9 reduce-scatter.2
  198.2 33.6 all-gather.4
  277.9 89.8 reduce-scatter.4
where the time goes:
time: 379 us; the launch traced here: 376 us
  waiting for transfers between devices  258 us (68%)
  matrix products  72.6 us (19%)
  local copies, waits for them, and re-layouts  26.1 us (7%)
  between operations  14.5 us (4%)
  other arithmetic  4.33 us (1%)
    reduce_scatter x1, waiting for transfers between devices, per_device(): lax.psum_scatter(author_part.reshape(col_blocks * side, width), 'prow', s...  90 us
    reduce_scatter x1, waiting for transfers between devices, per_device(): lax.psum_scatter(partial_value, 'pcol', scatter_dimension=0, tiled=True)  68.1 us
    all_gather x1, waiting for transfers between devices, per_device(): messages = lax.all_gather(own_msgs, 'prow', axis=1, tiled=True)  66.1 us
    all_gather x1, waiting for transfers between devices, per_device(): lax.all_gather(outgoing, 'pcol', axis=0, tiled=True)  33.6 us
    dot_general x2, matrix products, second_hop(): jnp.einsum('kc,kaf->caf', placing, product, precision=lax.Precision.HIGHEST)  22.4 us
    dot_general x2, matrix products, first_hop(): jnp.einsum('kr,kpf->rpf', placing, product, precision=lax.Precision.HIGHEST)  22.3 us
    dot_general x2, matrix products, second_hop(): jnp.einsum('kpa,kpf->kaf', content_now, picked, preferred_element_type=jn...  11.2 us
    dot_general x2, matrix products, first_hop(): jnp.einsum('kpa,kaf->kpf', content_now, picked, preferred_element_type=jn...  11 us
  transfers between devices with their start and end apart: 4, of which 4 were waited for; matrix products, arithmetic and copies ran while one was open for 1% of the time, Pallas kernels for 0%

commit v1 on v0

v1 whole, which is shorter than its diff:
```python
import jax
import jax.numpy as jnp
from jax import lax
from jax.experimental import pallas as pl
from jax.experimental.pallas import tpu as pltpu
from jax.sharding import Mesh
from jax.sharding import PartitionSpec as P

PROW = ("y", "zh")
CHIPS = ("x", "zl")
F32 = jnp.float32
BF16 = jnp.bfloat16
VMEM_LIMIT = 48 * 2**20


def hop_one(rows, cols, types, count, core, x_ref, w_ref, vals_ref, keep_ref, send_ref, msgs, acc):
    relations = w_ref.shape[0]
    tile = 256
    col_blocks = acc.shape[0]
    side = acc.shape[1]
    half = side // 2

    @pl.loop(0, x_ref.shape[0] // tile)
    def _(step):
        at = pl.ds(pl.multiple_of(step * tile, tile), tile)
        x = x_ref[at, :]
        for r in range(relations):
            msgs[r, at, :] = jnp.dot(x, w_ref[r], preferred_element_type=F32).astype(BF16)

    acc[...] = jnp.zeros_like(acc)

    def slot(k, carry):
        picked = msgs[types[k], pl.ds(pl.multiple_of(cols[k] * side, side), side), :]
        acc[rows[k]] += jnp.dot(vals_ref[k], picked, preferred_element_type=F32)
        return carry

    lax.fori_loop(0, count[0], slot, 0)
    mine = pl.multiple_of(core[0] * half, half)
    other = pl.multiple_of((1 - core[0]) * half, half)

    @pl.loop(0, col_blocks)
    def _(r):
        keep_ref[r] = acc[r, pl.ds(mine, half), :].astype(BF16)
        send_ref[r] = acc[r, pl.ds(other, half), :].astype(BF16)


def hop_two(rows, cols, count, core, mine_ref, other_ref, vals_ref, out_ref, table, acc):
    row_blocks, side, _ = table.shape
    half = side // 2
    mine = pl.multiple_of(core[0] * half, half)
    other = pl.multiple_of((1 - core[0]) * half, half)

    @pl.loop(0, row_blocks)
    def _(r):
        table[r, pl.ds(mine, half), :] = mine_ref[r]
        table[r, pl.ds(other, half), :] = other_ref[r]

    acc[...] = jnp.zeros_like(acc)

    def slot(k, carry):
        acc[cols[k]] += lax.dot_general(
            vals_ref[k], table[rows[k]], (((0,), (0,)), ((), ())), preferred_element_type=F32
        )
        return carry

    lax.fori_loop(0, count[0], slot, 0)
    out_ref[...] = acc[...].astype(BF16)


def hidden_step(got_ref, self_ref, w_ref, hidden_ref, out_ref):
    total = self_ref[...]
    for i in range(got_ref.shape[0]):
        total += got_ref[i].astype(F32)
    hidden = jnp.maximum(total, 0.0).astype(BF16)
    hidden_ref[...] = hidden
    out_ref[...] = jnp.dot(hidden, w_ref[...], preferred_element_type=F32).astype(BF16)


def spec(kind):
    return pl.BlockSpec(memory_space=kind)


def call(kernel, scalars, arrays, out_shape, scratch):
    return pl.pallas_call(
        kernel,
        out_shape=out_shape,
        in_specs=[spec(pltpu.SMEM)] * len(scalars) + [spec(pltpu.VMEM)] * len(arrays),
        out_specs=jax.tree.map(lambda _: spec(pltpu.VMEM), out_shape),
        scratch_shapes=scratch,
        compiler_params=pltpu.CompilerParams(vmem_limit_bytes=VMEM_LIMIT),
    )(*scalars, *arrays)


def exchange(value):
    return lax.ppermute(value, "core", [(0, 1), (1, 0)])


def to_all(value, axes, size):
    return lax.all_to_all(jnp.broadcast_to(value[None], (size, *value.shape)), axes, 0, 0, tiled=True)


def per_device(paper_x, author_x, w_self, w_rel, w_two, block_rows, block_cols, block_type, block_count, block_vals):
    slots = block_rows.shape[2]
    side = block_vals.shape[3]
    own, width = paper_x.shape
    chips = lax.axis_size(CHIPS)
    prows = lax.axis_size(PROW)
    rows, cols, types = (a.reshape(slots) for a in (block_rows, block_cols, block_type))
    count = block_count.reshape(1)
    vals = block_vals.reshape(slots, side, side)
    core = lax.axis_index("core").astype(jnp.int32).reshape(1)
    row_blocks = chips * 2 * own // side
    col_blocks = prows * own // side

    authors = to_all(author_x, PROW, prows).reshape(prows * own, width)
    self_term = jnp.dot(paper_x, w_self, preferred_element_type=F32)
    part = jax.ShapeDtypeStruct((row_blocks, side // 2, width), BF16)
    keep, send = call(
        hop_one,
        (rows, cols, types, count, core),
        (authors, w_rel, vals),
        (part, part),
        [pltpu.VMEM((w_rel.shape[0], prows * own, width), BF16), pltpu.VMEM((row_blocks, side, width), F32)],
    )
    pair = (keep.astype(F32) + exchange(send).astype(F32)).astype(BF16)
    got = lax.all_to_all(pair, CHIPS, 0, 0, tiled=True)
    rows_out = jax.ShapeDtypeStruct((own, width), BF16)
    paper_hidden, outgoing = call(hidden_step, (), (got, self_term, w_two), (rows_out, rows_out), [])
    mine = to_all(outgoing, CHIPS, chips)
    other = exchange(mine)
    author_part = call(
        hop_two,
        (rows, cols, count, core),
        (mine, other, vals),
        jax.ShapeDtypeStruct((col_blocks, side, width), BF16),
        [pltpu.VMEM((row_blocks, side, width), BF16), pltpu.VMEM((col_blocks, side, width), F32)],
    )
    pieces = lax.all_to_all(author_part.reshape(prows, own, width), PROW, 0, 0, tiled=True)
    return paper_hidden, pieces.astype(F32).sum(0).astype(BF16)


def solution(mesh):
    split = Mesh(mesh.devices.reshape(4, 4, 4, 2, 2), (*PROW, *CHIPS, "core"))
    pcol = (*CHIPS, "core")
    tile = P(PROW, pcol)
    return jax.shard_map(
        per_device,
        mesh=split,
        in_specs=(P((*PROW, *pcol)), P((*pcol, *PROW)), P(), P(), P(), tile, tile, tile, tile, tile),
        out_specs=(P((*PROW, *pcol)), P((*pcol, *PROW))),
        check_vma=False,
    )
```

time: 379 us -> 162 us (0.43)
  waiting for transfers between devices: 258 us -> 54.2 us
  matrix products: 72.6 us -> 0.33 us
  blocking collectives: 0 us -> 59.8 us
  local copies, waits for them, and re-layouts: 26.1 us -> 3.61 us
  Pallas kernels: 0 us -> 21.3 us
  starting transfers between devices: 0.34 us -> 17.6 us
  between operations: 14.5 us -> 1.36 us
    reduce_scatter x2 -> x0, waiting for transfers between devices: 158 us -> none  [the longest x1 90 us: per_device(): lax.psum_scatter(author_part.reshape(col_blocks * side, width), 'prow', s...]
    all_gather x2 -> x0, waiting for transfers between devices: 99.7 us -> none  [the longest x1 66.1 us: per_device(): messages = lax.all_gather(own_msgs, 'prow', axis=1, tiled=True)]
    dot_general x12 -> x1, matrix products: 72.6 us -> 0.33 us  [per_device(): self_term = jnp.dot(paper_x, w_self, preferred_element_type=F32)]
    all_to_all x0 -> x2, blocking collectives: none -> 59.8 us  [the longest x1 44 us: per_device(): lax.all_to_all(author_part.reshape(prows, own, width), PROW, 0, 0, tiled=...]
    all_to_all x0 -> x2, waiting for transfers between devices: none -> 49.6 us  [the longest x1 36.8 us: to_all(): lax.all_to_all(jnp.broadcast_to(value[None], (size, *value.shape)), axes,...]
    pallas_call x0 -> x3, Pallas kernels: none -> 21.3 us  [call(): pl.pallas_call(kernel, out_shape=out_shape, in_specs=[spec(pltpu.SMEM)] *...]
    all_to_all x0 -> x2, starting transfers between devices: none -> 17.5 us  [the longest x1 10.9 us: to_all(): lax.all_to_all(jnp.broadcast_to(value[None], (size, *value.shape)), axes,...]
    gather x4 -> x0, local copies, waits for them, and re-layouts: 16.2 us -> none  [the longest x2 8.57 us: first_hop(): picked = table[types_now * col_blocks + cols_now]]
  transfers between devices with their start and end apart: 4 -> 4, of which waited for: 4 -> 4; matrix products, arithmetic and copies ran while one was open for 1% -> 0% of each run, Pallas kernels for 0% -> 0%
where the time goes in v1:
time: 162 us; the launch traced here: 160 us
  blocking collectives  59.8 us (37%)
  waiting for transfers between devices  54.2 us (33%)
  Pallas kernels  21.3 us (13%)
  starting transfers between devices  17.6 us (11%)
  local copies, waits for them, and re-layouts  3.61 us (2%)
  other arithmetic  1.95 us (1%)
    all_to_all x1, blocking collectives, per_device(): lax.all_to_all(author_part.reshape(prows, own, width), PROW, 0, 0, tiled=...  44 us
    all_to_all x1, waiting for transfers between devices, to_all(): lax.all_to_all(jnp.broadcast_to(value[None], (size, *value.shape)), axes,...  36.8 us
    pallas_call x3, Pallas kernels, call(): pl.pallas_call(kernel, out_shape=out_shape, in_specs=[spec(pltpu.SMEM)] *...  21.3 us
    all_to_all x1, blocking collectives, to_all(): lax.all_to_all(jnp.broadcast_to(value[None], (size, *value.shape)), axes,...  15.8 us
    all_to_all x1, waiting for transfers between devices, per_device(): got = lax.all_to_all(pair, CHIPS, 0, 0, tiled=True)  12.8 us
    all_to_all x1, starting transfers between devices, to_all(): lax.all_to_all(jnp.broadcast_to(value[None], (size, *value.shape)), axes,...  10.9 us
    all_to_all x1, starting transfers between devices, per_device(): got = lax.all_to_all(pair, CHIPS, 0, 0, tiled=True)  6.57 us
    ppermute x2, waiting for transfers between devices, exchange(): return lax.ppermute(value, 'core', [(0, 1), (1, 0)])  4.55 us
  transfers between devices with their start and end apart: 4, of which 4 were waited for; matrix products, arithmetic and copies ran while one was open for 0% of the time, Pallas kernels for 0%

profile of v1, /device:TPU:64, one launch (start us, length us, event | category | flops | bytes accessed | tf_op | source)
XLA Modules:
  0.0 160.1 jit_solution(9975542858362251710)
XLA Ops:
  0.6 0.0 copy-start
  0.6 2.3 %broadcast_in_dim.4 = bf16[16,64,768]{2,1,0:T(8,128)(2,1)} broadcast(bf16[64,768]{1,0:T(8,128)(2,1)} %param.11), dimensions={1,2} | broadcast | bytes 1671168 | tf_op jit(solution)/shard_map/broadcast_in_dim | solution.py:99
  3.0 0.0 copy-start.4
  3.0 0.0 copy-start.5
  3.0 0.0 copy-start.6
  3.0 10.9 %all-to-all-start = ((bf16[16,64,768]{2,1,0:T(8,128)(2,1)}), bf16[16,64,768]{2,1,0:T(8,128)(2,1)S(1)}, u32[]{:S(2)}, u32[]{:S(2)}) async-start(bf16[16,64,768]{2,1,0:T(8,128)(2,1)} %broadcast_in_dim.4), calls=%async_computation | async-start | bytes 3145728 | tf_op jit(solution)/shard_map/all_to_all | solution.py:99
  14.5 36.8 %all-to-all-done = bf16[16,64,768]{2,1,0:T(8,128)(2,1)S(1)} async-done(((bf16[16,64,768]{2,1,0:T(8,128)(2,1)}), bf16[16,64,768]{2,1,0:T(8,128)(2,1)S(1)}, u32[]{:S(2)}, u32[]{:S(2)}) %all-to-all-start) | async-done | bytes 1572896 | tf_op jit(solution)/shard_map/all_to_all | solution.py:99
  51.3 0.0 copy-done.4
  51.3 0.0 copy-done.5
  51.3 0.0 copy-done.6
  51.3 0.0 copy-start.1
  51.3 1.2 copy-done.1
  52.5 11.7 %shard_map.113 = (bf16[8,64,768]{2,1,0:T(8,128)(2,1)S(1)}, bf16[8,64,768]{2,1,0:T(8,128)(2,1)S(1)}) custom-call(s32[32]{0:T(128)S(1)} %bitcast.16, s32[32]{0:T(128)S(1)} %bitcast.18, s32[32]{0:T(128)S(1)} %bitcast.20, s32[1]{0:T(128)} %bitcast.10.count, s32[1]{0:T(128)} %bitcast.4.core, bf16[1024,768]{1,0:T(8,128)(2,1)S(1)} %bitcast.12, ...), custom_call_target="tpu_custom_call" | custom-call | tf_op jit(solution)/shard_map/pallas_call | solution.py:84
  64.2 0.1 collective-permute-start
  64.3 2.3 %collective-permute-done = bf16[8,64,768]{2,1,0:T(8,128)(2,1)S(1)} collective-permute-done((bf16[8,64,768]{2,1,0:T(8,128)(2,1)S(1)}, bf16[8,64,768]{2,1,0:T(8,128)(2,1)S(1)}, u32[]{:S(2)}, u32[]{:S(2)}) %collective-permute-start) | collective-permute-done | bytes 786464 | tf_op jit(solution)/shard_map/ppermute | solution.py:95
  66.6 0.0 copy-start.7
  66.6 1.1 add_convert_fusion
  67.6 0.0 copy-start.3
  67.6 6.6 %all-to-all-start.1 = ((bf16[8,64,768]{2,1,0:T(8,128)(2,1)}), bf16[8,64,768]{2,1,0:T(8,128)(2,1)S(1)}, u32[]{:S(2)}, u32[]{:S(2)}) async-start(bf16[8,64,768]{2,1,0:T(8,128)(2,1)} %add_convert_fusion), calls=%async_computation.1 | async-start | bytes 1572864 | tf_op jit(solution)/shard_map/all_to_all | solution.py:126
  74.2 0.0 copy-done
  74.2 0.0 copy-done.7
  74.2 0.3 fusion.self_ref
  74.6 12.8 %all-to-all-done.1.got_ref = bf16[8,64,768]{2,1,0:T(8,128)(2,1)S(1)} async-done(((bf16[8,64,768]{2,1,0:T(8,128)(2,1)}), bf16[8,64,768]{2,1,0:T(8,128)(2,1)S(1)}, u32[]{:S(2)}, u32[]{:S(2)}) %all-to-all-start.1) | async-done | bytes 786464 | tf_op jit(solution)/shard_map/all_to_all | solution.py:126
  87.4 0.0 copy-done.3
  87.4 0.8 shard_map.114
  88.2 0.0 copy-start.2
  88.2 0.1 broadcast_in_dim.5
  88.3 15.8 %all_to_all.20.mine_ref = bf16[8,64,768]{2,1,0:T(8,128)(2,1)S(1)} all-to-all(bf16[8,64,768]{2,1,0:T(8,128)(2,1)S(1)} %broadcast_in_dim.5), channel_id=1, replica_groups=mesh['y'=4,'zh'=4,'x'=4,'zl'=2,'core'=2] {'x','zl'}, dimensions={0} | all-to-all | bytes 1572864 | tf_op jit(solution)/shard_map/all_to_all | solution.py:99
  104.1 0.0 collective-permute-start.1
  104.1 2.3 %collective-permute-done.1.other_ref = bf16[8,64,768]{2,1,0:T(8,128)(2,1)S(1)} collective-permute-done((bf16[8,64,768]{2,1,0:T(8,128)(2,1)S(1)}, bf16[8,64,768]{2,1,0:T(8,128)(2,1)S(1)}, u32[]{:S(2)}, u32[]{:S(2)}) %collective-permute-start.1) | collective-permute-done | bytes 786464 | tf_op jit(solution)/shard_map/ppermute | solution.py:95
  106.4 0.0 copy-done.2
  106.4 8.8 %shard_map.115 = bf16[8,128,768]{2,1,0:T(8,128)(2,1)S(1)} custom-call(s32[32]{0:T(128)S(1)} %bitcast.17, s32[32]{0:T(128)S(1)} %bitcast.19, s32[1]{0:T(128)} %bitcast.11.count, s32[1]{0:T(128)} %bitcast.4.core, bf16[8,64,768]{2,1,0:T(8,128)(2,1)S(1)} %all_to_all.20.mine_ref, bf16[8,64,768]{2,1,0:T(8,128)(2,1)S(1)} %collective-permute-done.1.other_ref, ...), custom_call_target="tpu_custom_call" | custom-call | tf_op jit(solution)/shard_map/pallas_call | solution.py:84
  115.2 44.0 %all_to_all.21 = bf16[16,64,768]{2,1,0:T(8,128)(2,1)S(1)} all-to-all(bf16[16,64,768]{2,1,0:T(8,128)(2,1)S(1)} %bitcast.13), channel_id=1, replica_groups=mesh['y'=4,'zh'=4,'x'=4,'zl'=2,'core'=2] {'y','zh'}, dimensions={0} | all-to-all | bytes 3145728 | tf_op jit(solution)/shard_map/all_to_all | solution.py:138
  159.2 0.9 reduce_sum.12
Async XLA Ops:
  0.6 73.6 %copy-start = (bf16[768,768]{1,0:T(8,128)(2,1)S(1)}, bf16[768,768]{1,0:T(8,128)(2,1)}, u32[]{:S(2)}) copy-start(bf16[768,768]{1,0:T(8,128)(2,1)} %param.12) | copy-start | bytes 3538948
  3.0 48.3 %copy-start.4 = (s32[1,1,32]{2,1,0:T(1,128)S(1)}, s32[1,1,32]{2,1,0:T(1,128)}, u32[]{:S(2)}) copy-start(s32[1,1,32]{2,1,0:T(1,128)} %param.15) | copy-start | bytes 388
  3.0 48.3 %copy-start.5 = (s32[1,1,32]{2,1,0:T(1,128)S(1)}, s32[1,1,32]{2,1,0:T(1,128)}, u32[]{:S(2)}) copy-start(s32[1,1,32]{2,1,0:T(1,128)} %param.16) | copy-start | bytes 388
  3.0 48.3 %copy-start.6 = (s32[1,1,32]{2,1,0:T(1,128)S(1)}, s32[1,1,32]{2,1,0:T(1,128)}, u32[]{:S(2)}) copy-start(s32[1,1,32]{2,1,0:T(1,128)} %param.17) | copy-start | bytes 388
  3.0 48.3 %all-to-all-start = ((bf16[16,64,768]{2,1,0:T(8,128)(2,1)}), bf16[16,64,768]{2,1,0:T(8,128)(2,1)S(1)}, u32[]{:S(2)}, u32[]{:S(2)}) async-start(bf16[16,64,768]{2,1,0:T(8,128)(2,1)} %broadcast_in_dim.4), calls=%async_computation | async-start | bytes 3145728 | tf_op jit(solution)/shard_map/all_to_all | solution.py:99
  51.3 1.2 copy-start.1
  64.2 2.4 %collective-permute-start = (bf16[8,64,768]{2,1,0:T(8,128)(2,1)S(1)}, bf16[8,64,768]{2,1,0:T(8,128)(2,1)S(1)}, u32[]{:S(2)}, u32[]{:S(2)}) collective-permute-start(bf16[8,64,768]{2,1,0:T(8,128)(2,1)S(1)} %get-tuple-element.7), channel_id=1, source_target_pairs={{0,1},{1,0},{2,3},{3,2},{4,5},{5,4},{6,7},{7,6},{8,9},{9,8},{10,11... | collective-permute-start | bytes 2359304 | tf_op jit(solution)/shard_map/ppermute | solution.py:95
  66.6 7.7 %copy-start.7 = (bf16[64,768]{1,0:T(8,128)(2,1)S(1)}, bf16[64,768]{1,0:T(8,128)(2,1)}, u32[]{:S(2)}) copy-start(bf16[64,768]{1,0:T(8,128)(2,1)} %param.10) | copy-start | bytes 294916
  67.6 19.8 %copy-start.3 = (bf16[768,768]{1,0:T(8,128)(2,1)S(1)}, bf16[768,768]{1,0:T(8,128)(2,1)}, u32[]{:S(2)}) copy-start(bf16[768,768]{1,0:T(8,128)(2,1)} %w_ref.3) | copy-start | bytes 3538948
  67.6 19.8 %all-to-all-start.1 = ((bf16[8,64,768]{2,1,0:T(8,128)(2,1)}), bf16[8,64,768]{2,1,0:T(8,128)(2,1)S(1)}, u32[]{:S(2)}, u32[]{:S(2)}) async-start(bf16[8,64,768]{2,1,0:T(8,128)(2,1)} %add_convert_fusion), calls=%async_computation.1 | async-start | bytes 1572864 | tf_op jit(solution)/shard_map/all_to_all | solution.py:126
  88.2 18.2 %copy-start.2 = (bf16[1,1,32,128,128]{4,3,2,1,0:T(8,128)(2,1)S(1)}, bf16[1,1,32,128,128]{4,3,2,1,0:T(8,128)(2,1)}, u32[]{:S(2)}) copy-start(bf16[1,1,32,128,128]{4,3,2,1,0:T(8,128)(2,1)} %param.19) | copy-start | bytes 3145732
  104.1 2.3 %collective-permute-start.1 = (bf16[8,64,768]{2,1,0:T(8,128)(2,1)S(1)}, bf16[8,64,768]{2,1,0:T(8,128)(2,1)S(1)}, u32[]{:S(2)}, u32[]{:S(2)}) collective-permute-start(bf16[8,64,768]{2,1,0:T(8,128)(2,1)S(1)} %all_to_all.20.mine_ref), channel_id=1, source_target_pairs={{0,1},{1,0},{2,3},{3,2},{4,5},{5,4},{6,7},{7,6},{8,9},{9,8},{10,11... | collective-permute-start | bytes 2359304 | tf_op jit(solution)/shard_map/ppermute | solution.py:95

commit v2 on v1

v2 whole, which is shorter than its diff:
```python
import jax
import jax.numpy as jnp
from jax import lax
from jax.experimental import pallas as pl
from jax.experimental.pallas import tpu as pltpu
from jax.sharding import Mesh
from jax.sharding import PartitionSpec as P

PROW = ("y", "zh")
PCOL = ("x", "zl", "core")
F32 = jnp.float32
BF16 = jnp.bfloat16
VMEM_LIMIT = 48 * 2**20
RING = 4


def shift(value, axis, by):
    return lax.ppermute(value, axis, [(i, (i + by) % RING) for i in range(RING)])


def swap(value, axis):
    return lax.ppermute(value, axis, [(0, 1), (1, 0)])


def behind(at, by):
    return lax.rem(at + (RING - by), RING)


def build_tiles(rows, cols, types, count, place, vals_ref, one_ref, two_ref):
    y, zh, x, zl, core = (place[i] for i in range(5))
    side = vals_ref.shape[1]
    half = side // 2
    span = RING * half
    one_ref[...] = jnp.zeros_like(one_ref)
    two_ref[...] = jnp.zeros_like(two_ref)

    def slot(k, carry):
        row, col = rows[k], cols[k]
        block = vals_ref[k]
        turned = block.T
        lanes = pl.ds(pl.multiple_of(types[k] * two_ref.shape[0] + col * side, side), side)
        d = lax.rem(lax.div(row, 2) + RING - x, RING)
        e = jnp.where(lax.rem(row, 2) == zl, 0, 1)
        for c in range(2):
            at = d * span + jnp.where(core == c, 0, side) + e * half
            one_ref[pl.ds(pl.multiple_of(at, half), half), lanes] = block[c * half : (c + 1) * half]
        lanes = pl.ds(pl.multiple_of(row * side, side), side)
        d = lax.rem(lax.div(col, 2) + RING - y, RING)
        for c in range(2):
            e = lax.rem(lax.rem(col, 2) * 2 + c + RING - zh, RING)
            at = d * span + e * half
            two_ref[pl.ds(pl.multiple_of(at, half), half), lanes] = turned[c * half : (c + 1) * half]
        return carry

    lax.fori_loop(0, count[0], slot, 0)


def copy_all(pairs, sem):
    copies = [pltpu.make_async_copy(src, dst, sem.at[i]) for i, (src, dst) in enumerate(pairs)]
    for c in copies:
        c.start()
    return copies


def near_messages(*refs):
    chunks, w_ref, out_ref, table, sem = refs[:7], *refs[7:]
    own = chunks[0].shape[0]
    for c in copy_all([(chunk, table.at[pl.ds(i * own, own), :]) for i, chunk in enumerate(chunks)], sem):
        c.wait()
    for r in range(w_ref.shape[0]):
        made = jnp.dot(table[...], w_ref[r], preferred_element_type=F32).astype(BF16)
        out_ref[r] = made.reshape(out_ref.shape[1:])


def hop_one(place, *refs):
    near_ref, far, (w_ref, tile_ref, keep_ref, send_ref, table, wide_w, msgs, sem) = refs[0], refs[1:4], refs[4:]
    y, zh = place[0], place[1]
    own, width = near_ref.shape[2:]
    relations = wide_w.shape[0]
    span = RING * own
    total = msgs.shape[0] // relations
    count = RING - 1

    def chunk(r, from_y, from_z):
        return pl.ds(pl.multiple_of(r * total + (from_y * RING + from_z) * own, own), own)

    first = copy_all([(w_ref, wide_w), *((f, table.at[pl.ds(i * count, count)]) for i, f in enumerate(far))], sem)
    late = []
    for r in range(relations):
        for i in range(7):
            at = (y, behind(zh, i)) if i < RING else (behind(y, i - count), zh)
            late.append(pltpu.make_async_copy(near_ref.at[r, i], msgs.at[chunk(r, *at), :], sem.at[RING + r * 7 + i]))
    for c in late:
        c.start()
    for c in first:
        c.wait()
    for r in range(relations):
        made = jnp.dot(
            table[...].reshape(count * count * own, width), wide_w[r], preferred_element_type=F32
        ).astype(BF16)
        for d in range(1, RING):
            for e in range(1, RING):
                at = ((d - 1) * count + e - 1) * own
                msgs[chunk(r, behind(y, d), behind(zh, e)), :] = made[at : at + own]
    for c in late:
        c.wait()

    @pl.loop(0, RING)
    def _(d):
        lhs = tile_ref[pl.ds(pl.multiple_of(d * span, span), span), :]
        made = jnp.dot(lhs, msgs[...], preferred_element_type=F32).reshape(2, 2, own, width)
        keep_ref[d] = made[0]
        send_ref[d] = made[1].astype(BF16)


def hop_two(place, *refs):
    mine, other, (tile_ref, same_ref, *parts) = refs[:4], refs[4:8], refs[8:]
    wide, narrow, table, sem = parts[:3], parts[3:6], parts[6], parts[7]
    x, zl, core = (place[i] for i in range(2, 5))
    own, width = same_ref.shape[1:]
    span = RING * own
    pairs = []
    for d in range(RING):
        for e in range(2):
            block = (behind(x, d) * 2 + (zl if e == 0 else 1 - zl)) * 2
            for source, c in ((mine, core), (other, 1 - core)):
                at = pl.ds(pl.multiple_of((block + c) * own, own), own)
                pairs.append((source[d].at[e], table.at[at, :]))
    for c in copy_all(pairs, sem):
        c.wait()
    for d in range(RING):
        made = jnp.dot(tile_ref[pl.ds(d * span, span), :], table[...], preferred_element_type=F32)
        made = made.reshape(RING, own, width)
        if d == 0:
            same_ref[...] = made
        else:
            narrow[d - 1][...] = made[0].astype(BF16)
            wide[d - 1][...] = made[1:].astype(BF16)


def hidden_step(base_ref, got_ref, self_ref, w_ref, hidden_ref, out_ref):
    total = self_ref[...] + base_ref[...] + got_ref[...].astype(F32)
    hidden = jnp.maximum(total, 0.0).astype(BF16)
    hidden_ref[...] = hidden
    out_ref[...] = jnp.dot(hidden, w_ref[...], preferred_element_type=F32).astype(BF16)


def call(kernel, flops, scalars, loose, arrays, out_shape, scratch):
    def spec(kind):
        return pl.BlockSpec(memory_space=kind)

    return pl.pallas_call(
        kernel,
        out_shape=out_shape,
        in_specs=[spec(pltpu.SMEM)] * len(scalars) + [spec(pl.ANY)] * len(loose) + [spec(pltpu.VMEM)] * len(arrays),
        out_specs=jax.tree.map(lambda _: spec(pltpu.VMEM), out_shape),
        scratch_shapes=scratch,
        compiler_params=pltpu.CompilerParams(vmem_limit_bytes=VMEM_LIMIT),
        cost_estimate=pl.CostEstimate(flops=flops, bytes_accessed=4 * 2**20, transcendentals=0),
    )(*scalars, *loose, *arrays)


def total_of(parts):
    return sum(p.astype(F32) for p in parts)


def per_device(paper_x, author_x, w_self, w_rel, w_two, block_rows, block_cols, block_type, block_count, block_vals):
    slots = block_rows.shape[2]
    side = block_vals.shape[3]
    own, width = paper_x.shape
    rows, cols, types = (a.reshape(slots) for a in (block_rows, block_cols, block_type))
    count = block_count.reshape(1)
    vals = block_vals.reshape(slots, side, side)
    place = jnp.stack([lax.axis_index(a).astype(jnp.int32) for a in (*PROW, *PCOL)])
    tile_rows = 16 * own

    def shaped(*dims, dtype=BF16):
        return jax.ShapeDtypeStruct((*dims, own, width), dtype)

    relations = w_rel.shape[0]
    sems = pltpu.SemaphoreType.DMA
    tile_one, tile_two = call(
        build_tiles,
        10**9,
        (rows, cols, types, count, place),
        (),
        (vals,),
        (
            jax.ShapeDtypeStruct((tile_rows, relations * tile_rows), BF16),
            jax.ShapeDtypeStruct((tile_rows, tile_rows), BF16),
        ),
        [],
    )
    with jax.named_scope("gather_authors"):
        by_z = [shift(author_x, "zh", e) for e in range(1, RING)]
        by_y = [shift(author_x, "y", d) for d in range(1, RING)]
        by_z, by_y = lax.optimization_barrier((by_z, by_y))
        relay = jnp.stack(by_z)
        far = [shift(relay, "y", d) for d in range(1, RING)]
    near = call(
        near_messages,
        2 * relations * 7 * own * width * width,
        (),
        (author_x, *by_z, *by_y),
        (w_rel,),
        shaped(relations, 7),
        [pltpu.VMEM((7 * own, width), BF16), sems((7,))],
    )
    self_term = jnp.dot(paper_x, w_self, preferred_element_type=F32)
    keep, send = call(
        hop_one,
        2 * relations * tile_rows * tile_rows * width,
        (place,),
        (near, *far, w_rel),
        (tile_one,),
        (shaped(RING, 2, dtype=F32), shaped(RING, 2)),
        [
            pltpu.VMEM((9, own, width), BF16),
            pltpu.VMEM(w_rel.shape, BF16),
            pltpu.VMEM((relations * tile_rows, width), BF16),
            sems((RING + relations * 7,)),
        ],
    )
    with jax.named_scope("sum_papers"):
        pair = keep + swap(send, "core").astype(F32)
        by_x = [shift(pair[d].astype(BF16), "x", d) for d in range(1, RING)]
        both = total_of([pair[0], *by_x])
        last = swap(both[1].astype(BF16), "zl")
    paper_hidden, outgoing = call(
        hidden_step, 2 * own * width * width, (), (), (both[0], last, self_term, w_two), (shaped(), shaped()), []
    )
    with jax.named_scope("gather_papers"):
        near = jnp.stack([outgoing, swap(outgoing, "zl")])
        mine = [near, *(shift(near, "x", d) for d in range(1, RING))]
        other = [swap(m, "core") for m in mine]
    same, *parts = call(
        hop_two,
        2 * tile_rows * tile_rows * width,
        (place,),
        (*mine, *other),
        (tile_two,),
        (shaped(RING, dtype=F32), *[shaped(RING - 1)] * 3, *[shaped()] * 3),
        [pltpu.VMEM((tile_rows, width), BF16), sems((16,))],
    )
    with jax.named_scope("sum_authors"):
        wide = [shift(parts[d - 1], "y", d) for d in range(1, RING)]
        narrow = [shift(parts[2 + d], "y", d) for d in range(1, RING)]
        relayed = total_of([same[1:], *wide]).astype(BF16)
        by_z = [shift(relayed[e - 1], "zh", e) for e in range(1, RING)]
        author_out = total_of([same[0], *narrow, *by_z]).astype(BF16)
    return paper_hidden, author_out


def solution(mesh):
    split = Mesh(mesh.devices.reshape(4, 4, 4, 2, 2), (*PROW, *PCOL))
    tile = P(PROW, PCOL)
    return jax.shard_map(
        per_device,
        mesh=split,
        in_specs=(P((*PROW, *PCOL)), P((*PCOL, *PROW)), P(), P(), P(), tile, tile, tile, tile, tile),
        out_specs=(P((*PROW, *PCOL)), P((*PCOL, *PROW))),
        check_vma=False,
    )
```

time: 162 us -> 125 us (0.77)
  blocking collectives: 59.8 us -> 0 us
  starting transfers between devices: 17.6 us -> 46.7 us
  waiting for transfers between devices: 54.2 us -> 48.5 us
    all_to_all x2 -> x0, blocking collectives: 59.8 us -> none  [the longest x1 44 us: per_device(): lax.all_to_all(author_part.reshape(prows, own, width), PROW, 0, 0, tiled=...]
    all_to_all x2 -> x0, waiting for transfers between devices: 49.6 us -> none  [the longest x1 36.8 us: to_all(): lax.all_to_all(jnp.broadcast_to(value[None], (size, *value.shape)), axes,...]
    ppermute x2 -> x31, starting transfers between devices: 0.1 us -> 46.7 us  [the longest x24 45 us: shift(): lax.ppermute(value, axis, [(i, (i + by) % RING) for i in range(RING)])]
    ppermute x2 -> x31, waiting for transfers between devices: 4.55 us -> 48.5 us  [the longest x24 36.8 us: shift(): lax.ppermute(value, axis, [(i, (i + by) % RING) for i in range(RING)])]
    all_to_all x2 -> x0, starting transfers between devices: 17.5 us -> none  [the longest x1 10.9 us: to_all(): lax.all_to_all(jnp.broadcast_to(value[None], (size, *value.shape)), axes,...]
    broadcast_in_dim x2 -> x0, local copies, waits for them, and re-layouts: 2.36 us -> none  [to_all(): jnp.broadcast_to(value[None], (size, *value.shape))]
    unnamed x16 -> x18, local copies, waits for them, and re-layouts: 1.25 us -> 3.21 us
    pallas_call x3 -> x5, Pallas kernels: 21.3 us -> 21.5 us  [call(): pl.pallas_call(kernel, out_shape=out_shape, in_specs=[spec(pltpu.SMEM)] *...]
  transfers between devices with their start and end apart: 4 -> 31, of which waited for: 4 -> 19; matrix products, arithmetic and copies ran while one was open for 0% -> 0% of each run, Pallas kernels for 0% -> 5%
where the time goes in v2:
time: 125 us; the launch traced here: 123 us
  waiting for transfers between devices  48.5 us (39%)
  starting transfers between devices  46.7 us (37%)
  Pallas kernels  21.5 us (17%)
  local copies, waits for them, and re-layouts  3.39 us (3%)
  between operations  1.42 us (1%)
  other arithmetic  1.26 us (1%)
    ppermute x24, starting transfers between devices, shift(): lax.ppermute(value, axis, [(i, (i + by) % RING) for i in range(RING)])  45 us
    ppermute x24, waiting for transfers between devices, shift(): lax.ppermute(value, axis, [(i, (i + by) % RING) for i in range(RING)])  36.8 us
    pallas_call x5, Pallas kernels, call(): pl.pallas_call(kernel, out_shape=out_shape, in_specs=[spec(pltpu.SMEM)] *...  21.5 us
    ppermute x7, waiting for transfers between devices, swap(): return lax.ppermute(value, axis, [(0, 1), (1, 0)])  11.7 us
    unnamed x18, local copies, waits for them, and re-layouts  3.21 us
  transfers between devices with their start and end apart: 31, of which 19 were waited for; matrix products, arithmetic and copies ran while one was open for 0% of the time, Pallas kernels for 5%

profile of v2, /device:TPU:64, one launch (start us, length us, event | category | flops | bytes accessed | tf_op | source)
XLA Modules:
  0.0 123.0 jit_solution(16957607687092810652)
XLA Ops:
  0.6 0.0 copy-start
  0.6 4.6 %collective-permute-start = (bf16[64,768]{1,0:T(8,128)(2,1)}, bf16[64,768]{1,0:T(8,128)(2,1)S(1)}, u32[]{:S(2)}, u32[]{:S(2)}) collective-permute-start(bf16[64,768]{1,0:T(8,128)(2,1)} %refs_0_.1), channel_id=1, source_target_pairs={{0,16},{16,32},{32,48},{48,0},{1,17},{17,33},{33,49},{49,1},{2,18}... | collective-permute-start | bytes 294920 | tf_op jit(solution)/shard_map/gather_authors/ppermute | solution.py:18
  5.2 1.0 collective-permute-start.1
  6.2 2.8 %collective-permute-start.2 = (bf16[64,768]{1,0:T(8,128)(2,1)}, bf16[64,768]{1,0:T(8,128)(2,1)S(1)}, u32[]{:S(2)}, u32[]{:S(2)}) collective-permute-start(bf16[64,768]{1,0:T(8,128)(2,1)} %refs_0_.1), channel_id=1, source_target_pairs={{0,48},{16,0},{32,16},{48,32},{1,49},{17,1},{33,17},{49,33},{2,50}... | collective-permute-start | bytes 294920 | tf_op jit(solution)/shard_map/gather_authors/ppermute | solution.py:18
  9.0 1.6 %collective-permute-start.3 = (bf16[64,768]{1,0:T(8,128)(2,1)}, bf16[64,768]{1,0:T(8,128)(2,1)S(1)}, u32[]{:S(2)}, u32[]{:S(2)}) collective-permute-start(bf16[64,768]{1,0:T(8,128)(2,1)} %refs_0_.1), channel_id=1, source_target_pairs={{0,64},{64,128},{128,192},{192,0},{1,65},{65,129},{129,193},{193,1... | collective-permute-start | bytes 294920 | tf_op jit(solution)/shard_map/gather_authors/ppermute | solution.py:18
  10.6 2.9 %collective-permute-start.4 = (bf16[64,768]{1,0:T(8,128)(2,1)}, bf16[64,768]{1,0:T(8,128)(2,1)S(1)}, u32[]{:S(2)}, u32[]{:S(2)}) collective-permute-start(bf16[64,768]{1,0:T(8,128)(2,1)} %refs_0_.1), channel_id=1, source_target_pairs={{0,128},{64,192},{128,0},{192,64},{1,129},{65,193},{129,1},{193,65... | collective-permute-start | bytes 294920 | tf_op jit(solution)/shard_map/gather_authors/ppermute | solution.py:18
  13.5 0.0 collective-permute-done.refs_1_
  13.5 1.3 %collective-permute-start.5 = (bf16[64,768]{1,0:T(8,128)(2,1)}, bf16[64,768]{1,0:T(8,128)(2,1)S(1)}, u32[]{:S(2)}, u32[]{:S(2)}) collective-permute-start(bf16[64,768]{1,0:T(8,128)(2,1)} %refs_0_.1), channel_id=1, source_target_pairs={{0,192},{64,0},{128,64},{192,128},{1,193},{65,1},{129,65},{193,129... | collective-permute-start | bytes 294920 | tf_op jit(solution)/shard_map/gather_authors/ppermute | solution.py:18
  14.9 1.5 %collective-permute-done.1.refs_2_ = bf16[64,768]{1,0:T(8,128)(2,1)S(1)} collective-permute-done((bf16[64,768]{1,0:T(8,128)(2,1)}, bf16[64,768]{1,0:T(8,128)(2,1)S(1)}, u32[]{:S(2)}, u32[]{:S(2)}) %collective-permute-start.1) | collective-permute-done | bytes 98336 | tf_op jit(solution)/shard_map/gather_authors/ppermute | solution.py:18
  16.3 1.0 collective-permute-done.2.refs_3_
  17.4 0.2 collective-permute-done.4.refs_5_
  17.6 0.8 collective-permute-done.5.refs_6_
  18.4 0.7 collective-permute-start.6
  19.1 3.4 %collective-permute-start.7 = (bf16[3,64,768]{2,1,0:T(8,128)(2,1)S(1)}, bf16[3,64,768]{2,1,0:T(8,128)(2,1)S(1)}, u32[]{:S(2)}, u32[]{:S(2)}) collective-permute-start(bf16[3,64,768]{2,1,0:T(8,128)(2,1)S(1)} %pad_maximum_fusion), channel_id=1, source_target_pairs={{0,128},{64,192},{128,0},{192,64},{1,129},{65,193},{129,1},{193,65... | collective-permute-start | bytes 884744 | tf_op jit(solution)/shard_map/gather_authors/ppermute | solution.py:18
  22.5 0.8 collective-permute-start.8
  24.0 0.1 stack.44.place
  24.0 1.2 copy-done.4
  25.3 0.7 copy-done.5
  25.9 0.7 copy-done.6
  26.6 0.7 copy-done.7
  27.2 3.8 %shard_map.114 = (bf16[1024,2048]{1,0:T(8,128)(2,1)}, bf16[1024,1024]{1,0:T(8,128)(2,1)S(1)}) custom-call(s32[32]{0:T(128)S(1)} %bitcast.61, s32[32]{0:T(128)S(1)} %bitcast.62, s32[32]{0:T(128)S(1)} %bitcast.63, s32[1]{0:T(128)} %bitcast.55.count, s32[5]{0:T(128)S(1)} %stack.44.place, bf16[32,128,128]{2,1,0:T(8,128)(2,1)S(1)} %bitcast.60), custom_call_target="tpu_custom_call" | custom-call | flops 1000000000 | bytes 4194304 | tf_op jit(solution)/shard_map/pallas_call | solution.py:152
  31.0 2.2 %shard_map.113.refs_0_ = bf16[2,7,64,768]{3,2,1,0:T(8,128)(2,1)S(1)} custom-call(bf16[64,768]{1,0:T(8,128)(2,1)S(1)} %copy-done.3, bf16[64,768]{1,0:T(8,128)(2,1)S(1)} %collective-permute-done.refs_1_, bf16[64,768]{1,0:T(8,128)(2,1)S(1)} %collective-permute-done.1.refs_2_, bf16[64,768]{1,0:T(8,128)(2,1)S(1)} %collective-permute-done.2.refs_3_, ...), custom_call_target="tpu_custom_call" | custom-call | flops 1056964608 | bytes 4194304 | tf_op jit(solution)/shard_map/pallas_call | solution.py:152
  33.2 0.0 collective-permute-done.6.refs_1_
  33.3 1.4 %collective-permute-done.7.refs_2_ = bf16[3,64,768]{2,1,0:T(8,128)(2,1)S(1)} collective-permute-done((bf16[3,64,768]{2,1,0:T(8,128)(2,1)S(1)}, bf16[3,64,768]{2,1,0:T(8,128)(2,1)S(1)}, u32[]{:S(2)}, u32[]{:S(2)}) %collective-permute-start.7) | collective-permute-done | bytes 294944 | tf_op jit(solution)/shard_map/gather_authors/ppermute | solution.py:18
  34.6 9.9 %shard_map.115 = (f32[4,2,64,768]{3,2,1,0:T(8,128)S(1)}, bf16[4,2,64,768]{3,2,1,0:T(8,128)(2,1)S(1)}) custom-call(s32[5]{0:T(128)S(1)} %stack.44.place, bf16[2,7,64,768]{3,2,1,0:T(8,128)(2,1)S(1)} %shard_map.113.refs_0_, bf16[3,64,768]{2,1,0:T(8,128)(2,1)S(1)} %collective-permute-done.6.refs_1_, bf16[3,64,768]{2,1,0:T(8,128)(2,1)S(1)} %collective-permute-done.7.refs_2_, ...), custom_call_target="tpu_custom_call" | custom-call | flops 3221225472 | bytes 4194304 | tf_op jit(solution)/shard_map/pallas_call | solution.py:152
  44.5 0.1 collective-permute-start.9
  44.6 2.3 %collective-permute-done.9 = bf16[4,2,64,768]{3,2,1,0:T(8,128)(2,1)S(1)} collective-permute-done((bf16[4,2,64,768]{3,2,1,0:T(8,128)(2,1)S(1)}, bf16[4,2,64,768]{3,2,1,0:T(8,128)(2,1)S(1)}, u32[]{:S(2)}, u32[]{:S(2)}) %collective-permute-start.9) | collective-permute-done | bytes 786464 | tf_op jit(solution)/shard_map/sum_papers/ppermute | solution.py:22
  46.9 0.3 fusion.10
  47.2 1.6 %collective-permute-start.10 = (bf16[2,64,768]{2,1,0:T(8,128)(2,1)S(1)}, bf16[2,64,768]{2,1,0:T(8,128)(2,1)S(1)}, u32[]{:S(2)}, u32[]{:S(2)}) collective-permute-start(bf16[2,64,768]{2,1,0:T(8,128)(2,1)S(1)} %get-tuple-element.42), channel_id=1, source_target_pairs={{0,4},{4,8},{8,12},{12,0},{1,5},{5,9},{9,13},{13,1},{2,6},{6,10},{... | collective-permute-start | bytes 589832 | tf_op jit(solution)/shard_map/sum_papers/ppermute | solution.py:18
  48.8 2.7 %collective-permute-start.11 = (bf16[2,64,768]{2,1,0:T(8,128)(2,1)S(1)}, bf16[2,64,768]{2,1,0:T(8,128)(2,1)S(1)}, u32[]{:S(2)}, u32[]{:S(2)}) collective-permute-start(bf16[2,64,768]{2,1,0:T(8,128)(2,1)S(1)} %get-tuple-element.44), channel_id=1, source_target_pairs={{0,8},{4,12},{8,0},{12,4},{1,9},{5,13},{9,1},{13,5},{2,10},{6,14},... | collective-permute-start | bytes 589832 | tf_op jit(solution)/shard_map/sum_papers/ppermute | solution.py:18
  51.5 1.4 %collective-permute-start.12 = (bf16[2,64,768]{2,1,0:T(8,128)(2,1)S(1)}, bf16[2,64,768]{2,1,0:T(8,128)(2,1)S(1)}, u32[]{:S(2)}, u32[]{:S(2)}) collective-permute-start(bf16[2,64,768]{2,1,0:T(8,128)(2,1)S(1)} %get-tuple-element.43), channel_id=1, source_target_pairs={{0,12},{4,0},{8,4},{12,8},{1,13},{5,1},{9,5},{13,9},{2,14},{6,2},{... | collective-permute-start | bytes 589832 | tf_op jit(solution)/shard_map/sum_papers/ppermute | solution.py:18
  52.9 0.3 fusion.11.self_ref
  53.3 2.2 %collective-permute-done.10 = bf16[2,64,768]{2,1,0:T(8,128)(2,1)S(1)} collective-permute-done((bf16[2,64,768]{2,1,0:T(8,128)(2,1)S(1)}, bf16[2,64,768]{2,1,0:T(8,128)(2,1)S(1)}, u32[]{:S(2)}, u32[]{:S(2)}) %collective-permute-start.10) | collective-permute-done | bytes 196640 | tf_op jit(solution)/shard_map/sum_papers/ppermute | solution.py:18
  55.4 5.2 %collective-permute-done.11 = bf16[2,64,768]{2,1,0:T(8,128)(2,1)S(1)} collective-permute-done((bf16[2,64,768]{2,1,0:T(8,128)(2,1)S(1)}, bf16[2,64,768]{2,1,0:T(8,128)(2,1)S(1)}, u32[]{:S(2)}, u32[]{:S(2)}) %collective-permute-start.11) | collective-permute-done | bytes 196640 | tf_op jit(solution)/shard_map/sum_papers/ppermute | solution.py:18
  60.6 0.1 fusion.2
  60.7 0.6 collective-permute-start.13
  61.3 4.1 %collective-permute-done.13.got_ref = bf16[64,768]{1,0:T(8,128)(2,1)S(1)} collective-permute-done((bf16[64,768]{1,0:T(8,128)(2,1)S(1)}, bf16[64,768]{1,0:T(8,128)(2,1)S(1)}, u32[]{:S(2)}, u32[]{:S(2)}) %collective-permute-start.13) | collective-permute-done | bytes 98336 | tf_op jit(solution)/shard_map/sum_papers/ppermute | solution.py:22
  65.4 0.8 shard_map.116
  66.2 0.5 collective-permute-start.14
  66.7 4.1 %collective-permute-done.14 = bf16[64,768]{1,0:T(8,128)(2,1)S(1)} collective-permute-done((bf16[64,768]{1,0:T(8,128)(2,1)S(1)}, bf16[64,768]{1,0:T(8,128)(2,1)S(1)}, u32[]{:S(2)}, u32[]{:S(2)}) %collective-permute-start.14) | collective-permute-done | bytes 98336 | tf_op jit(solution)/shard_map/gather_papers/ppermute | solution.py:22
  70.9 1.4 %collective-permute-start.15 = (bf16[2,64,768]{2,1,0:T(8,128)(2,1)S(1)}, bf16[2,64,768]{2,1,0:T(8,128)(2,1)S(1)}, u32[]{:S(2)}, u32[]{:S(2)}) collective-permute-start(bf16[2,64,768]{2,1,0:T(8,128)(2,1)S(1)} %pad_maximum_fusion.1.refs_0_), channel_id=1, source_target_pairs={{0,4},{4,8},{8,12},{12,0},{1,5},{5,9},{9,13},{13,1},{2,6},{6,10},{... | collective-permute-start | bytes 589832 | tf_op jit(solution)/shard_map/gather_papers/ppermute | solution.py:18
  72.3 2.5 %collective-permute-start.16 = (bf16[2,64,768]{2,1,0:T(8,128)(2,1)S(1)}, bf16[2,64,768]{2,1,0:T(8,128)(2,1)S(1)}, u32[]{:S(2)}, u32[]{:S(2)}) collective-permute-start(bf16[2,64,768]{2,1,0:T(8,128)(2,1)S(1)} %pad_maximum_fusion.1.refs_0_), channel_id=1, source_target_pairs={{0,8},{4,12},{8,0},{12,4},{1,9},{5,13},{9,1},{13,5},{2,10},{6,14},... | collective-permute-start | bytes 589832 | tf_op jit(solution)/shard_map/gather_papers/ppermute | solution.py:18
  74.8 1.5 %collective-permute-start.17 = (bf16[2,64,768]{2,1,0:T(8,128)(2,1)S(1)}, bf16[2,64,768]{2,1,0:T(8,128)(2,1)S(1)}, u32[]{:S(2)}, u32[]{:S(2)}) collective-permute-start(bf16[2,64,768]{2,1,0:T(8,128)(2,1)S(1)} %pad_maximum_fusion.1.refs_0_), channel_id=1, source_target_pairs={{0,12},{4,0},{8,4},{12,8},{1,13},{5,1},{9,5},{13,9},{2,14},{6,2},{... | collective-permute-start | bytes 589832 | tf_op jit(solution)/shard_map/gather_papers/ppermute | solution.py:18
  76.2 3.4 %collective-permute-done.15.refs_1_ = bf16[2,64,768]{2,1,0:T(8,128)(2,1)S(1)} collective-permute-done((bf16[2,64,768]{2,1,0:T(8,128)(2,1)S(1)}, bf16[2,64,768]{2,1,0:T(8,128)(2,1)S(1)}, u32[]{:S(2)}, u32[]{:S(2)}) %collective-permute-start.15) | collective-permute-done | bytes 196640 | tf_op jit(solution)/shard_map/gather_papers/ppermute | solution.py:18
  79.7 2.1 %collective-permute-done.16.refs_2_ = bf16[2,64,768]{2,1,0:T(8,128)(2,1)S(1)} collective-permute-done((bf16[2,64,768]{2,1,0:T(8,128)(2,1)S(1)}, bf16[2,64,768]{2,1,0:T(8,128)(2,1)S(1)}, u32[]{:S(2)}, u32[]{:S(2)}) %collective-permute-start.16) | collective-permute-done | bytes 196640 | tf_op jit(solution)/shard_map/gather_papers/ppermute | solution.py:18
  81.8 0.5 collective-permute-start.21
  82.3 0.9 collective-permute-done.20.refs_6_
  83.2 0.3 collective-permute-done.21.refs_7_
  83.5 4.8 %shard_map.117 = (f32[4,64,768]{2,1,0:T(8,128)S(1)}, bf16[3,64,768]{2,1,0:T(8,128)(2,1)S(1)}, bf16[3,64,768]{2,1,0:T(8,128)(2,1)S(1)}, bf16[3,64,768]{2,1,0:T(8,...) custom-call(s32[5]{0:T(128)S(1)} %stack.44.place, ...), custom_call_target="tpu_custom_call" | custom-call | flops 1610612736 | bytes 4194304 | tf_op jit(solution)/shard_map/pallas_call | solution.py:152
  88.3 1.3 %collective-permute-start.25 = (bf16[3,64,768]{2,1,0:T(8,128)(2,1)S(1)}, bf16[3,64,768]{2,1,0:T(8,128)(2,1)S(1)}, u32[]{:S(2)}, u32[]{:S(2)}) collective-permute-start(bf16[3,64,768]{2,1,0:T(8,128)(2,1)S(1)} %get-tuple-element.37), channel_id=1, source_target_pairs={{0,64},{64,128},{128,192},{192,0},{1,65},{65,129},{129,193},{193,1... | collective-permute-start | bytes 884744 | tf_op jit(solution)/shard_map/sum_authors/ppermute | solution.py:18
  89.7 2.4 %collective-permute-start.26 = (bf16[3,64,768]{2,1,0:T(8,128)(2,1)S(1)}, bf16[3,64,768]{2,1,0:T(8,128)(2,1)S(1)}, u32[]{:S(2)}, u32[]{:S(2)}) collective-permute-start(bf16[3,64,768]{2,1,0:T(8,128)(2,1)S(1)} %get-tuple-element.38), channel_id=1, source_target_pairs={{0,128},{64,192},{128,0},{192,64},{1,129},{65,193},{129,1},{193,65... | collective-permute-start | bytes 884744 | tf_op jit(solution)/shard_map/sum_authors/ppermute | solution.py:18
  92.0 1.6 %collective-permute-start.27 = (bf16[3,64,768]{2,1,0:T(8,128)(2,1)S(1)}, bf16[3,64,768]{2,1,0:T(8,128)(2,1)S(1)}, u32[]{:S(2)}, u32[]{:S(2)}) collective-permute-start(bf16[3,64,768]{2,1,0:T(8,128)(2,1)S(1)} %get-tuple-element.39), channel_id=1, source_target_pairs={{0,192},{64,0},{128,64},{192,128},{1,193},{65,1},{129,65},{193,129... | collective-permute-start | bytes 884744 | tf_op jit(solution)/shard_map/sum_authors/ppermute | solution.py:18
  93.6 0.5 collective-permute-start.22
  94.1 1.1 collective-permute-start.23
  95.2 10.1 %collective-permute-done.25 = bf16[3,64,768]{2,1,0:T(8,128)(2,1)S(1)} collective-permute-done((bf16[3,64,768]{2,1,0:T(8,128)(2,1)S(1)}, bf16[3,64,768]{2,1,0:T(8,128)(2,1)S(1)}, u32[]{:S(2)}, u32[]{:S(2)}) %collective-permute-start.25) | collective-permute-done | bytes 294944 | tf_op jit(solution)/shard_map/sum_authors/ppermute | solution.py:18
  105.3 0.9 collective-permute-done.26
  106.2 0.5 collective-permute-done.27
  106.7 0.1 add_convert_fusion
  106.9 4.0 %collective-permute-start.28 = (bf16[64,768]{1,0:T(8,128)(2,1)S(1)}, bf16[64,768]{1,0:T(8,128)(2,1)S(1)}, u32[]{:S(2)}, u32[]{:S(2)}) collective-permute-start(bf16[64,768]{1,0:T(8,128)(2,1)S(1)} %get-tuple-element.45), channel_id=1, source_target_pairs={{0,16},{16,32},{32,48},{48,0},{1,17},{17,33},{33,49},{49,1},{2,18}... | collective-permute-start | bytes 294920 | tf_op jit(solution)/shard_map/sum_authors/ppermute | solution.py:18
  110.9 1.8 %collective-permute-start.29 = (bf16[64,768]{1,0:T(8,128)(2,1)S(1)}, bf16[64,768]{1,0:T(8,128)(2,1)S(1)}, u32[]{:S(2)}, u32[]{:S(2)}) collective-permute-start(bf16[64,768]{1,0:T(8,128)(2,1)S(1)} %get-tuple-element.47), channel_id=1, source_target_pairs={{0,32},{16,48},{32,0},{48,16},{1,33},{17,49},{33,1},{49,17},{2,34}... | collective-permute-start | bytes 294920 | tf_op jit(solution)/shard_map/sum_authors/ppermute | solution.py:18
  112.7 2.1 %collective-permute-start.30 = (bf16[64,768]{1,0:T(8,128)(2,1)S(1)}, bf16[64,768]{1,0:T(8,128)(2,1)S(1)}, u32[]{:S(2)}, u32[]{:S(2)}) collective-permute-start(bf16[64,768]{1,0:T(8,128)(2,1)S(1)} %get-tuple-element.46), channel_id=1, source_target_pairs={{0,48},{16,0},{32,16},{48,32},{1,49},{17,1},{33,17},{49,33},{2,50}... | collective-permute-start | bytes 294920 | tf_op jit(solution)/shard_map/sum_authors/ppermute | solution.py:18
  114.8 6.0 %collective-permute-done.29 = bf16[64,768]{1,0:T(8,128)(2,1)S(1)} collective-permute-done((bf16[64,768]{1,0:T(8,128)(2,1)S(1)}, bf16[64,768]{1,0:T(8,128)(2,1)S(1)}, u32[]{:S(2)}, u32[]{:S(2)}) %collective-permute-start.29) | collective-permute-done | bytes 98336 | tf_op jit(solution)/shard_map/sum_authors/ppermute | solution.py:18
  120.8 1.5 %collective-permute-done.30 = bf16[64,768]{1,0:T(8,128)(2,1)S(1)} collective-permute-done((bf16[64,768]{1,0:T(8,128)(2,1)S(1)}, bf16[64,768]{1,0:T(8,128)(2,1)S(1)}, u32[]{:S(2)}, u32[]{:S(2)}) %collective-permute-start.30) | collective-permute-done | bytes 98336 | tf_op jit(solution)/shard_map/sum_authors/ppermute | solution.py:18
  122.3 0.7 fusion.8
  (33 shorter events, 0.2 us)
Async XLA Ops:
  0.6 52.3 %copy-start = (bf16[768,768]{1,0:T(8,128)(2,1)S(1)}, bf16[768,768]{1,0:T(8,128)(2,1)}, u32[]{:S(2)}) copy-start(bf16[768,768]{1,0:T(8,128)(2,1)} %param.12) | copy-start | bytes 3538948
  0.6 12.9 %collective-permute-start = (bf16[64,768]{1,0:T(8,128)(2,1)}, bf16[64,768]{1,0:T(8,128)(2,1)S(1)}, u32[]{:S(2)}, u32[]{:S(2)}) collective-permute-start(bf16[64,768]{1,0:T(8,128)(2,1)} %refs_0_.1), channel_id=1, source_target_pairs={{0,16},{16,32},{32,48},{48,0},{1,17},{17,33},{33,49},{49,1},{2,18}... | collective-permute-start | bytes 294920 | tf_op jit(solution)/shard_map/gather_authors/ppermute | solution.py:18
  5.2 11.1 %collective-permute-start.1 = (bf16[64,768]{1,0:T(8,128)(2,1)}, bf16[64,768]{1,0:T(8,128)(2,1)S(1)}, u32[]{:S(2)}, u32[]{:S(2)}) collective-permute-start(bf16[64,768]{1,0:T(8,128)(2,1)} %refs_0_.1), channel_id=1, source_target_pairs={{0,32},{16,48},{32,0},{48,16},{1,33},{17,49},{33,1},{49,17},{2,34}... | collective-permute-start | bytes 294920 | tf_op jit(solution)/shard_map/gather_authors/ppermute | solution.py:18
  6.2 11.1 %collective-permute-start.2 = (bf16[64,768]{1,0:T(8,128)(2,1)}, bf16[64,768]{1,0:T(8,128)(2,1)S(1)}, u32[]{:S(2)}, u32[]{:S(2)}) collective-permute-start(bf16[64,768]{1,0:T(8,128)(2,1)} %refs_0_.1), channel_id=1, source_target_pairs={{0,48},{16,0},{32,16},{48,32},{1,49},{17,1},{33,17},{49,33},{2,50}... | collective-permute-start | bytes 294920 | tf_op jit(solution)/shard_map/gather_authors/ppermute | solution.py:18
  9.0 8.3 %collective-permute-start.3 = (bf16[64,768]{1,0:T(8,128)(2,1)}, bf16[64,768]{1,0:T(8,128)(2,1)S(1)}, u32[]{:S(2)}, u32[]{:S(2)}) collective-permute-start(bf16[64,768]{1,0:T(8,128)(2,1)} %refs_0_.1), channel_id=1, source_target_pairs={{0,64},{64,128},{128,192},{192,0},{1,65},{65,129},{129,193},{193,1... | collective-permute-start | bytes 294920 | tf_op jit(solution)/shard_map/gather_authors/ppermute | solution.py:18
  10.6 6.9 %collective-permute-start.4 = (bf16[64,768]{1,0:T(8,128)(2,1)}, bf16[64,768]{1,0:T(8,128)(2,1)S(1)}, u32[]{:S(2)}, u32[]{:S(2)}) collective-permute-start(bf16[64,768]{1,0:T(8,128)(2,1)} %refs_0_.1), channel_id=1, source_target_pairs={{0,128},{64,192},{128,0},{192,64},{1,129},{65,193},{129,1},{193,65... | collective-permute-start | bytes 294920 | tf_op jit(solution)/shard_map/gather_authors/ppermute | solution.py:18
  13.5 4.8 %collective-permute-start.5 = (bf16[64,768]{1,0:T(8,128)(2,1)}, bf16[64,768]{1,0:T(8,128)(2,1)S(1)}, u32[]{:S(2)}, u32[]{:S(2)}) collective-permute-start(bf16[64,768]{1,0:T(8,128)(2,1)} %refs_0_.1), channel_id=1, source_target_pairs={{0,192},{64,0},{128,64},{192,128},{1,193},{65,1},{129,65},{193,129... | collective-permute-start | bytes 294920 | tf_op jit(solution)/shard_map/gather_authors/ppermute | solution.py:18
  18.4 14.9 %collective-permute-start.6 = (bf16[3,64,768]{2,1,0:T(8,128)(2,1)S(1)}, bf16[3,64,768]{2,1,0:T(8,128)(2,1)S(1)}, u32[]{:S(2)}, u32[]{:S(2)}) collective-permute-start(bf16[3,64,768]{2,1,0:T(8,128)(2,1)S(1)} %pad_maximum_fusion), channel_id=1, source_target_pairs={{0,64},{64,128},{128,192},{192,0},{1,65},{65,129},{129,193},{193,1... | collective-permute-start | bytes 884744 | tf_op jit(solution)/shard_map/gather_authors/ppermute | solution.py:18
  19.1 15.5 %collective-permute-start.7 = (bf16[3,64,768]{2,1,0:T(8,128)(2,1)S(1)}, bf16[3,64,768]{2,1,0:T(8,128)(2,1)S(1)}, u32[]{:S(2)}, u32[]{:S(2)}) collective-permute-start(bf16[3,64,768]{2,1,0:T(8,128)(2,1)S(1)} %pad_maximum_fusion), channel_id=1, source_target_pairs={{0,128},{64,192},{128,0},{192,64},{1,129},{65,193},{129,1},{193,65... | collective-permute-start | bytes 884744 | tf_op jit(solution)/shard_map/gather_authors/ppermute | solution.py:18
  22.5 12.1 %collective-permute-start.8 = (bf16[3,64,768]{2,1,0:T(8,128)(2,1)S(1)}, bf16[3,64,768]{2,1,0:T(8,128)(2,1)S(1)}, u32[]{:S(2)}, u32[]{:S(2)}) collective-permute-start(bf16[3,64,768]{2,1,0:T(8,128)(2,1)S(1)} %pad_maximum_fusion), channel_id=1, source_target_pairs={{0,192},{64,0},{128,64},{192,128},{1,193},{65,1},{129,65},{193,129... | collective-permute-start | bytes 884744 | tf_op jit(solution)/shard_map/gather_authors/ppermute | solution.py:18
  24.0 1.2 copy-start.4
  25.3 0.7 copy-start.5
  25.9 0.7 copy-start.6
  26.6 0.7 copy-start.7
  27.2 3.8 %copy-start.1 = (bf16[2,768,768]{2,1,0:T(8,128)(2,1)S(1)}, bf16[2,768,768]{2,1,0:T(8,128)(2,1)}, u32[]{:S(2)}) copy-start(bf16[2,768,768]{2,1,0:T(8,128)(2,1)} %refs_4_.1) | copy-start | bytes 7077892
  27.2 3.8 %copy-start.3 = (bf16[64,768]{1,0:T(8,128)(2,1)S(1)}, bf16[64,768]{1,0:T(8,128)(2,1)}, u32[]{:S(2)}) copy-start(bf16[64,768]{1,0:T(8,128)(2,1)} %refs_0_.1) | copy-start | bytes 294916
  44.5 2.4 %collective-permute-start.9 = (bf16[4,2,64,768]{3,2,1,0:T(8,128)(2,1)S(1)}, bf16[4,2,64,768]{3,2,1,0:T(8,128)(2,1)S(1)}, u32[]{:S(2)}, u32[]{:S(2)}) collective-permute-start(bf16[4,2,64,768]{3,2,1,0:T(8,128)(2,1)S(1)} %get-tuple-element.29), channel_id=1, source_target_pairs={{0,1},{1,0},{2,3},{3,2},{4,5},{5,4},{6,7},{7,6},{8,9},{9,8},{10,11... | collective-permute-start | bytes 2359304 | tf_op jit(solution)/shard_map/sum_papers/ppermute | solution.py:22
  46.9 6.1 %copy-start.8 = (bf16[64,768]{1,0:T(8,128)(2,1)S(1)}, bf16[64,768]{1,0:T(8,128)(2,1)}, u32[]{:S(2)}) copy-start(bf16[64,768]{1,0:T(8,128)(2,1)} %param.10) | copy-start | bytes 294916
  47.2 8.2 %collective-permute-start.10 = (bf16[2,64,768]{2,1,0:T(8,128)(2,1)S(1)}, bf16[2,64,768]{2,1,0:T(8,128)(2,1)S(1)}, u32[]{:S(2)}, u32[]{:S(2)}) collective-permute-start(bf16[2,64,768]{2,1,0:T(8,128)(2,1)S(1)} %get-tuple-element.42), channel_id=1, source_target_pairs={{0,4},{4,8},{8,12},{12,0},{1,5},{5,9},{9,13},{13,1},{2,6},{6,10},{... | collective-permute-start | bytes 589832 | tf_op jit(solution)/shard_map/sum_papers/ppermute | solution.py:18
  48.8 11.9 %collective-permute-start.11 = (bf16[2,64,768]{2,1,0:T(8,128)(2,1)S(1)}, bf16[2,64,768]{2,1,0:T(8,128)(2,1)S(1)}, u32[]{:S(2)}, u32[]{:S(2)}) collective-permute-start(bf16[2,64,768]{2,1,0:T(8,128)(2,1)S(1)} %get-tuple-element.44), channel_id=1, source_target_pairs={{0,8},{4,12},{8,0},{12,4},{1,9},{5,13},{9,1},{13,5},{2,10},{6,14},... | collective-permute-start | bytes 589832 | tf_op jit(solution)/shard_map/sum_papers/ppermute | solution.py:18
  51.5 14.0 %copy-start.2 = (bf16[768,768]{1,0:T(8,128)(2,1)S(1)}, bf16[768,768]{1,0:T(8,128)(2,1)}, u32[]{:S(2)}) copy-start(bf16[768,768]{1,0:T(8,128)(2,1)} %w_ref.1) | copy-start | bytes 3538948
  51.5 9.1 %collective-permute-start.12 = (bf16[2,64,768]{2,1,0:T(8,128)(2,1)S(1)}, bf16[2,64,768]{2,1,0:T(8,128)(2,1)S(1)}, u32[]{:S(2)}, u32[]{:S(2)}) collective-permute-start(bf16[2,64,768]{2,1,0:T(8,128)(2,1)S(1)} %get-tuple-element.43), channel_id=1, source_target_pairs={{0,12},{4,0},{8,4},{12,8},{1,13},{5,1},{9,5},{13,9},{2,14},{6,2},{... | collective-permute-start | bytes 589832 | tf_op jit(solution)/shard_map/sum_papers/ppermute | solution.py:18
  60.7 4.7 %collective-permute-start.13 = (bf16[64,768]{1,0:T(8,128)(2,1)S(1)}, bf16[64,768]{1,0:T(8,128)(2,1)S(1)}, u32[]{:S(2)}, u32[]{:S(2)}) collective-permute-start(bf16[64,768]{1,0:T(8,128)(2,1)S(1)} %fusion.9), channel_id=1, source_target_pairs={{0,2},{2,0},{1,3},{3,1},{4,6},{6,4},{5,7},{7,5},{8,10},{10,8},{9,1... | collective-permute-start | bytes 294920 | tf_op jit(solution)/shard_map/sum_papers/ppermute | solution.py:22
  66.2 4.6 %collective-permute-start.14 = (bf16[64,768]{1,0:T(8,128)(2,1)S(1)}, bf16[64,768]{1,0:T(8,128)(2,1)S(1)}, u32[]{:S(2)}, u32[]{:S(2)}) collective-permute-start(bf16[64,768]{1,0:T(8,128)(2,1)S(1)} %get-tuple-element.31), channel_id=1, source_target_pairs={{0,2},{2,0},{1,3},{3,1},{4,6},{6,4},{5,7},{7,5},{8,10},{10,8},{9,1... | collective-permute-start | bytes 294920 | tf_op jit(solution)/shard_map/gather_papers/ppermute | solution.py:22
  70.9 8.8 %collective-permute-start.15 = (bf16[2,64,768]{2,1,0:T(8,128)(2,1)S(1)}, bf16[2,64,768]{2,1,0:T(8,128)(2,1)S(1)}, u32[]{:S(2)}, u32[]{:S(2)}) collective-permute-start(bf16[2,64,768]{2,1,0:T(8,128)(2,1)S(1)} %pad_maximum_fusion.1.refs_0_), channel_id=1, source_target_pairs={{0,4},{4,8},{8,12},{12,0},{1,5},{5,9},{9,13},{13,1},{2,6},{6,10},{... | collective-permute-start | bytes 589832 | tf_op jit(solution)/shard_map/gather_papers/ppermute | solution.py:18
  72.3 9.5 %collective-permute-start.16 = (bf16[2,64,768]{2,1,0:T(8,128)(2,1)S(1)}, bf16[2,64,768]{2,1,0:T(8,128)(2,1)S(1)}, u32[]{:S(2)}, u32[]{:S(2)}) collective-permute-start(bf16[2,64,768]{2,1,0:T(8,128)(2,1)S(1)} %pad_maximum_fusion.1.refs_0_), channel_id=1, source_target_pairs={{0,8},{4,12},{8,0},{12,4},{1,9},{5,13},{9,1},{13,5},{2,10},{6,14},... | collective-permute-start | bytes 589832 | tf_op jit(solution)/shard_map/gather_papers/ppermute | solution.py:18
  74.8 7.0 %collective-permute-start.17 = (bf16[2,64,768]{2,1,0:T(8,128)(2,1)S(1)}, bf16[2,64,768]{2,1,0:T(8,128)(2,1)S(1)}, u32[]{:S(2)}, u32[]{:S(2)}) collective-permute-start(bf16[2,64,768]{2,1,0:T(8,128)(2,1)S(1)} %pad_maximum_fusion.1.refs_0_), channel_id=1, source_target_pairs={{0,12},{4,0},{8,4},{12,8},{1,13},{5,1},{9,5},{13,9},{2,14},{6,2},{... | collective-permute-start | bytes 589832 | tf_op jit(solution)/shard_map/gather_papers/ppermute | solution.py:18
  76.2 6.0 %collective-permute-start.18 = (bf16[2,64,768]{2,1,0:T(8,128)(2,1)S(1)}, bf16[2,64,768]{2,1,0:T(8,128)(2,1)S(1)}, u32[]{:S(2)}, u32[]{:S(2)}) collective-permute-start(bf16[2,64,768]{2,1,0:T(8,128)(2,1)S(1)} %pad_maximum_fusion.1.refs_0_), channel_id=1, source_target_pairs={{0,1},{1,0},{2,3},{3,2},{4,5},{5,4},{6,7},{7,6},{8,9},{9,8},{10,11... | collective-permute-start | bytes 589832 | tf_op jit(solution)/shard_map/gather_papers/ppermute | solution.py:22
  79.7 2.6 %collective-permute-start.19 = (bf16[2,64,768]{2,1,0:T(8,128)(2,1)S(1)}, bf16[2,64,768]{2,1,0:T(8,128)(2,1)S(1)}, u32[]{:S(2)}, u32[]{:S(2)}) collective-permute-start(bf16[2,64,768]{2,1,0:T(8,128)(2,1)S(1)} %collective-permute-done.15.refs_1_), channel_id=1, source_target_pairs={{0,1},{1,0},{2,3},{3,2},{4,5},{5,4},{6,7},{7,6},{8,9},{9,8},{10,11... | collective-permute-start | bytes 589832 | tf_op jit(solution)/shard_map/gather_papers/ppermute | solution.py:22
  81.8 1.4 %collective-permute-start.20 = (bf16[2,64,768]{2,1,0:T(8,128)(2,1)S(1)}, bf16[2,64,768]{2,1,0:T(8,128)(2,1)S(1)}, u32[]{:S(2)}, u32[]{:S(2)}) collective-permute-start(bf16[2,64,768]{2,1,0:T(8,128)(2,1)S(1)} %collective-permute-done.16.refs_2_), channel_id=1, source_target_pairs={{0,1},{1,0},{2,3},{3,2},{4,5},{5,4},{6,7},{7,6},{8,9},{9,8},{10,11... | collective-permute-start | bytes 589832 | tf_op jit(solution)/shard_map/gather_papers/ppermute | solution.py:22
  81.8 1.7 %collective-permute-start.21 = (bf16[2,64,768]{2,1,0:T(8,128)(2,1)S(1)}, bf16[2,64,768]{2,1,0:T(8,128)(2,1)S(1)}, u32[]{:S(2)}, u32[]{:S(2)}) collective-permute-start(bf16[2,64,768]{2,1,0:T(8,128)(2,1)S(1)} %collective-permute-done.17.refs_3_), channel_id=1, source_target_pairs={{0,1},{1,0},{2,3},{3,2},{4,5},{5,4},{6,7},{7,6},{8,9},{9,8},{10,11... | collective-permute-start | bytes 589832 | tf_op jit(solution)/shard_map/gather_papers/ppermute | solution.py:22
  88.3 17.0 %collective-permute-start.25 = (bf16[3,64,768]{2,1,0:T(8,128)(2,1)S(1)}, bf16[3,64,768]{2,1,0:T(8,128)(2,1)S(1)}, u32[]{:S(2)}, u32[]{:S(2)}) collective-permute-start(bf16[3,64,768]{2,1,0:T(8,128)(2,1)S(1)} %get-tuple-element.37), channel_id=1, source_target_pairs={{0,64},{64,128},{128,192},{192,0},{1,65},{65,129},{129,193},{193,1... | collective-permute-start | bytes 884744 | tf_op jit(solution)/shard_map/sum_authors/ppermute | solution.py:18
  89.7 16.6 %collective-permute-start.26 = (bf16[3,64,768]{2,1,0:T(8,128)(2,1)S(1)}, bf16[3,64,768]{2,1,0:T(8,128)(2,1)S(1)}, u32[]{:S(2)}, u32[]{:S(2)}) collective-permute-start(bf16[3,64,768]{2,1,0:T(8,128)(2,1)S(1)} %get-tuple-element.38), channel_id=1, source_target_pairs={{0,128},{64,192},{128,0},{192,64},{1,129},{65,193},{129,1},{193,65... | collective-permute-start | bytes 884744 | tf_op jit(solution)/shard_map/sum_authors/ppermute | solution.py:18
  92.0 14.7 %collective-permute-start.27 = (bf16[3,64,768]{2,1,0:T(8,128)(2,1)S(1)}, bf16[3,64,768]{2,1,0:T(8,128)(2,1)S(1)}, u32[]{:S(2)}, u32[]{:S(2)}) collective-permute-start(bf16[3,64,768]{2,1,0:T(8,128)(2,1)S(1)} %get-tuple-element.39), channel_id=1, source_target_pairs={{0,192},{64,0},{128,64},{192,128},{1,193},{65,1},{129,65},{193,129... | collective-permute-start | bytes 884744 | tf_op jit(solution)/shard_map/sum_authors/ppermute | solution.py:18
  93.6 19.0 %collective-permute-start.22 = (bf16[64,768]{1,0:T(8,128)(2,1)S(1)}, bf16[64,768]{1,0:T(8,128)(2,1)S(1)}, u32[]{:S(2)}, u32[]{:S(2)}) collective-permute-start(bf16[64,768]{1,0:T(8,128)(2,1)S(1)} %get-tuple-element.34), channel_id=1, source_target_pairs={{0,64},{64,128},{128,192},{192,0},{1,65},{65,129},{129,193},{193,1... | collective-permute-start | bytes 294920 | tf_op jit(solution)/shard_map/sum_authors/ppermute | solution.py:18
  94.1 20.7 %collective-permute-start.23 = (bf16[64,768]{1,0:T(8,128)(2,1)S(1)}, bf16[64,768]{1,0:T(8,128)(2,1)S(1)}, u32[]{:S(2)}, u32[]{:S(2)}) collective-permute-start(bf16[64,768]{1,0:T(8,128)(2,1)S(1)} %get-tuple-element.35), channel_id=1, source_target_pairs={{0,128},{64,192},{128,0},{192,64},{1,129},{65,193},{129,1},{193,65... | collective-permute-start | bytes 294920 | tf_op jit(solution)/shard_map/sum_authors/ppermute | solution.py:18
  105.3 9.4 %collective-permute-start.24 = (bf16[64,768]{1,0:T(8,128)(2,1)S(1)}, bf16[64,768]{1,0:T(8,128)(2,1)S(1)}, u32[]{:S(2)}, u32[]{:S(2)}) collective-permute-start(bf16[64,768]{1,0:T(8,128)(2,1)S(1)} %get-tuple-element.36), channel_id=1, source_target_pairs={{0,192},{64,0},{128,64},{192,128},{1,193},{65,1},{129,65},{193,129... | collective-permute-start | bytes 294920 | tf_op jit(solution)/shard_map/sum_authors/ppermute | solution.py:18
  106.9 7.9 %collective-permute-start.28 = (bf16[64,768]{1,0:T(8,128)(2,1)S(1)}, bf16[64,768]{1,0:T(8,128)(2,1)S(1)}, u32[]{:S(2)}, u32[]{:S(2)}) collective-permute-start(bf16[64,768]{1,0:T(8,128)(2,1)S(1)} %get-tuple-element.45), channel_id=1, source_target_pairs={{0,16},{16,32},{32,48},{48,0},{1,17},{17,33},{33,49},{49,1},{2,18}... | collective-permute-start | bytes 294920 | tf_op jit(solution)/shard_map/sum_authors/ppermute | solution.py:18
  110.9 9.9 %collective-permute-start.29 = (bf16[64,768]{1,0:T(8,128)(2,1)S(1)}, bf16[64,768]{1,0:T(8,128)(2,1)S(1)}, u32[]{:S(2)}, u32[]{:S(2)}) collective-permute-start(bf16[64,768]{1,0:T(8,128)(2,1)S(1)} %get-tuple-element.47), channel_id=1, source_target_pairs={{0,32},{16,48},{32,0},{48,16},{1,33},{17,49},{33,1},{49,17},{2,34}... | collective-permute-start | bytes 294920 | tf_op jit(solution)/shard_map/sum_authors/ppermute | solution.py:18
  112.7 9.6 %collective-permute-start.30 = (bf16[64,768]{1,0:T(8,128)(2,1)S(1)}, bf16[64,768]{1,0:T(8,128)(2,1)S(1)}, u32[]{:S(2)}, u32[]{:S(2)}) collective-permute-start(bf16[64,768]{1,0:T(8,128)(2,1)S(1)} %get-tuple-element.46), channel_id=1, source_target_pairs={{0,48},{16,0},{32,16},{48,32},{1,49},{17,1},{33,17},{49,33},{2,50}... | collective-permute-start | bytes 294920 | tf_op jit(solution)/shard_map/sum_authors/ppermute | solution.py:18

commit v3 on v2

v3 whole, which is shorter than its diff:
```python
import functools

import jax
import jax.numpy as jnp
from jax import lax
from jax.experimental import pallas as pl
from jax.experimental.pallas import tpu as pltpu
from jax.sharding import Mesh
from jax.sharding import PartitionSpec as P

PROW = ("y", "zh")
PCOL = ("x", "zl", "core")
F32 = jnp.float32
BF16 = jnp.bfloat16
VMEM_LIMIT = 24 * 2**20
PLACE = 5
RING = 4


def shift(value, axis, by):
    return lax.ppermute(value, axis, [(i, (i + by) % RING) for i in range(RING)])


def swap(value, axis):
    return lax.ppermute(value, axis, [(0, 1), (1, 0)])


def behind(at, by):
    return lax.rem(at + (RING - by), RING)


def build_tiles(place, vals_ref, one_ref, two_ref, vals, sem):
    y, zh, x, zl, core = (place[i] for i in range(PLACE))
    slots, side = vals.shape[:2]
    half = side // 2
    span = RING * half
    relations = one_ref.shape[1] // two_ref.shape[1]
    load = pltpu.make_async_copy(vals_ref, vals, sem)
    load.start()
    one_ref[...] = jnp.zeros_like(one_ref)
    two_ref[...] = jnp.zeros_like(two_ref)
    load.wait()

    def slot(k, carry):
        row, col, kind = (place[PLACE + 1 + i * slots + k] for i in range(3))
        block = vals[k]
        turned = block.T
        d = lax.rem(y + RING - lax.div(col, 2), RING)
        group = jnp.where(d == 2, 3, jnp.where(d == 3, 2, d))
        at = (group * relations + kind) * span + lax.rem(col, 2) * side
        lanes = pl.ds(pl.multiple_of(at, side), side)
        d = lax.rem(lax.div(row, 2) + RING - x, RING)
        e = jnp.where(lax.rem(row, 2) == zl, 0, 1)
        for c in range(2):
            at = jnp.where(core == c, 0, RING * side) + d * side + e * half
            one_ref[pl.ds(pl.multiple_of(at, half), half), lanes] = block[c * half : (c + 1) * half]
        lanes = pl.ds(pl.multiple_of(row * side, side), side)
        d = lax.rem(lax.div(col, 2) + RING - y, RING)
        for c in range(2):
            e = lax.rem(lax.rem(col, 2) * 2 + c + RING - zh, RING)
            place_of = jnp.where(e == 2, 0, jnp.where(e == 3, 3, e + 1))
            at = d * span + place_of * half
            two_ref[pl.ds(pl.multiple_of(at, half), half), lanes] = turned[c * half : (c + 1) * half]
        return carry

    lax.fori_loop(0, place[PLACE], slot, 0)


def copy_all(pairs, sem):
    copies = [pltpu.make_async_copy(src, dst, sem.at[i]) for i, (src, dst) in enumerate(pairs)]
    for c in copies:
        c.start()
    return copies


def add_part(first, split, has_base, is_last, place, *refs):
    pieces, refs = refs[: len(split)], refs[len(split) :]
    tile_ref, w_ref = refs[:2]
    base_ref, refs = (refs[2], refs[3:]) if has_base else (None, refs[2:])
    outs, (table, msgs, tile, sem) = refs[:-4], refs[-4:]
    relations = w_ref.shape[0]
    span = tile.shape[0] // RING
    own = span // RING
    pairs = []
    for piece, chunks in zip(pieces, split, strict=True):
        for i, (group, e) in enumerate(chunks):
            at = pl.multiple_of((group * RING + behind(place[1], e)) * own, own)
            pairs.append((piece.at[pl.ds(i * own, own), :], table.at[pl.ds(at, own), :]))
    copies = copy_all([*pairs, (tile_ref.at[:, pl.ds(first * relations * span, tile.shape[1])], tile)], sem)
    for c in copies[:-1]:
        c.wait()
    for r in range(relations):
        made = jnp.dot(table[...], w_ref[r], preferred_element_type=F32).astype(BF16)
        for i in range(table.shape[0] // span):
            at = (i * relations + r) * span
            msgs[at : at + span, :] = made[i * span : (i + 1) * span]
    copies[-1].wait()
    for step in range(RING):
        at = slice(step * span, (step + 1) * span)
        made = jnp.dot(tile[at, :], msgs[...], preferred_element_type=F32)
        if has_base:
            made += base_ref[at, :]
        if is_last:
            out = outs[step // 2]
            half = step % 2 * 2
            out[half : half + 2] = made.reshape(2, *out.shape[1:]).astype(out.dtype)
        else:
            outs[0][at, :] = made


def hop_two(place, *refs):
    mine, other, refs = refs[:4], refs[4:8], refs[8:]
    tile_ref, same_ref, up_ref, down_ref, two_up_ref, two_down_ref, table, tile, sem = refs
    x, zl, core = (place[i] for i in range(2, 5))
    own, width = same_ref.shape[1:]
    span = RING * own
    pairs = [(tile_ref, tile)]
    for d in range(RING):
        for e in range(2):
            block = (behind(x, d) * 2 + (zl if e == 0 else 1 - zl)) * 2
            for source, c in ((mine, core), (other, 1 - core)):
                at = pl.ds(pl.multiple_of((block + c) * own, own), own)
                pairs.append((source[d].at[e], table.at[at, :]))
    for c in copy_all(pairs, sem):
        c.wait()
    for d in range(RING):
        made = jnp.dot(tile[pl.ds(d * span, span), :], table[...], preferred_element_type=F32)
        made = made.reshape(RING, own, width)
        if d == 2:
            two_up_ref[...] = made[:, : own // 2].astype(BF16)
            two_down_ref[...] = made[:, own // 2 :].astype(BF16)
        else:
            out = (same_ref, up_ref, None, down_ref)[d]
            out[...] = made


def hidden_step(base_ref, got_ref, w_ref, hidden_ref, out_ref):
    first = jnp.maximum(base_ref[0] + got_ref[1].astype(F32), 0.0).astype(BF16)
    second = jnp.maximum(base_ref[1] + got_ref[0].astype(F32), 0.0).astype(BF16)
    hidden_ref[...] = first
    both = jnp.concatenate([first, second])
    out_ref[...] = jnp.dot(both, w_ref[...], preferred_element_type=F32).astype(BF16).reshape(out_ref.shape)


def call(kernel, flops, scalars, loose, arrays, out_shape, scratch, loose_space=pl.ANY):
    def spec(kind):
        return pl.BlockSpec(memory_space=kind)

    return pl.pallas_call(
        kernel,
        out_shape=out_shape,
        in_specs=[spec(pltpu.SMEM)] * len(scalars) + [spec(loose_space)] * len(loose) + [spec(pltpu.VMEM)] * len(arrays),
        out_specs=jax.tree.map(lambda _: spec(pltpu.VMEM), out_shape),
        scratch_shapes=scratch,
        compiler_params=pltpu.CompilerParams(vmem_limit_bytes=VMEM_LIMIT),
        cost_estimate=pl.CostEstimate(flops=flops, bytes_accessed=4 * 2**20, transcendentals=0),
    )(*scalars, *loose, *arrays)


def total_of(parts):
    return sum(p.astype(F32) for p in parts)


def per_device(paper_x, author_x, w_self, w_rel, w_two, block_rows, block_cols, block_type, block_count, block_vals):
    slots = block_rows.shape[2]
    side = block_vals.shape[3]
    own, width = paper_x.shape
    vals = block_vals.reshape(slots, side, side)
    at = jnp.stack([lax.axis_index(a).astype(jnp.int32) for a in (*PROW, *PCOL)])
    place = jnp.concatenate([at, *(a.reshape(-1) for a in (block_count, block_rows, block_cols, block_type))])
    tile_rows = 16 * own

    def shaped(*dims, dtype=BF16):
        return jax.ShapeDtypeStruct((*dims, own, width), dtype)

    relations = w_rel.shape[0]
    sems = pltpu.SemaphoreType.DMA
    tile_one, tile_two = call(
        build_tiles,
        10**9,
        (place,),
        (vals,),
        (),
        (
            jax.ShapeDtypeStruct((tile_rows, relations * tile_rows), BF16),
            jax.ShapeDtypeStruct((tile_rows, tile_rows), BF16),
        ),
        [pltpu.VMEM(vals.shape, BF16), sems(())],
        pltpu.HBM,
    )
    self_term = jnp.dot(paper_x, w_self, preferred_element_type=F32)
    span = RING * own

    def part(first, groups, split, pieces, base, out_shape):
        return call(
            functools.partial(add_part, first, split, base is not None, first + groups == RING),
            10**9,
            (place,),
            (*pieces, tile_one),
            (w_rel,) if base is None else (w_rel, base),
            out_shape,
            [
                pltpu.VMEM((groups * span, width), BF16),
                pltpu.VMEM((groups * relations * span, width), BF16),
                pltpu.VMEM((tile_rows, groups * relations * span), BF16),
                sems((RING * groups + 1,)),
            ],
        )

    base_shape = jax.ShapeDtypeStruct((tile_rows, width), F32)
    with jax.named_scope("gather_authors"):
        by_z = [shift(author_x, "zh", e) for e in range(1, RING)]
        by_z, tile_one, tile_two = lax.optimization_barrier((by_z, tile_one, tile_two))
        relay = jnp.concatenate([author_x, *by_z])
        ups, downs = shift(relay, "y", 1), shift(relay, "y", RING - 1)
    base = part(0, 1, [[(0, e)] for e in range(RING)], (author_x, *by_z), None, base_shape)
    with jax.named_scope("forward_authors"):
        ups, downs, base = lax.optimization_barrier((ups, downs, base))
        up_two = shift(ups[: 2 * own], "y", 1)
        down_two = shift(downs[2 * own :], "y", RING - 1)
    base = part(1, 2, [[(g, e) for e in range(RING)] for g in range(2)], (ups, downs), base, base_shape)
    keep, send = part(
        3,
        1,
        [[(0, 0), (0, 1)], [(0, 2), (0, 3)]],
        (up_two, down_two),
        base,
        (shaped(RING, 2, dtype=F32), shaped(RING, 2)),
    )
    with jax.named_scope("sum_papers"):
        pair = keep + swap(send, "core").astype(F32)
        by_x = [shift(pair[d].astype(BF16), "x", d) for d in range(1, RING)]
        both = total_of([pair[0], *by_x])
        both = jnp.stack([both[0] + self_term, both[1]])
        got = swap(both.astype(BF16), "zl")
    paper_hidden, outgoing = call(
        hidden_step, 4 * own * width * width, (), (), (both, got, w_two), (shaped(), shaped(2)), []
    )
    with jax.named_scope("gather_papers"):
        mine = [outgoing, *(shift(outgoing, "x", d) for d in range(1, RING))]
        other = [swap(m, "core") for m in mine]
    whole = shaped(RING, dtype=F32)
    piece = jax.ShapeDtypeStruct((RING, own // 2, width), BF16)
    same, up, down, two_up, two_down = call(
        hop_two,
        10**9,
        (place,),
        (*mine, *other, tile_two),
        (),
        (whole, whole, whole, piece, piece),
        [pltpu.VMEM((tile_rows, width), BF16), pltpu.VMEM((tile_rows, tile_rows), BF16), sems((17,))],
    )
    with jax.named_scope("sum_authors"):
        half = own // 2
        from_down = shift(two_up, "y", 1).astype(F32)
        from_up = shift(two_down, "y", RING - 1).astype(F32)
        up = jnp.concatenate([up[:, :half] + from_down, up[:, half:]], axis=1).astype(BF16)
        down = jnp.concatenate([down[:, :half], down[:, half:] + from_up], axis=1).astype(BF16)
        opposite = total_of([same[0], shift(up[0], "y", 1), shift(down[0], "y", RING - 1)])
        rest = total_of([same[1:], shift(up[1:], "y", 1), shift(down[1:], "y", RING - 1)])
        by_z = [
            shift(opposite.astype(BF16), "zh", 2),
            shift(rest[1].astype(BF16), "zh", 1),
            shift(rest[2].astype(BF16), "zh", RING - 1),
        ]
        author_out = total_of([rest[0], *by_z]).astype(BF16)
    return paper_hidden, author_out


def solution(mesh):
    split = Mesh(mesh.devices.reshape(4, 4, 4, 2, 2), (*PROW, *PCOL))
    tile = P(PROW, PCOL)
    return jax.shard_map(
        per_device,
        mesh=split,
        in_specs=(P((*PROW, *PCOL)), P((*PCOL, *PROW)), P(), P(), P(), tile, tile, tile, tile, tile),
        out_specs=(P((*PROW, *PCOL)), P((*PCOL, *PROW))),
        check_vma=False,
    )
```

time: 125 us -> 119 us (0.952); the launches traced: 123 us -> 118 us
  starting transfers between devices: 46.7 us -> 43.8 us
  Pallas kernels: 21.5 us -> 19.2 us
    ppermute x24 -> x22, waiting for transfers between devices: 36.8 us -> 41 us  [shift(): lax.ppermute(value, axis, [(i, (i + by) % RING) for i in range(RING)])]
    ppermute x7 -> x6, waiting for transfers between devices: 11.7 us -> 8.05 us  [swap(): return lax.ppermute(value, axis, [(0, 1), (1, 0)])]
    ppermute x24 -> x22, starting transfers between devices: 45 us -> 41.6 us  [shift(): lax.ppermute(value, axis, [(i, (i + by) % RING) for i in range(RING)])]
    pallas_call x5 -> x6, Pallas kernels: 21.5 us -> 19.2 us  [call(): pl.pallas_call(kernel, out_shape=out_shape, in_specs=[spec(pltpu.SMEM)] *...]
    unnamed x18 -> x15, local copies, waits for them, and re-layouts: 3.21 us -> 2.21 us
  transfers between devices with their start and end apart: 31 -> 28, of which waited for: 19 -> 18; matrix products, arithmetic and copies ran while one was open for 0% -> 2% of each run, Pallas kernels for 5% -> 9%
where the time goes in v3:
time: 119 us; the launch traced here: 118 us
  waiting for transfers between devices  49.1 us (41%)
  starting transfers between devices  43.8 us (37%)
  Pallas kernels  19.2 us (16%)
  local copies, waits for them, and re-layouts  3.13 us (3%)
  between operations  1.62 us (1%)
  other arithmetic  1.35 us (1%)
    ppermute x22, starting transfers between devices, shift(): lax.ppermute(value, axis, [(i, (i + by) % RING) for i in range(RING)])  41.6 us
    ppermute x22, waiting for transfers between devices, shift(): lax.ppermute(value, axis, [(i, (i + by) % RING) for i in range(RING)])  41 us
    pallas_call x6, Pallas kernels, call(): pl.pallas_call(kernel, out_shape=out_shape, in_specs=[spec(pltpu.SMEM)] *...  19.2 us
    ppermute x6, waiting for transfers between devices, swap(): return lax.ppermute(value, axis, [(0, 1), (1, 0)])  8.05 us
  transfers between devices with their start and end apart: 28, of which 18 were waited for; matrix products, arithmetic and copies ran while one was open for 2% of the time, Pallas kernels for 9%

profile of v3, /device:TPU:64, one launch (start us, length us, event | category | flops | bytes accessed | tf_op | source)
XLA Modules:
  0.0 118.5 jit_solution(3700761176543904411)
XLA Ops:
  0.6 0.0 copy-start
  0.6 1.5 %collective-permute-start.2 = (bf16[64,768]{1,0:T(8,128)(2,1)}, bf16[64,768]{1,0:T(8,128)(2,1)S(1)}, u32[]{:S(2)}, u32[]{:S(2)}) collective-permute-start(bf16[64,768]{1,0:T(8,128)(2,1)} %refs_0_.1), channel_id=1, source_target_pairs={{0,48},{16,0},{32,16},{48,32},{1,49},{17,1},{33,17},{49,33},{2,50}... | collective-permute-start | bytes 294920 | tf_op jit(solution)/shard_map/gather_authors/ppermute | solution.py:21
  2.1 5.5 %collective-permute-start.1 = (bf16[64,768]{1,0:T(8,128)(2,1)}, bf16[64,768]{1,0:T(8,128)(2,1)S(1)}, u32[]{:S(2)}, u32[]{:S(2)}) collective-permute-start(bf16[64,768]{1,0:T(8,128)(2,1)} %refs_0_.1), channel_id=1, source_target_pairs={{0,32},{16,48},{32,0},{48,16},{1,33},{17,49},{33,1},{49,17},{2,34}... | collective-permute-start | bytes 294920 | tf_op jit(solution)/shard_map/gather_authors/ppermute | solution.py:21
  7.6 2.7 %collective-permute-start = (bf16[64,768]{1,0:T(8,128)(2,1)}, bf16[64,768]{1,0:T(8,128)(2,1)S(1)}, u32[]{:S(2)}, u32[]{:S(2)}) collective-permute-start(bf16[64,768]{1,0:T(8,128)(2,1)} %refs_0_.1), channel_id=1, source_target_pairs={{0,16},{16,32},{32,48},{48,0},{1,17},{17,33},{33,49},{49,1},{2,18}... | collective-permute-start | bytes 294920 | tf_op jit(solution)/shard_map/gather_authors/ppermute | solution.py:21
  10.2 0.9 constant_dynamic-update-slice_fusion.3
  11.8 0.8 concatenate.14.place
  12.6 1.2 %copy-done.4 = bf16[1,1,32,128,128]{4,3,2,1,0:T(8,128)(2,1)S(1)} copy-done((bf16[1,1,32,128,128]{4,3,2,1,0:T(8,128)(2,1)S(1)}, bf16[1,1,32,128,128]{4,3,2,1,0:T(8,128)(2,1)}, u32[]{:S(2)}) %copy-start.4) | copy-done | bytes 1048600
  13.8 2.1 %shard_map.113 = (bf16[1024,2048]{1,0:T(8,128)(2,1)S(1)}, bf16[1024,1024]{1,0:T(8,128)(2,1)S(1)}) custom-call(s32[102]{0:T(128)S(1)} %concatenate.14.place, bf16[32,128,128]{2,1,0:T(8,128)(2,1)S(1)} %bitcast.59), custom_call_target="tpu_custom_call" | custom-call | flops 1000000000 | bytes 4194304 | tf_op jit(solution)/shard_map/pallas_call | solution.py:149
  16.0 0.0 collective-permute-done.2.refs_3_
  16.0 0.0 collective-permute-done.refs_1_
  16.0 4.0 %collective-permute-start.4 = (bf16[256,768]{1,0:T(8,128)(2,1)S(1)}, bf16[256,768]{1,0:T(8,128)(2,1)S(1)}, u32[]{:S(2)}, u32[]{:S(2)}) collective-permute-start(bf16[256,768]{1,0:T(8,128)(2,1)S(1)} %constant_dynamic-update-slice_fusion), channel_id=1, source_target_pairs={{0,192},{64,0},{128,64},{192,128},{1,193},{65,1},{129,65},{193,129... | collective-permute-start | bytes 1179656 | tf_op jit(solution)/shard_map/gather_authors/ppermute | solution.py:21
  20.1 3.0 %shard_map.114.refs_4_ = f32[1024,768]{1,0:T(8,128)S(1)} custom-call(s32[102]{0:T(128)S(1)} %concatenate.14.place, bf16[64,768]{1,0:T(8,128)(2,1)S(1)} %copy-done.3, bf16[64,768]{1,0:T(8,128)(2,1)S(1)} %collective-permute-done.refs_1_, bf16[64,768]{1,0:T(8,128)(2,1)S(1)} %collective-permute-done.1.refs_2_, ...), custom_call_target="tpu_custom_call" | custom-call | flops 1000000000 | bytes 4194304 | tf_op jit(solution)/shard_map/pallas_call | solution.py:149
  23.1 4.4 %collective-permute-done.4.refs_1_ = bf16[256,768]{1,0:T(8,128)(2,1)S(1)} collective-permute-done((bf16[256,768]{1,0:T(8,128)(2,1)S(1)}, bf16[256,768]{1,0:T(8,128)(2,1)S(1)}, u32[]{:S(2)}, u32[]{:S(2)}) %collective-permute-start.4) | collective-permute-done | bytes 393248 | tf_op jit(solution)/shard_map/gather_authors/ppermute | solution.py:21
  27.5 3.4 %collective-permute-done.3.refs_0_ = bf16[256,768]{1,0:T(8,128)(2,1)S(1)} collective-permute-done((bf16[256,768]{1,0:T(8,128)(2,1)S(1)}, bf16[256,768]{1,0:T(8,128)(2,1)S(1)}, u32[]{:S(2)}, u32[]{:S(2)}) %collective-permute-start.3) | collective-permute-done | bytes 393248 | tf_op jit(solution)/shard_map/gather_authors/ppermute | solution.py:21
  31.0 0.1 collective-permute-start.5
  31.1 3.2 %collective-permute-start.6 = (bf16[128,768]{1,0:T(8,128)(2,1)S(1)}, bf16[128,768]{1,0:T(8,128)(2,1)S(1)}, u32[]{:S(2)}, u32[]{:S(2)}) collective-permute-start(bf16[128,768]{1,0:T(8,128)(2,1)S(1)} %slice.71), channel_id=1, source_target_pairs={{0,192},{64,0},{128,64},{192,128},{1,193},{65,1},{129,65},{193,129... | collective-permute-start | bytes 589832 | tf_op jit(solution)/shard_map/forward_authors/ppermute | solution.py:21
  34.3 5.2 %shard_map.115.refs_4_ = f32[1024,768]{1,0:T(8,128)S(1)} custom-call(s32[102]{0:T(128)S(1)} %concatenate.14.place, bf16[256,768]{1,0:T(8,128)(2,1)S(1)} %collective-permute-done.3.refs_0_, bf16[256,768]{1,0:T(8,128)(2,1)S(1)} %collective-permute-done.4.refs_1_, bf16[1024,2048]{1,0:T(8,128)(2,1)S(1)} %get-tuple-element.26.refs_4_.refs_2_, ...), custom_call_target="tpu_custom_call" | custom-call | flops 1000000000 | bytes 4194304 | tf_op jit(solution)/shard_map/pallas_call | solution.py:149
  39.5 3.1 %shard_map.116 = (f32[4,2,64,768]{3,2,1,0:T(8,128)S(1)}, bf16[4,2,64,768]{3,2,1,0:T(8,128)(2,1)S(1)}) custom-call(s32[102]{0:T(128)S(1)} %concatenate.14.place, bf16[128,768]{1,0:T(8,128)(2,1)S(1)} %collective-permute-done.5.refs_0_, bf16[128,768]{1,0:T(8,128)(2,1)S(1)} %collective-permute-done.6.refs_1_, ...), custom_call_target="tpu_custom_call" | custom-call | flops 1000000000 | bytes 4194304 | tf_op jit(solution)/shard_map/pallas_call | solution.py:149
  42.6 0.1 collective-permute-start.7
  42.7 2.3 %collective-permute-done.7 = bf16[4,2,64,768]{3,2,1,0:T(8,128)(2,1)S(1)} collective-permute-done((bf16[4,2,64,768]{3,2,1,0:T(8,128)(2,1)S(1)}, bf16[4,2,64,768]{3,2,1,0:T(8,128)(2,1)S(1)}, u32[]{:S(2)}, u32[]{:S(2)}) %collective-permute-start.7) | collective-permute-done | bytes 786464 | tf_op jit(solution)/shard_map/sum_papers/ppermute | solution.py:25
  45.0 0.2 fusion.17
  45.2 0.0 copy-start.5
  45.3 1.8 %collective-permute-start.8 = (bf16[2,64,768]{2,1,0:T(8,128)(2,1)S(1)}, bf16[2,64,768]{2,1,0:T(8,128)(2,1)S(1)}, u32[]{:S(2)}, u32[]{:S(2)}) collective-permute-start(bf16[2,64,768]{2,1,0:T(8,128)(2,1)S(1)} %get-tuple-element.44), channel_id=1, source_target_pairs={{0,4},{4,8},{8,12},{12,0},{1,5},{5,9},{9,13},{13,1},{2,6},{6,10},{... | collective-permute-start | bytes 589832 | tf_op jit(solution)/shard_map/sum_papers/ppermute | solution.py:21
  47.1 1.7 %collective-permute-start.10 = (bf16[2,64,768]{2,1,0:T(8,128)(2,1)S(1)}, bf16[2,64,768]{2,1,0:T(8,128)(2,1)S(1)}, u32[]{:S(2)}, u32[]{:S(2)}) collective-permute-start(bf16[2,64,768]{2,1,0:T(8,128)(2,1)S(1)} %get-tuple-element.45), channel_id=1, source_target_pairs={{0,12},{4,0},{8,4},{12,8},{1,13},{5,1},{9,5},{13,9},{2,14},{6,2},{... | collective-permute-start | bytes 589832 | tf_op jit(solution)/shard_map/sum_papers/ppermute | solution.py:21
  48.8 1.3 %collective-permute-start.9 = (bf16[2,64,768]{2,1,0:T(8,128)(2,1)S(1)}, bf16[2,64,768]{2,1,0:T(8,128)(2,1)S(1)}, u32[]{:S(2)}, u32[]{:S(2)}) collective-permute-start(bf16[2,64,768]{2,1,0:T(8,128)(2,1)S(1)} %get-tuple-element.46), channel_id=1, source_target_pairs={{0,8},{4,12},{8,0},{12,4},{1,9},{5,13},{9,1},{13,5},{2,10},{6,14},... | collective-permute-start | bytes 589832 | tf_op jit(solution)/shard_map/sum_papers/ppermute | solution.py:21
  50.1 3.6 %collective-permute-done.8 = bf16[2,64,768]{2,1,0:T(8,128)(2,1)S(1)} collective-permute-done((bf16[2,64,768]{2,1,0:T(8,128)(2,1)S(1)}, bf16[2,64,768]{2,1,0:T(8,128)(2,1)S(1)}, u32[]{:S(2)}, u32[]{:S(2)}) %collective-permute-start.8) | collective-permute-done | bytes 196640 | tf_op jit(solution)/shard_map/sum_papers/ppermute | solution.py:21
  53.7 1.2 %collective-permute-done.10 = bf16[2,64,768]{2,1,0:T(8,128)(2,1)S(1)} collective-permute-done((bf16[2,64,768]{2,1,0:T(8,128)(2,1)S(1)}, bf16[2,64,768]{2,1,0:T(8,128)(2,1)S(1)}, u32[]{:S(2)}, u32[]{:S(2)}) %collective-permute-start.10) | collective-permute-done | bytes 196640 | tf_op jit(solution)/shard_map/sum_papers/ppermute | solution.py:21
  54.9 4.1 %collective-permute-done.9 = bf16[2,64,768]{2,1,0:T(8,128)(2,1)S(1)} collective-permute-done((bf16[2,64,768]{2,1,0:T(8,128)(2,1)S(1)}, bf16[2,64,768]{2,1,0:T(8,128)(2,1)S(1)}, u32[]{:S(2)}, u32[]{:S(2)}) %collective-permute-start.9) | collective-permute-done | bytes 196640 | tf_op jit(solution)/shard_map/sum_papers/ppermute | solution.py:21
  59.0 0.1 fusion.2
  59.2 0.0 copy-start.2
  59.2 0.3 fusion.10
  59.5 2.1 %collective-permute-start.11 = (bf16[2,64,768]{2,1,0:T(8,128)(2,1)S(1)}, bf16[2,64,768]{2,1,0:T(8,128)(2,1)S(1)}, u32[]{:S(2)}, u32[]{:S(2)}) collective-permute-start(bf16[2,64,768]{2,1,0:T(8,128)(2,1)S(1)} %fusion.15), channel_id=1, source_target_pairs={{0,2},{2,0},{1,3},{3,1},{4,6},{6,4},{5,7},{7,5},{8,10},{10,8},{9,1... | collective-permute-start | bytes 589832 | tf_op jit(solution)/shard_map/sum_papers/ppermute | solution.py:25
  61.6 4.3 %collective-permute-done.11.got_ref = bf16[2,64,768]{2,1,0:T(8,128)(2,1)S(1)} collective-permute-done((bf16[2,64,768]{2,1,0:T(8,128)(2,1)S(1)}, bf16[2,64,768]{2,1,0:T(8,128)(2,1)S(1)}, u32[]{:S(2)}, u32[]{:S(2)}) %collective-permute-start.11) | collective-permute-done | bytes 196640 | tf_op jit(solution)/shard_map/sum_papers/ppermute | solution.py:25
  66.0 0.8 shard_map.117
  66.8 1.4 %collective-permute-start.14 = (bf16[2,64,768]{2,1,0:T(8,128)(2,1)S(1)}, bf16[2,64,768]{2,1,0:T(8,128)(2,1)S(1)}, u32[]{:S(2)}, u32[]{:S(2)}) collective-permute-start(bf16[2,64,768]{2,1,0:T(8,128)(2,1)S(1)} %get-tuple-element.33.refs_0_), channel_id=1, source_target_pairs={{0,12},{4,0},{8,4},{12,8},{1,13},{5,1},{9,5},{13,9},{2,14},{6,2},{... | collective-permute-start | bytes 589832 | tf_op jit(solution)/shard_map/gather_papers/ppermute | solution.py:21
  68.2 1.5 %collective-permute-start.13 = (bf16[2,64,768]{2,1,0:T(8,128)(2,1)S(1)}, bf16[2,64,768]{2,1,0:T(8,128)(2,1)S(1)}, u32[]{:S(2)}, u32[]{:S(2)}) collective-permute-start(bf16[2,64,768]{2,1,0:T(8,128)(2,1)S(1)} %get-tuple-element.33.refs_0_), channel_id=1, source_target_pairs={{0,8},{4,12},{8,0},{12,4},{1,9},{5,13},{9,1},{13,5},{2,10},{6,14},... | collective-permute-start | bytes 589832 | tf_op jit(solution)/shard_map/gather_papers/ppermute | solution.py:21
  69.7 0.0 collective-permute-start.12
  69.7 0.0 collective-permute-start.15
  69.7 4.7 %collective-permute-done.14.refs_3_ = bf16[2,64,768]{2,1,0:T(8,128)(2,1)S(1)} collective-permute-done((bf16[2,64,768]{2,1,0:T(8,128)(2,1)S(1)}, bf16[2,64,768]{2,1,0:T(8,128)(2,1)S(1)}, u32[]{:S(2)}, u32[]{:S(2)}) %collective-permute-start.14) | collective-permute-done | bytes 196640 | tf_op jit(solution)/shard_map/gather_papers/ppermute | solution.py:21
  74.4 2.2 %collective-permute-done.13.refs_2_ = bf16[2,64,768]{2,1,0:T(8,128)(2,1)S(1)} collective-permute-done((bf16[2,64,768]{2,1,0:T(8,128)(2,1)S(1)}, bf16[2,64,768]{2,1,0:T(8,128)(2,1)S(1)}, u32[]{:S(2)}, u32[]{:S(2)}) %collective-permute-start.13) | collective-permute-done | bytes 196640 | tf_op jit(solution)/shard_map/gather_papers/ppermute | solution.py:21
  76.5 0.0 collective-permute-start.17
  76.5 2.0 %collective-permute-done.12.refs_1_ = bf16[2,64,768]{2,1,0:T(8,128)(2,1)S(1)} collective-permute-done((bf16[2,64,768]{2,1,0:T(8,128)(2,1)S(1)}, bf16[2,64,768]{2,1,0:T(8,128)(2,1)S(1)}, u32[]{:S(2)}, u32[]{:S(2)}) %collective-permute-start.12) | collective-permute-done | bytes 196640 | tf_op jit(solution)/shard_map/gather_papers/ppermute | solution.py:21
  78.6 0.0 collective-permute-start.16
  78.6 0.0 collective-permute-done.15.refs_4_
  78.6 0.0 collective-permute-done.18.refs_7_
  78.6 1.4 %collective-permute-done.16.refs_5_ = bf16[2,64,768]{2,1,0:T(8,128)(2,1)S(1)} collective-permute-done((bf16[2,64,768]{2,1,0:T(8,128)(2,1)S(1)}, bf16[2,64,768]{2,1,0:T(8,128)(2,1)S(1)}, u32[]{:S(2)}, u32[]{:S(2)}) %collective-permute-start.16) | collective-permute-done | bytes 196640 | tf_op jit(solution)/shard_map/gather_papers/ppermute | solution.py:25
  80.0 5.0 %shard_map.118 = (f32[4,64,768]{2,1,0:T(8,128)S(1)}, f32[4,64,768]{2,1,0:T(8,128)S(1)}, f32[4,64,768]{2,1,0:T(8,128)S(1)}, bf16[4,32,768]{2,1,0:T(8,128)(2,1)S(1)}, bf16[4,32,768]{2,1,0:T(8,128)(2,1)S(1)}) custom-call(s32[102]{0:T(128)S(1)} %concatenate.14.place, bf16[2,64,768]{2,1,0:T(8,128)(2,1)S(1)} %get-tuple-element.33.refs_0_, ...), custom_call_target="tpu_custom_call" | custom-call | flops 1000000000 | bytes 4194304 | tf_op jit(solution)/shard_map/pallas_call | solution.py:149
  85.0 0.1 collective-permute-start.19
  85.2 3.3 %collective-permute-start.21 = (bf16[4,32,768]{2,1,0:T(8,128)(2,1)S(1)}, bf16[4,32,768]{2,1,0:T(8,128)(2,1)S(1)}, u32[]{:S(2)}, u32[]{:S(2)}) collective-permute-start(bf16[4,32,768]{2,1,0:T(8,128)(2,1)S(1)} %get-tuple-element.39), channel_id=1, source_target_pairs={{0,192},{64,0},{128,64},{192,128},{1,193},{65,1},{129,65},{193,129... | collective-permute-start | bytes 589832 | tf_op jit(solution)/shard_map/sum_authors/ppermute | solution.py:21
  88.4 4.8 %collective-permute-done.19 = bf16[4,32,768]{2,1,0:T(8,128)(2,1)S(1)} collective-permute-done((bf16[4,32,768]{2,1,0:T(8,128)(2,1)S(1)}, bf16[4,32,768]{2,1,0:T(8,128)(2,1)S(1)}, u32[]{:S(2)}, u32[]{:S(2)}) %collective-permute-start.19) | collective-permute-done | bytes 196640 | tf_op jit(solution)/shard_map/sum_authors/ppermute | solution.py:21
  93.3 0.1 collective-permute-start.23
  93.5 3.3 %collective-permute-start.24 = (bf16[64,768]{1,0:T(8,128)(2,1)S(1)}, bf16[64,768]{1,0:T(8,128)(2,1)S(1)}, u32[]{:S(2)}, u32[]{:S(2)}) collective-permute-start(bf16[64,768]{1,0:T(8,128)(2,1)S(1)} %fusion.13), channel_id=1, source_target_pairs={{0,192},{64,0},{128,64},{192,128},{1,193},{65,1},{129,65},{193,129... | collective-permute-start | bytes 294920 | tf_op jit(solution)/shard_map/sum_authors/ppermute | solution.py:21
  96.8 0.3 collective-permute-start.22
  97.1 2.0 %collective-permute-start.20 = (bf16[3,64,768]{2,1,0:T(8,128)(2,1)S(1)}, bf16[3,64,768]{2,1,0:T(8,128)(2,1)S(1)}, u32[]{:S(2)}, u32[]{:S(2)}) collective-permute-start(bf16[3,64,768]{2,1,0:T(8,128)(2,1)S(1)} %fusion.4), channel_id=1, source_target_pairs={{0,64},{64,128},{128,192},{192,0},{1,65},{65,129},{129,193},{193,1... | collective-permute-start | bytes 884744 | tf_op jit(solution)/shard_map/sum_authors/ppermute | solution.py:21
  99.1 0.1 collective-permute-done.23
  99.2 0.8 collective-permute-done.24
  100.1 4.1 %collective-permute-start.25 = (bf16[64,768]{1,0:T(8,128)(2,1)S(1)}, bf16[64,768]{1,0:T(8,128)(2,1)S(1)}, u32[]{:S(2)}, u32[]{:S(2)}) collective-permute-start(bf16[64,768]{1,0:T(8,128)(2,1)S(1)} %fusion.12), channel_id=1, source_target_pairs={{0,32},{16,48},{32,0},{48,16},{1,33},{17,49},{33,1},{49,17},{2,34}... | collective-permute-start | bytes 294920 | tf_op jit(solution)/shard_map/sum_authors/ppermute | solution.py:21
  104.2 0.6 collective-permute-done.22
  104.8 1.3 %collective-permute-done.20 = bf16[3,64,768]{2,1,0:T(8,128)(2,1)S(1)} collective-permute-done((bf16[3,64,768]{2,1,0:T(8,128)(2,1)S(1)}, bf16[3,64,768]{2,1,0:T(8,128)(2,1)S(1)}, u32[]{:S(2)}, u32[]{:S(2)}) %collective-permute-start.20) | collective-permute-done | bytes 294944 | tf_op jit(solution)/shard_map/sum_authors/ppermute | solution.py:21
  106.1 0.1 fusion.16
  106.2 3.8 %collective-permute-start.26 = (bf16[64,768]{1,0:T(8,128)(2,1)S(1)}, bf16[64,768]{1,0:T(8,128)(2,1)S(1)}, u32[]{:S(2)}, u32[]{:S(2)}) collective-permute-start(bf16[64,768]{1,0:T(8,128)(2,1)S(1)} %get-tuple-element.47), channel_id=1, source_target_pairs={{0,16},{16,32},{32,48},{48,0},{1,17},{17,33},{33,49},{49,1},{2,18}... | collective-permute-start | bytes 294920 | tf_op jit(solution)/shard_map/sum_authors/ppermute | solution.py:21
  110.0 4.0 %collective-permute-done.26 = bf16[64,768]{1,0:T(8,128)(2,1)S(1)} collective-permute-done((bf16[64,768]{1,0:T(8,128)(2,1)S(1)}, bf16[64,768]{1,0:T(8,128)(2,1)S(1)}, u32[]{:S(2)}, u32[]{:S(2)}) %collective-permute-start.26) | collective-permute-done | bytes 98336 | tf_op jit(solution)/shard_map/sum_authors/ppermute | solution.py:21
  114.0 3.8 %collective-permute-done.27 = bf16[64,768]{1,0:T(8,128)(2,1)S(1)} collective-permute-done((bf16[64,768]{1,0:T(8,128)(2,1)S(1)}, bf16[64,768]{1,0:T(8,128)(2,1)S(1)}, u32[]{:S(2)}, u32[]{:S(2)}) %collective-permute-start.27) | collective-permute-done | bytes 98336 | tf_op jit(solution)/shard_map/sum_authors/ppermute | solution.py:21
  117.8 0.7 fusion.8
  (36 shorter events, 0.4 us)
Async XLA Ops:
  0.6 58.5 %copy-start = (bf16[768,768]{1,0:T(8,128)(2,1)S(1)}, bf16[768,768]{1,0:T(8,128)(2,1)}, u32[]{:S(2)}) copy-start(bf16[768,768]{1,0:T(8,128)(2,1)} %param.12) | copy-start | bytes 3538948
  0.6 15.3 %collective-permute-start.2 = (bf16[64,768]{1,0:T(8,128)(2,1)}, bf16[64,768]{1,0:T(8,128)(2,1)S(1)}, u32[]{:S(2)}, u32[]{:S(2)}) collective-permute-start(bf16[64,768]{1,0:T(8,128)(2,1)} %refs_0_.1), channel_id=1, source_target_pairs={{0,48},{16,0},{32,16},{48,32},{1,49},{17,1},{33,17},{49,33},{2,50}... | collective-permute-start | bytes 294920 | tf_op jit(solution)/shard_map/gather_authors/ppermute | solution.py:21
  2.1 13.9 %collective-permute-start.1 = (bf16[64,768]{1,0:T(8,128)(2,1)}, bf16[64,768]{1,0:T(8,128)(2,1)S(1)}, u32[]{:S(2)}, u32[]{:S(2)}) collective-permute-start(bf16[64,768]{1,0:T(8,128)(2,1)} %refs_0_.1), channel_id=1, source_target_pairs={{0,32},{16,48},{32,0},{48,16},{1,33},{17,49},{33,1},{49,17},{2,34}... | collective-permute-start | bytes 294920 | tf_op jit(solution)/shard_map/gather_authors/ppermute | solution.py:21
  7.6 8.4 %collective-permute-start = (bf16[64,768]{1,0:T(8,128)(2,1)}, bf16[64,768]{1,0:T(8,128)(2,1)S(1)}, u32[]{:S(2)}, u32[]{:S(2)}) collective-permute-start(bf16[64,768]{1,0:T(8,128)(2,1)} %refs_0_.1), channel_id=1, source_target_pairs={{0,16},{16,32},{32,48},{48,0},{1,17},{17,33},{33,49},{49,1},{2,18}... | collective-permute-start | bytes 294920 | tf_op jit(solution)/shard_map/gather_authors/ppermute | solution.py:21
  12.6 1.2 %copy-start.4 = (bf16[1,1,32,128,128]{4,3,2,1,0:T(8,128)(2,1)S(1)}, bf16[1,1,32,128,128]{4,3,2,1,0:T(8,128)(2,1)}, u32[]{:S(2)}) copy-start(bf16[1,1,32,128,128]{4,3,2,1,0:T(8,128)(2,1)} %param.19) | copy-start | bytes 3145732
  13.8 6.2 %copy-start.1 = (bf16[2,768,768]{2,1,0:T(8,128)(2,1)S(1)}, bf16[2,768,768]{2,1,0:T(8,128)(2,1)}, u32[]{:S(2)}) copy-start(bf16[2,768,768]{2,1,0:T(8,128)(2,1)} %refs_3_.3) | copy-start | bytes 7077892
  13.8 6.2 %copy-start.3 = (bf16[64,768]{1,0:T(8,128)(2,1)S(1)}, bf16[64,768]{1,0:T(8,128)(2,1)}, u32[]{:S(2)}) copy-start(bf16[64,768]{1,0:T(8,128)(2,1)} %refs_0_.1) | copy-start | bytes 294916
  16.0 11.5 %collective-permute-start.4 = (bf16[256,768]{1,0:T(8,128)(2,1)S(1)}, bf16[256,768]{1,0:T(8,128)(2,1)S(1)}, u32[]{:S(2)}, u32[]{:S(2)}) collective-permute-start(bf16[256,768]{1,0:T(8,128)(2,1)S(1)} %constant_dynamic-update-slice_fusion), channel_id=1, source_target_pairs={{0,192},{64,0},{128,64},{192,128},{1,193},{65,1},{129,65},{193,129... | collective-permute-start | bytes 1179656 | tf_op jit(solution)/shard_map/gather_authors/ppermute | solution.py:21
  20.1 10.9 %collective-permute-start.3 = (bf16[256,768]{1,0:T(8,128)(2,1)S(1)}, bf16[256,768]{1,0:T(8,128)(2,1)S(1)}, u32[]{:S(2)}, u32[]{:S(2)}) collective-permute-start(bf16[256,768]{1,0:T(8,128)(2,1)S(1)} %constant_dynamic-update-slice_fusion), channel_id=1, source_target_pairs={{0,64},{64,128},{128,192},{192,0},{1,65},{65,129},{129,193},{193,1... | collective-permute-start | bytes 1179656 | tf_op jit(solution)/shard_map/gather_authors/ppermute | solution.py:21
  31.0 8.5 %collective-permute-start.5 = (bf16[128,768]{1,0:T(8,128)(2,1)S(1)}, bf16[128,768]{1,0:T(8,128)(2,1)S(1)}, u32[]{:S(2)}, u32[]{:S(2)}) collective-permute-start(bf16[128,768]{1,0:T(8,128)(2,1)S(1)} %slice.70), channel_id=1, source_target_pairs={{0,64},{64,128},{128,192},{192,0},{1,65},{65,129},{129,193},{193,1... | collective-permute-start | bytes 589832 | tf_op jit(solution)/shard_map/forward_authors/ppermute | solution.py:21
  31.1 8.4 %collective-permute-start.6 = (bf16[128,768]{1,0:T(8,128)(2,1)S(1)}, bf16[128,768]{1,0:T(8,128)(2,1)S(1)}, u32[]{:S(2)}, u32[]{:S(2)}) collective-permute-start(bf16[128,768]{1,0:T(8,128)(2,1)S(1)} %slice.71), channel_id=1, source_target_pairs={{0,192},{64,0},{128,64},{192,128},{1,193},{65,1},{129,65},{193,129... | collective-permute-start | bytes 589832 | tf_op jit(solution)/shard_map/forward_authors/ppermute | solution.py:21
  42.6 2.4 %collective-permute-start.7 = (bf16[4,2,64,768]{3,2,1,0:T(8,128)(2,1)S(1)}, bf16[4,2,64,768]{3,2,1,0:T(8,128)(2,1)S(1)}, u32[]{:S(2)}, u32[]{:S(2)}) collective-permute-start(bf16[4,2,64,768]{3,2,1,0:T(8,128)(2,1)S(1)} %get-tuple-element.31), channel_id=1, source_target_pairs={{0,1},{1,0},{2,3},{3,2},{4,5},{5,4},{6,7},{7,6},{8,9},{9,8},{10,11... | collective-permute-start | bytes 2359304 | tf_op jit(solution)/shard_map/sum_papers/ppermute | solution.py:25
  45.2 13.9 %copy-start.5 = (bf16[64,768]{1,0:T(8,128)(2,1)S(1)}, bf16[64,768]{1,0:T(8,128)(2,1)}, u32[]{:S(2)}) copy-start(bf16[64,768]{1,0:T(8,128)(2,1)} %param.10) | copy-start | bytes 294916
  45.3 8.4 %collective-permute-start.8 = (bf16[2,64,768]{2,1,0:T(8,128)(2,1)S(1)}, bf16[2,64,768]{2,1,0:T(8,128)(2,1)S(1)}, u32[]{:S(2)}, u32[]{:S(2)}) collective-permute-start(bf16[2,64,768]{2,1,0:T(8,128)(2,1)S(1)} %get-tuple-element.44), channel_id=1, source_target_pairs={{0,4},{4,8},{8,12},{12,0},{1,5},{5,9},{9,13},{13,1},{2,6},{6,10},{... | collective-permute-start | bytes 589832 | tf_op jit(solution)/shard_map/sum_papers/ppermute | solution.py:21
  47.1 7.8 %collective-permute-start.10 = (bf16[2,64,768]{2,1,0:T(8,128)(2,1)S(1)}, bf16[2,64,768]{2,1,0:T(8,128)(2,1)S(1)}, u32[]{:S(2)}, u32[]{:S(2)}) collective-permute-start(bf16[2,64,768]{2,1,0:T(8,128)(2,1)S(1)} %get-tuple-element.45), channel_id=1, source_target_pairs={{0,12},{4,0},{8,4},{12,8},{1,13},{5,1},{9,5},{13,9},{2,14},{6,2},{... | collective-permute-start | bytes 589832 | tf_op jit(solution)/shard_map/sum_papers/ppermute | solution.py:21
  48.8 10.3 %collective-permute-start.9 = (bf16[2,64,768]{2,1,0:T(8,128)(2,1)S(1)}, bf16[2,64,768]{2,1,0:T(8,128)(2,1)S(1)}, u32[]{:S(2)}, u32[]{:S(2)}) collective-permute-start(bf16[2,64,768]{2,1,0:T(8,128)(2,1)S(1)} %get-tuple-element.46), channel_id=1, source_target_pairs={{0,8},{4,12},{8,0},{12,4},{1,9},{5,13},{9,1},{13,5},{2,10},{6,14},... | collective-permute-start | bytes 589832 | tf_op jit(solution)/shard_map/sum_papers/ppermute | solution.py:21
  59.2 6.8 %copy-start.2 = (bf16[768,768]{1,0:T(8,128)(2,1)S(1)}, bf16[768,768]{1,0:T(8,128)(2,1)}, u32[]{:S(2)}) copy-start(bf16[768,768]{1,0:T(8,128)(2,1)} %w_ref.1) | copy-start | bytes 3538948
  59.5 6.4 %collective-permute-start.11 = (bf16[2,64,768]{2,1,0:T(8,128)(2,1)S(1)}, bf16[2,64,768]{2,1,0:T(8,128)(2,1)S(1)}, u32[]{:S(2)}, u32[]{:S(2)}) collective-permute-start(bf16[2,64,768]{2,1,0:T(8,128)(2,1)S(1)} %fusion.15), channel_id=1, source_target_pairs={{0,2},{2,0},{1,3},{3,1},{4,6},{6,4},{5,7},{7,5},{8,10},{10,8},{9,1... | collective-permute-start | bytes 589832 | tf_op jit(solution)/shard_map/sum_papers/ppermute | solution.py:25
  66.8 7.6 %collective-permute-start.14 = (bf16[2,64,768]{2,1,0:T(8,128)(2,1)S(1)}, bf16[2,64,768]{2,1,0:T(8,128)(2,1)S(1)}, u32[]{:S(2)}, u32[]{:S(2)}) collective-permute-start(bf16[2,64,768]{2,1,0:T(8,128)(2,1)S(1)} %get-tuple-element.33.refs_0_), channel_id=1, source_target_pairs={{0,12},{4,0},{8,4},{12,8},{1,13},{5,1},{9,5},{13,9},{2,14},{6,2},{... | collective-permute-start | bytes 589832 | tf_op jit(solution)/shard_map/gather_papers/ppermute | solution.py:21
  68.2 8.3 %collective-permute-start.13 = (bf16[2,64,768]{2,1,0:T(8,128)(2,1)S(1)}, bf16[2,64,768]{2,1,0:T(8,128)(2,1)S(1)}, u32[]{:S(2)}, u32[]{:S(2)}) collective-permute-start(bf16[2,64,768]{2,1,0:T(8,128)(2,1)S(1)} %get-tuple-element.33.refs_0_), channel_id=1, source_target_pairs={{0,8},{4,12},{8,0},{12,4},{1,9},{5,13},{9,1},{13,5},{2,10},{6,14},... | collective-permute-start | bytes 589832 | tf_op jit(solution)/shard_map/gather_papers/ppermute | solution.py:21
  69.7 8.9 %collective-permute-start.12 = (bf16[2,64,768]{2,1,0:T(8,128)(2,1)S(1)}, bf16[2,64,768]{2,1,0:T(8,128)(2,1)S(1)}, u32[]{:S(2)}, u32[]{:S(2)}) collective-permute-start(bf16[2,64,768]{2,1,0:T(8,128)(2,1)S(1)} %get-tuple-element.33.refs_0_), channel_id=1, source_target_pairs={{0,4},{4,8},{8,12},{12,0},{1,5},{5,9},{9,13},{13,1},{2,6},{6,10},{... | collective-permute-start | bytes 589832 | tf_op jit(solution)/shard_map/gather_papers/ppermute | solution.py:21
  69.7 8.9 %collective-permute-start.15 = (bf16[2,64,768]{2,1,0:T(8,128)(2,1)S(1)}, bf16[2,64,768]{2,1,0:T(8,128)(2,1)S(1)}, u32[]{:S(2)}, u32[]{:S(2)}) collective-permute-start(bf16[2,64,768]{2,1,0:T(8,128)(2,1)S(1)} %get-tuple-element.33.refs_0_), channel_id=1, source_target_pairs={{0,1},{1,0},{2,3},{3,2},{4,5},{5,4},{6,7},{7,6},{8,9},{9,8},{10,11... | collective-permute-start | bytes 589832 | tf_op jit(solution)/shard_map/gather_papers/ppermute | solution.py:25
  74.4 4.2 %collective-permute-start.18 = (bf16[2,64,768]{2,1,0:T(8,128)(2,1)S(1)}, bf16[2,64,768]{2,1,0:T(8,128)(2,1)S(1)}, u32[]{:S(2)}, u32[]{:S(2)}) collective-permute-start(bf16[2,64,768]{2,1,0:T(8,128)(2,1)S(1)} %collective-permute-done.14.refs_3_), channel_id=1, source_target_pairs={{0,1},{1,0},{2,3},{3,2},{4,5},{5,4},{6,7},{7,6},{8,9},{9,8},{10,11... | collective-permute-start | bytes 589832 | tf_op jit(solution)/shard_map/gather_papers/ppermute | solution.py:25
  76.5 2.1 %collective-permute-start.17 = (bf16[2,64,768]{2,1,0:T(8,128)(2,1)S(1)}, bf16[2,64,768]{2,1,0:T(8,128)(2,1)S(1)}, u32[]{:S(2)}, u32[]{:S(2)}) collective-permute-start(bf16[2,64,768]{2,1,0:T(8,128)(2,1)S(1)} %collective-permute-done.13.refs_2_), channel_id=1, source_target_pairs={{0,1},{1,0},{2,3},{3,2},{4,5},{5,4},{6,7},{7,6},{8,9},{9,8},{10,11... | collective-permute-start | bytes 589832 | tf_op jit(solution)/shard_map/gather_papers/ppermute | solution.py:25
  78.6 1.4 %collective-permute-start.16 = (bf16[2,64,768]{2,1,0:T(8,128)(2,1)S(1)}, bf16[2,64,768]{2,1,0:T(8,128)(2,1)S(1)}, u32[]{:S(2)}, u32[]{:S(2)}) collective-permute-start(bf16[2,64,768]{2,1,0:T(8,128)(2,1)S(1)} %collective-permute-done.12.refs_1_), channel_id=1, source_target_pairs={{0,1},{1,0},{2,3},{3,2},{4,5},{5,4},{6,7},{7,6},{8,9},{9,8},{10,11... | collective-permute-start | bytes 589832 | tf_op jit(solution)/shard_map/gather_papers/ppermute | solution.py:25
  85.0 8.2 %collective-permute-start.19 = (bf16[4,32,768]{2,1,0:T(8,128)(2,1)S(1)}, bf16[4,32,768]{2,1,0:T(8,128)(2,1)S(1)}, u32[]{:S(2)}, u32[]{:S(2)}) collective-permute-start(bf16[4,32,768]{2,1,0:T(8,128)(2,1)S(1)} %get-tuple-element.37), channel_id=1, source_target_pairs={{0,64},{64,128},{128,192},{192,0},{1,65},{65,129},{129,193},{193,1... | collective-permute-start | bytes 589832 | tf_op jit(solution)/shard_map/sum_authors/ppermute | solution.py:21
  85.2 8.3 %collective-permute-start.21 = (bf16[4,32,768]{2,1,0:T(8,128)(2,1)S(1)}, bf16[4,32,768]{2,1,0:T(8,128)(2,1)S(1)}, u32[]{:S(2)}, u32[]{:S(2)}) collective-permute-start(bf16[4,32,768]{2,1,0:T(8,128)(2,1)S(1)} %get-tuple-element.39), channel_id=1, source_target_pairs={{0,192},{64,0},{128,64},{192,128},{1,193},{65,1},{129,65},{193,129... | collective-permute-start | bytes 589832 | tf_op jit(solution)/shard_map/sum_authors/ppermute | solution.py:21
  93.3 5.9 %collective-permute-start.23 = (bf16[64,768]{1,0:T(8,128)(2,1)S(1)}, bf16[64,768]{1,0:T(8,128)(2,1)S(1)}, u32[]{:S(2)}, u32[]{:S(2)}) collective-permute-start(bf16[64,768]{1,0:T(8,128)(2,1)S(1)} %fusion.14), channel_id=1, source_target_pairs={{0,64},{64,128},{128,192},{192,0},{1,65},{65,129},{129,193},{193,1... | collective-permute-start | bytes 294920 | tf_op jit(solution)/shard_map/sum_authors/ppermute | solution.py:21
  93.5 6.5 %collective-permute-start.24 = (bf16[64,768]{1,0:T(8,128)(2,1)S(1)}, bf16[64,768]{1,0:T(8,128)(2,1)S(1)}, u32[]{:S(2)}, u32[]{:S(2)}) collective-permute-start(bf16[64,768]{1,0:T(8,128)(2,1)S(1)} %fusion.13), channel_id=1, source_target_pairs={{0,192},{64,0},{128,64},{192,128},{1,193},{65,1},{129,65},{193,129... | collective-permute-start | bytes 294920 | tf_op jit(solution)/shard_map/sum_authors/ppermute | solution.py:21
  96.8 8.0 %collective-permute-start.22 = (bf16[3,64,768]{2,1,0:T(8,128)(2,1)S(1)}, bf16[3,64,768]{2,1,0:T(8,128)(2,1)S(1)}, u32[]{:S(2)}, u32[]{:S(2)}) collective-permute-start(bf16[3,64,768]{2,1,0:T(8,128)(2,1)S(1)} %fusion.3), channel_id=1, source_target_pairs={{0,192},{64,0},{128,64},{192,128},{1,193},{65,1},{129,65},{193,129... | collective-permute-start | bytes 884744 | tf_op jit(solution)/shard_map/sum_authors/ppermute | solution.py:21
  97.1 8.9 %collective-permute-start.20 = (bf16[3,64,768]{2,1,0:T(8,128)(2,1)S(1)}, bf16[3,64,768]{2,1,0:T(8,128)(2,1)S(1)}, u32[]{:S(2)}, u32[]{:S(2)}) collective-permute-start(bf16[3,64,768]{2,1,0:T(8,128)(2,1)S(1)} %fusion.4), channel_id=1, source_target_pairs={{0,64},{64,128},{128,192},{192,0},{1,65},{65,129},{129,193},{193,1... | collective-permute-start | bytes 884744 | tf_op jit(solution)/shard_map/sum_authors/ppermute | solution.py:21
  100.1 9.9 %collective-permute-start.25 = (bf16[64,768]{1,0:T(8,128)(2,1)S(1)}, bf16[64,768]{1,0:T(8,128)(2,1)S(1)}, u32[]{:S(2)}, u32[]{:S(2)}) collective-permute-start(bf16[64,768]{1,0:T(8,128)(2,1)S(1)} %fusion.12), channel_id=1, source_target_pairs={{0,32},{16,48},{32,0},{48,16},{1,33},{17,49},{33,1},{49,17},{2,34}... | collective-permute-start | bytes 294920 | tf_op jit(solution)/shard_map/sum_authors/ppermute | solution.py:21
  106.2 7.8 %collective-permute-start.26 = (bf16[64,768]{1,0:T(8,128)(2,1)S(1)}, bf16[64,768]{1,0:T(8,128)(2,1)S(1)}, u32[]{:S(2)}, u32[]{:S(2)}) collective-permute-start(bf16[64,768]{1,0:T(8,128)(2,1)S(1)} %get-tuple-element.47), channel_id=1, source_target_pairs={{0,16},{16,32},{32,48},{48,0},{1,17},{17,33},{33,49},{49,1},{2,18}... | collective-permute-start | bytes 294920 | tf_op jit(solution)/shard_map/sum_authors/ppermute | solution.py:21
  110.0 7.8 %collective-permute-start.27 = (bf16[64,768]{1,0:T(8,128)(2,1)S(1)}, bf16[64,768]{1,0:T(8,128)(2,1)S(1)}, u32[]{:S(2)}, u32[]{:S(2)}) collective-permute-start(bf16[64,768]{1,0:T(8,128)(2,1)S(1)} %get-tuple-element.48), channel_id=1, source_target_pairs={{0,48},{16,0},{32,16},{48,32},{1,49},{17,1},{33,17},{49,33},{2,50}... | collective-permute-start | bytes 294920 | tf_op jit(solution)/shard_map/sum_authors/ppermute | solution.py:21

commit v4 on v3

v4 whole, which is shorter than its diff:
```python
import functools

import jax
import jax.numpy as jnp
from jax import lax
from jax.experimental import pallas as pl
from jax.experimental.pallas import tpu as pltpu
from jax.sharding import Mesh
from jax.sharding import PartitionSpec as P

PROW = ("y", "zh")
PCOL = ("x", "zl", "core")
F32 = jnp.float32
BF16 = jnp.bfloat16
VMEM_LIMIT = 24 * 2**20
PLACE = 5
RING = 4


def shift(value, axis, by):
    return lax.ppermute(value, axis, [(i, (i + by) % RING) for i in range(RING)])


def swap(value, axis):
    return lax.ppermute(value, axis, [(0, 1), (1, 0)])


def behind(at, by):
    return lax.rem(at + (RING - by), RING)


def build_tiles(place, vals, one_ref, two_ref):
    y, zh, x, zl, core = (place[i] for i in range(PLACE))
    slots, side = vals.shape[:2]
    half = side // 2
    span = RING * half
    relations = one_ref.shape[1] // two_ref.shape[1]
    one_ref[...] = jnp.zeros_like(one_ref)
    two_ref[...] = jnp.zeros_like(two_ref)

    def slot(k, carry):
        row, col, kind = (place[PLACE + 1 + i * slots + k] for i in range(3))
        block = [vals[k, pl.ds(pl.multiple_of(c * half, half), half), :] for c in (core, 1 - core)]
        turned = jnp.concatenate(block).T
        d = lax.rem(y + RING - lax.div(col, 2), RING)
        group = jnp.where(d == 2, 3, jnp.where(d == 3, 2, d))
        at = (group * relations + kind) * span + lax.rem(col, 2) * side
        lanes = pl.ds(pl.multiple_of(at, side), side)
        d = lax.rem(lax.div(row, 2) + RING - x, RING)
        e = jnp.where(lax.rem(row, 2) == zl, 0, 1)
        for c in range(2):
            at = (c * RING + d) * side + e * half
            one_ref[pl.ds(pl.multiple_of(at, half), half), lanes] = block[c]
        d = lax.rem(x + RING - lax.div(row, 2), RING)
        lanes = pl.ds(pl.multiple_of((d * 2 + e) * side, side), side)
        d = lax.rem(lax.div(col, 2) + RING - y, RING)
        for c in range(2):
            e = lax.rem(lax.rem(col, 2) * 2 + c + RING - zh, RING)
            place_of = jnp.where(e == 2, 0, jnp.where(e == 3, 3, e + 1))
            at = d * span + place_of * half
            two_ref[pl.ds(pl.multiple_of(at, half), half), lanes] = turned[c * half : (c + 1) * half]
        return carry

    lax.fori_loop(0, place[PLACE], slot, 0)


def add_product(step, first, tile_ref, msgs_ref, base_ref):
    span = tile_ref.shape[0] // RING
    at = slice(step * span, (step + 1) * span)
    made = jnp.dot(tile_ref[at, first : first + msgs_ref.shape[0]], msgs_ref[...], preferred_element_type=F32)
    return made if base_ref is None else made + base_ref[at, :]


def add_part(first, split, has_base, is_last, place, *refs):
    tile_ref, w_ref, refs = refs[0], refs[1], refs[2:]
    base_ref, refs = (refs[0], refs[1:]) if has_base else (None, refs)
    pieces, (out_ref, msgs, table) = refs[: len(split)], refs[len(split) :]
    relations = w_ref.shape[0]
    span = tile_ref.shape[0] // RING
    own = span // RING
    for piece, chunks in zip(pieces, split, strict=True):
        for i, (group, e) in enumerate(chunks):
            at = pl.multiple_of((group * RING + behind(place[1], e)) * own, own)
            table[pl.ds(at, own), :] = piece[i * own : (i + 1) * own, :]
    for r in range(relations):
        made = jnp.dot(table[...], w_ref[r], preferred_element_type=F32).astype(BF16)
        for i in range(table.shape[0] // span):
            at = (i * relations + r) * span
            msgs[at : at + span, :] = made[i * span : (i + 1) * span]
    skip = first * relations * span
    if is_last:
        for step in range(2):
            made = add_product(2 + step, skip, tile_ref, msgs, base_ref)
            out_ref[2 * step : 2 * step + 2] = made.reshape(2, *out_ref.shape[1:]).astype(BF16)
    else:
        for step in range(RING):
            out_ref[step * span : (step + 1) * span, :] = add_product(step, skip, tile_ref, msgs, base_ref)


def keep_part(msgs_ref, tile_ref, base_ref, out_ref):
    skip = tile_ref.shape[1] - msgs_ref.shape[0]
    for step in range(2):
        made = add_product(step, skip, tile_ref, msgs_ref, base_ref)
        out_ref[2 * step : 2 * step + 2] = made.reshape(2, *out_ref.shape[1:])


def hop_two(*refs):
    mine, other, refs = refs[:4], refs[4:8], refs[8:]
    tile_ref, same_ref, up_ref, down_ref, two_up_ref, two_down_ref, table = refs
    own, width = same_ref.shape[1:]
    span = RING * own
    for d in range(RING):
        for e in range(2):
            at = (d * 2 + e) * 2 * own
            table[at : at + own, :] = mine[d][e]
            table[at + own : at + 2 * own, :] = other[d][e]
    for d in range(RING):
        made = jnp.dot(tile_ref[d * span : (d + 1) * span, :], table[...], preferred_element_type=F32)
        made = made.reshape(RING, own, width)
        if d == 2:
            two_up_ref[...] = made[:, : own // 2].astype(BF16)
            two_down_ref[...] = made[:, own // 2 :].astype(BF16)
        else:
            out = (same_ref, up_ref, None, down_ref)[d]
            out[...] = made


def hidden_step(base_ref, got_ref, w_ref, hidden_ref, out_ref):
    first = jnp.maximum(base_ref[0] + got_ref[1].astype(F32), 0.0).astype(BF16)
    second = jnp.maximum(base_ref[1] + got_ref[0].astype(F32), 0.0).astype(BF16)
    hidden_ref[...] = first
    both = jnp.concatenate([first, second])
    out_ref[...] = jnp.dot(both, w_ref[...], preferred_element_type=F32).astype(BF16).reshape(out_ref.shape)


def call(kernel, flops, scalars, arrays, out_shape, scratch):
    def spec(kind):
        return pl.BlockSpec(memory_space=kind)

    return pl.pallas_call(
        kernel,
        out_shape=out_shape,
        in_specs=[spec(pltpu.SMEM)] * len(scalars) + [spec(pltpu.VMEM)] * len(arrays),
        out_specs=jax.tree.map(lambda _: spec(pltpu.VMEM), out_shape),
        scratch_shapes=scratch,
        compiler_params=pltpu.CompilerParams(vmem_limit_bytes=VMEM_LIMIT),
        cost_estimate=pl.CostEstimate(flops=flops, bytes_accessed=4 * 2**20, transcendentals=0),
    )(*scalars, *arrays)


def total_of(parts):
    return sum(p.astype(F32) for p in parts)


def per_device(paper_x, author_x, w_self, w_rel, w_two, block_rows, block_cols, block_type, block_count, block_vals):
    slots = block_rows.shape[2]
    side = block_vals.shape[3]
    own, width = paper_x.shape
    vals = block_vals.reshape(slots, side, side)
    at = jnp.stack([lax.axis_index(a).astype(jnp.int32) for a in (*PROW, *PCOL)])
    place = jnp.concatenate([at, *(a.reshape(-1) for a in (block_count, block_rows, block_cols, block_type))])
    tile_rows = 16 * own

    def shaped(*dims, dtype=BF16):
        return jax.ShapeDtypeStruct((*dims, own, width), dtype)

    relations = w_rel.shape[0]
    tile_one, tile_two = call(
        build_tiles,
        10**9,
        (place,),
        (vals,),
        (
            jax.ShapeDtypeStruct((tile_rows, relations * tile_rows), BF16),
            jax.ShapeDtypeStruct((tile_rows, tile_rows), BF16),
        ),
        [],
    )
    self_term = jnp.dot(paper_x, w_self, preferred_element_type=F32)
    span = RING * own

    def part(first, groups, split, pieces, base, out_shape):
        is_last = first + groups == RING
        rows = groups * relations * span
        table = pltpu.VMEM((groups * span, width), BF16)
        return call(
            functools.partial(add_part, first, split, base is not None, is_last),
            10**9,
            (place,),
            (tile_one, w_rel, *pieces) if base is None else (tile_one, w_rel, base, *pieces),
            (out_shape, jax.ShapeDtypeStruct((rows, width), BF16)) if is_last else out_shape,
            [table] if is_last else [pltpu.VMEM((rows, width), BF16), table],
        )

    base_shape = jax.ShapeDtypeStruct((tile_rows, width), F32)
    with jax.named_scope("gather_authors"):
        by_z = [shift(author_x, "zh", e) for e in range(1, RING)]
        by_z, tile_one, tile_two = lax.optimization_barrier((by_z, tile_one, tile_two))
        own_up, own_down = shift(author_x, "y", 1), shift(author_x, "y", RING - 1)
        by_z, own_up, own_down = lax.optimization_barrier((by_z, own_up, own_down))
        relay = jnp.concatenate(by_z)
        ups, downs = shift(relay, "y", 1), shift(relay, "y", RING - 1)
    base = part(0, 1, [[(0, e)] for e in range(RING)], (author_x, *by_z), None, base_shape)
    with jax.named_scope("forward_authors"):
        ups, downs, base, self_term = lax.optimization_barrier((ups, downs, base, self_term))
        up_two = shift(jnp.concatenate([own_up, ups[:own]]), "y", 1)
        down_two = shift(downs[own:], "y", RING - 1)
    split = [es for g in range(2) for es in ([(g, 0)], [(g, e) for e in range(1, RING)])]
    base = part(1, 2, split, (own_up, ups, own_down, downs), base, base_shape)
    send, msgs = part(
        3,
        1,
        [[(0, 0), (0, 1)], [(0, 2), (0, 3)]],
        (up_two, down_two),
        base,
        shaped(RING, 2),
    )
    keep = call(keep_part, 10**9, (), (msgs, tile_one, base), shaped(RING, 2, dtype=F32), [])
    with jax.named_scope("sum_papers"):
        pair = keep + swap(send, "core").astype(F32)
        by_x = [shift(pair[d].astype(BF16), "x", d) for d in range(1, RING)]
        both = total_of([pair[0], *by_x])
        both = jnp.stack([both[0] + self_term, both[1]])
        got = swap(both.astype(BF16), "zl")
    paper_hidden, outgoing = call(
        hidden_step, 4 * own * width * width, (), (both, got, w_two), (shaped(), shaped(2)), []
    )
    with jax.named_scope("gather_papers"):
        mine = [outgoing, *(shift(outgoing, "x", d) for d in range(1, RING))]
        other = [swap(m, "core") for m in mine]
    whole = shaped(RING, dtype=F32)
    piece = jax.ShapeDtypeStruct((RING, own // 2, width), BF16)
    same, up, down, two_up, two_down = call(
        hop_two,
        10**9,
        (),
        (*mine, *other, tile_two),
        (whole, whole, whole, piece, piece),
        [pltpu.VMEM((tile_rows, width), BF16)],
    )
    with jax.named_scope("sum_authors"):
        half = own // 2
        from_down = shift(two_up, "y", 1).astype(F32)
        from_up = shift(two_down, "y", RING - 1).astype(F32)
        up = jnp.concatenate([up[:, :half] + from_down, up[:, half:]], axis=1).astype(BF16)
        down = jnp.concatenate([down[:, :half], down[:, half:] + from_up], axis=1).astype(BF16)
        opposite = total_of([same[0], shift(up[0], "y", 1), shift(down[0], "y", RING - 1)])
        rest = total_of([same[1:], shift(up[1:], "y", 1), shift(down[1:], "y", RING - 1)])
        by_z = [
            shift(opposite.astype(BF16), "zh", 2),
            shift(rest[1].astype(BF16), "zh", 1),
            shift(rest[2].astype(BF16), "zh", RING - 1),
        ]
        author_out = total_of([rest[0], *by_z]).astype(BF16)
    return paper_hidden, author_out


def solution(mesh):
    split = Mesh(mesh.devices.reshape(4, 4, 4, 2, 2), (*PROW, *PCOL))
    tile = P(PROW, PCOL)
    return jax.shard_map(
        per_device,
        mesh=split,
        in_specs=(P((*PROW, *PCOL)), P((*PCOL, *PROW)), P(), P(), P(), tile, tile, tile, tile, tile),
        out_specs=(P((*PROW, *PCOL)), P((*PCOL, *PROW))),
        check_vma=False,
    )
```

time: 119 us -> 110 us (0.924)
  Pallas kernels: 19.2 us -> 14.1 us
  waiting for transfers between devices: 49.1 us -> 45.7 us
    pallas_call x6 -> x7, Pallas kernels: 19.2 us -> 14.1 us  [call(): pl.pallas_call(kernel, out_shape=out_shape, in_specs=[spec(pltpu.SMEM)] *...]
    ppermute x22 -> x24, waiting for transfers between devices: 41 us -> 38.3 us  [shift(): lax.ppermute(value, axis, [(i, (i + by) % RING) for i in range(RING)])]
    ppermute x22 -> x24, starting transfers between devices: 41.6 us -> 42.7 us  [shift(): lax.ppermute(value, axis, [(i, (i + by) % RING) for i in range(RING)])]
  transfers between devices with their start and end apart: 28 -> 30, of which waited for: 18 -> 18; matrix products, arithmetic and copies ran while one was open for 2% -> 1% of each run, Pallas kernels for 9% -> 9%
where the time goes in v4:
time: 110 us
  waiting for transfers between devices  45.7 us (42%)
  starting transfers between devices  44.8 us (41%)
  Pallas kernels  14.1 us (13%)
  local copies, waits for them, and re-layouts  2.19 us (2%)
  between operations  1.63 us (1%)
  other arithmetic  1.37 us (1%)
    ppermute x24, starting transfers between devices, shift(): lax.ppermute(value, axis, [(i, (i + by) % RING) for i in range(RING)])  42.7 us
    ppermute x24, waiting for transfers between devices, shift(): lax.ppermute(value, axis, [(i, (i + by) % RING) for i in range(RING)])  38.3 us
    pallas_call x7, Pallas kernels, call(): pl.pallas_call(kernel, out_shape=out_shape, in_specs=[spec(pltpu.SMEM)] *...  14.1 us
    ppermute x6, waiting for transfers between devices, swap(): return lax.ppermute(value, axis, [(0, 1), (1, 0)])  7.46 us
  transfers between devices with their start and end apart: 30, of which 18 were waited for; matrix products, arithmetic and copies ran while one was open for 1% of the time, Pallas kernels for 9%

profile of v4, /device:TPU:64, one launch (start us, length us, event | category | flops | bytes accessed | tf_op | source)
XLA Modules:
  0.0 110.1 jit_solution(11266198934430630849)
XLA Ops:
  0.6 0.0 copy-start
  0.6 1.5 %collective-permute-start.2 = (bf16[64,768]{1,0:T(8,128)(2,1)}, bf16[64,768]{1,0:T(8,128)(2,1)S(1)}, u32[]{:S(2)}, u32[]{:S(2)}) collective-permute-start(bf16[64,768]{1,0:T(8,128)(2,1)} %refs_2_.1), channel_id=1, source_target_pairs={{0,48},{16,0},{32,16},{48,32},{1,49},{17,1},{33,17},{49,33},{2,50}... | collective-permute-start | bytes 294920 | tf_op jit(solution)/shard_map/gather_authors/ppermute | solution.py:21
  2.1 5.5 %collective-permute-start.1 = (bf16[64,768]{1,0:T(8,128)(2,1)}, bf16[64,768]{1,0:T(8,128)(2,1)S(1)}, u32[]{:S(2)}, u32[]{:S(2)}) collective-permute-start(bf16[64,768]{1,0:T(8,128)(2,1)} %refs_2_.1), channel_id=1, source_target_pairs={{0,32},{16,48},{32,0},{48,16},{1,33},{17,49},{33,1},{49,17},{2,34}... | collective-permute-start | bytes 294920 | tf_op jit(solution)/shard_map/gather_authors/ppermute | solution.py:21
  7.6 2.7 %collective-permute-start = (bf16[64,768]{1,0:T(8,128)(2,1)}, bf16[64,768]{1,0:T(8,128)(2,1)S(1)}, u32[]{:S(2)}, u32[]{:S(2)}) collective-permute-start(bf16[64,768]{1,0:T(8,128)(2,1)} %refs_2_.1), channel_id=1, source_target_pairs={{0,16},{16,32},{32,48},{48,0},{1,17},{17,33},{33,49},{49,1},{2,18}... | collective-permute-start | bytes 294920 | tf_op jit(solution)/shard_map/gather_authors/ppermute | solution.py:21
  10.3 1.6 %collective-permute-start.3 = (bf16[64,768]{1,0:T(8,128)(2,1)}, bf16[64,768]{1,0:T(8,128)(2,1)S(1)}, u32[]{:S(2)}, u32[]{:S(2)}) collective-permute-start(bf16[64,768]{1,0:T(8,128)(2,1)} %refs_2_.1), channel_id=1, source_target_pairs={{0,64},{64,128},{128,192},{192,0},{1,65},{65,129},{129,193},{193,1... | collective-permute-start | bytes 294920 | tf_op jit(solution)/shard_map/gather_authors/ppermute | solution.py:21
  11.8 1.7 %collective-permute-start.4 = (bf16[64,768]{1,0:T(8,128)(2,1)}, bf16[64,768]{1,0:T(8,128)(2,1)S(1)}, u32[]{:S(2)}, u32[]{:S(2)}) collective-permute-start(bf16[64,768]{1,0:T(8,128)(2,1)} %refs_2_.1), channel_id=1, source_target_pairs={{0,192},{64,0},{128,64},{192,128},{1,193},{65,1},{129,65},{193,129... | collective-permute-start | bytes 294920 | tf_op jit(solution)/shard_map/gather_authors/ppermute | solution.py:21
  14.1 0.8 concatenate.17.place
  14.9 1.2 %copy-done.4 = bf16[1,1,32,128,128]{4,3,2,1,0:T(8,128)(2,1)S(1)} copy-done((bf16[1,1,32,128,128]{4,3,2,1,0:T(8,128)(2,1)S(1)}, bf16[1,1,32,128,128]{4,3,2,1,0:T(8,128)(2,1)}, u32[]{:S(2)}) %copy-start.4) | copy-done | bytes 1048600
  16.1 3.3 %shard_map.113 = (bf16[1024,2048]{1,0:T(8,128)(2,1)S(1)}, bf16[1024,1024]{1,0:T(8,128)(2,1)S(1)}) custom-call(s32[102]{0:T(128)S(1)} %concatenate.17.place, bf16[32,128,128]{2,1,0:T(8,128)(2,1)S(1)} %bitcast.59), custom_call_target="tpu_custom_call" | custom-call | flops 1000000000 | bytes 4194304 | tf_op jit(solution)/shard_map/pallas_call | solution.py:140
  19.4 0.0 copy-start.3
  19.4 0.0 collective-permute-done.2.refs_5_
  19.5 0.0 collective-permute-done.refs_3_
  19.5 0.0 collective-permute-done.3.refs_3_
  19.5 1.0 collective-permute-start.6
  20.6 1.1 collective-permute-start.5
  21.7 0.3 fusion.18
  22.0 0.0 copy-done.1
  22.0 2.2 %shard_map.114.refs_2_ = f32[1024,768]{1,0:T(8,128)S(1)} custom-call(s32[102]{0:T(128)S(1)} %concatenate.17.place, bf16[1024,2048]{1,0:T(8,128)(2,1)S(1)} %get-tuple-element.29.refs_0_.tile_ref, bf16[2,768,768]{2,1,0:T(8,128)(2,1)S(1)} %copy-done.1, bf16[64,768]{1,0:T(8,128)(2,1)S(1)} %copy-done.3, bf16[64,768]{1,0:T(8,128)(2,1)S(1)} %collective-permute-done.refs_3_, ...), custom_call_target="tpu_custom_call" | custom-call | flops 1000000000 | bytes 4194304 | tf_op jit(solution)/shard_map/pallas_call | solution.py:140
  24.2 2.2 %collective-permute-done.6.refs_6_ = bf16[192,768]{1,0:T(8,128)(2,1)S(1)} collective-permute-done((bf16[192,768]{1,0:T(8,128)(2,1)S(1)}, bf16[192,768]{1,0:T(8,128)(2,1)S(1)}, u32[]{:S(2)}, u32[]{:S(2)}) %collective-permute-start.6) | collective-permute-done | bytes 294944 | tf_op jit(solution)/shard_map/gather_authors/ppermute | solution.py:21
  26.4 2.8 %collective-permute-done.5.refs_4_ = bf16[192,768]{1,0:T(8,128)(2,1)S(1)} collective-permute-done((bf16[192,768]{1,0:T(8,128)(2,1)S(1)}, bf16[192,768]{1,0:T(8,128)(2,1)S(1)}, u32[]{:S(2)}, u32[]{:S(2)}) %collective-permute-start.5) | collective-permute-done | bytes 294944 | tf_op jit(solution)/shard_map/gather_authors/ppermute | solution.py:21
  29.3 0.1 collective-permute-start.7
  29.4 3.2 %collective-permute-start.8 = (bf16[128,768]{1,0:T(8,128)(2,1)S(1)}, bf16[128,768]{1,0:T(8,128)(2,1)S(1)}, u32[]{:S(2)}, u32[]{:S(2)}) collective-permute-start(bf16[128,768]{1,0:T(8,128)(2,1)S(1)} %slice.71), channel_id=1, source_target_pairs={{0,192},{64,0},{128,64},{192,128},{1,193},{65,1},{129,65},{193,129... | collective-permute-start | bytes 589832 | tf_op jit(solution)/shard_map/forward_authors/ppermute | solution.py:21
  32.7 3.6 %shard_map.115.refs_2_.base_ref = f32[1024,768]{1,0:T(8,128)S(1)} custom-call(s32[102]{0:T(128)S(1)} %concatenate.17.place, bf16[1024,2048]{1,0:T(8,128)(2,1)S(1)} %get-tuple-element.29.refs_0_.tile_ref, bf16[2,768,768]{2,1,0:T(8,128)(2,1)S(1)} %copy-done.1, f32[1024,768]{1,0:T(8,128)S(1)} %shard_map.114.refs_2_, ...), custom_call_target="tpu_custom_call" | custom-call | flops 1000000000 | bytes 4194304 | tf_op jit(solution)/shard_map/pallas_call | solution.py:140
  36.3 0.0 collective-permute-done.7.refs_3_
  36.3 1.8 %shard_map.116 = (bf16[4,2,64,768]{3,2,1,0:T(8,128)(2,1)S(1)}, bf16[512,768]{1,0:T(8,128)(2,1)S(1)}) custom-call(s32[102]{0:T(128)S(1)} %concatenate.17.place, bf16[1024,2048]{1,0:T(8,128)(2,1)S(1)} %get-tuple-element.29.refs_0_.tile_ref, bf16[2,768,768]{2,1,0:T(8,128)(2,1)S(1)} %copy-done.1, f32[1024,768]{1,0:T(8,128)S(1)} %shard_map.115.refs_2_.base_ref, ...), custom_call_target="tpu_custom_call" | custom-call | flops 1000000000 | bytes 4194304 | tf_op jit(solution)/shard_map/pallas_call | solution.py:140
  38.1 0.1 collective-permute-start.9
  38.2 0.6 shard_map.117
  38.8 1.7 %collective-permute-done.9 = bf16[4,2,64,768]{3,2,1,0:T(8,128)(2,1)S(1)} collective-permute-done((bf16[4,2,64,768]{3,2,1,0:T(8,128)(2,1)S(1)}, bf16[4,2,64,768]{3,2,1,0:T(8,128)(2,1)S(1)}, u32[]{:S(2)}, u32[]{:S(2)}) %collective-permute-start.9) | collective-permute-done | bytes 786464 | tf_op jit(solution)/shard_map/sum_papers/ppermute | solution.py:25
  40.5 0.2 fusion.17
  40.8 1.9 %collective-permute-start.10 = (bf16[2,64,768]{2,1,0:T(8,128)(2,1)S(1)}, bf16[2,64,768]{2,1,0:T(8,128)(2,1)S(1)}, u32[]{:S(2)}, u32[]{:S(2)}) collective-permute-start(bf16[2,64,768]{2,1,0:T(8,128)(2,1)S(1)} %get-tuple-element.56), channel_id=1, source_target_pairs={{0,4},{4,8},{8,12},{12,0},{1,5},{5,9},{9,13},{13,1},{2,6},{6,10},{... | collective-permute-start | bytes 589832 | tf_op jit(solution)/shard_map/sum_papers/ppermute | solution.py:21
  42.7 1.4 %collective-permute-start.12 = (bf16[2,64,768]{2,1,0:T(8,128)(2,1)S(1)}, bf16[2,64,768]{2,1,0:T(8,128)(2,1)S(1)}, u32[]{:S(2)}, u32[]{:S(2)}) collective-permute-start(bf16[2,64,768]{2,1,0:T(8,128)(2,1)S(1)} %get-tuple-element.57), channel_id=1, source_target_pairs={{0,12},{4,0},{8,4},{12,8},{1,13},{5,1},{9,5},{13,9},{2,14},{6,2},{... | collective-permute-start | bytes 589832 | tf_op jit(solution)/shard_map/sum_papers/ppermute | solution.py:21
  44.1 2.1 %collective-permute-start.11 = (bf16[2,64,768]{2,1,0:T(8,128)(2,1)S(1)}, bf16[2,64,768]{2,1,0:T(8,128)(2,1)S(1)}, u32[]{:S(2)}, u32[]{:S(2)}) collective-permute-start(bf16[2,64,768]{2,1,0:T(8,128)(2,1)S(1)} %get-tuple-element.58), channel_id=1, source_target_pairs={{0,8},{4,12},{8,0},{12,4},{1,9},{5,13},{9,1},{13,5},{2,10},{6,14},... | collective-permute-start | bytes 589832 | tf_op jit(solution)/shard_map/sum_papers/ppermute | solution.py:21
  46.2 2.8 %collective-permute-done.10 = bf16[2,64,768]{2,1,0:T(8,128)(2,1)S(1)} collective-permute-done((bf16[2,64,768]{2,1,0:T(8,128)(2,1)S(1)}, bf16[2,64,768]{2,1,0:T(8,128)(2,1)S(1)}, u32[]{:S(2)}, u32[]{:S(2)}) %collective-permute-start.10) | collective-permute-done | bytes 196640 | tf_op jit(solution)/shard_map/sum_papers/ppermute | solution.py:21
  49.0 1.5 %collective-permute-done.12 = bf16[2,64,768]{2,1,0:T(8,128)(2,1)S(1)} collective-permute-done((bf16[2,64,768]{2,1,0:T(8,128)(2,1)S(1)}, bf16[2,64,768]{2,1,0:T(8,128)(2,1)S(1)}, u32[]{:S(2)}, u32[]{:S(2)}) %collective-permute-start.12) | collective-permute-done | bytes 196640 | tf_op jit(solution)/shard_map/sum_papers/ppermute | solution.py:21
  50.5 3.6 %collective-permute-done.11 = bf16[2,64,768]{2,1,0:T(8,128)(2,1)S(1)} collective-permute-done((bf16[2,64,768]{2,1,0:T(8,128)(2,1)S(1)}, bf16[2,64,768]{2,1,0:T(8,128)(2,1)S(1)}, u32[]{:S(2)}, u32[]{:S(2)}) %collective-permute-start.11) | collective-permute-done | bytes 196640 | tf_op jit(solution)/shard_map/sum_papers/ppermute | solution.py:21
  54.0 0.1 fusion.2
  54.2 1.9 %collective-permute-start.13 = (bf16[2,64,768]{2,1,0:T(8,128)(2,1)S(1)}, bf16[2,64,768]{2,1,0:T(8,128)(2,1)S(1)}, u32[]{:S(2)}, u32[]{:S(2)}) collective-permute-start(bf16[2,64,768]{2,1,0:T(8,128)(2,1)S(1)} %fusion.15), channel_id=1, source_target_pairs={{0,2},{2,0},{1,3},{3,1},{4,6},{6,4},{5,7},{7,5},{8,10},{10,8},{9,1... | collective-permute-start | bytes 589832 | tf_op jit(solution)/shard_map/sum_papers/ppermute | solution.py:25
  56.2 4.3 %collective-permute-done.13.got_ref = bf16[2,64,768]{2,1,0:T(8,128)(2,1)S(1)} collective-permute-done((bf16[2,64,768]{2,1,0:T(8,128)(2,1)S(1)}, bf16[2,64,768]{2,1,0:T(8,128)(2,1)S(1)}, u32[]{:S(2)}, u32[]{:S(2)}) %collective-permute-start.13) | collective-permute-done | bytes 196640 | tf_op jit(solution)/shard_map/sum_papers/ppermute | solution.py:25
  60.5 0.8 shard_map.118
  61.3 1.7 %collective-permute-start.16 = (bf16[2,64,768]{2,1,0:T(8,128)(2,1)S(1)}, bf16[2,64,768]{2,1,0:T(8,128)(2,1)S(1)}, u32[]{:S(2)}, u32[]{:S(2)}) collective-permute-start(bf16[2,64,768]{2,1,0:T(8,128)(2,1)S(1)} %get-tuple-element.45.refs_0_), channel_id=1, source_target_pairs={{0,12},{4,0},{8,4},{12,8},{1,13},{5,1},{9,5},{13,9},{2,14},{6,2},{... | collective-permute-start | bytes 589832 | tf_op jit(solution)/shard_map/gather_papers/ppermute | solution.py:21
  63.1 1.1 %collective-permute-start.15 = (bf16[2,64,768]{2,1,0:T(8,128)(2,1)S(1)}, bf16[2,64,768]{2,1,0:T(8,128)(2,1)S(1)}, u32[]{:S(2)}, u32[]{:S(2)}) collective-permute-start(bf16[2,64,768]{2,1,0:T(8,128)(2,1)S(1)} %get-tuple-element.45.refs_0_), channel_id=1, source_target_pairs={{0,8},{4,12},{8,0},{12,4},{1,9},{5,13},{9,1},{13,5},{2,10},{6,14},... | collective-permute-start | bytes 589832 | tf_op jit(solution)/shard_map/gather_papers/ppermute | solution.py:21
  64.2 4.5 %collective-permute-done.16.refs_3_ = bf16[2,64,768]{2,1,0:T(8,128)(2,1)S(1)} collective-permute-done((bf16[2,64,768]{2,1,0:T(8,128)(2,1)S(1)}, bf16[2,64,768]{2,1,0:T(8,128)(2,1)S(1)}, u32[]{:S(2)}, u32[]{:S(2)}) %collective-permute-start.16) | collective-permute-done | bytes 196640 | tf_op jit(solution)/shard_map/gather_papers/ppermute | solution.py:21
  68.7 2.6 %collective-permute-done.15.refs_2_ = bf16[2,64,768]{2,1,0:T(8,128)(2,1)S(1)} collective-permute-done((bf16[2,64,768]{2,1,0:T(8,128)(2,1)S(1)}, bf16[2,64,768]{2,1,0:T(8,128)(2,1)S(1)}, u32[]{:S(2)}, u32[]{:S(2)}) %collective-permute-start.15) | collective-permute-done | bytes 196640 | tf_op jit(solution)/shard_map/gather_papers/ppermute | solution.py:21
  71.3 2.0 %collective-permute-done.14.refs_1_ = bf16[2,64,768]{2,1,0:T(8,128)(2,1)S(1)} collective-permute-done((bf16[2,64,768]{2,1,0:T(8,128)(2,1)S(1)}, bf16[2,64,768]{2,1,0:T(8,128)(2,1)S(1)}, u32[]{:S(2)}, u32[]{:S(2)}) %collective-permute-start.14) | collective-permute-done | bytes 196640 | tf_op jit(solution)/shard_map/gather_papers/ppermute | solution.py:21
  73.4 0.0 collective-permute-start.18
  73.4 1.4 %collective-permute-done.18.refs_5_ = bf16[2,64,768]{2,1,0:T(8,128)(2,1)S(1)} collective-permute-done((bf16[2,64,768]{2,1,0:T(8,128)(2,1)S(1)}, bf16[2,64,768]{2,1,0:T(8,128)(2,1)S(1)}, u32[]{:S(2)}, u32[]{:S(2)}) %collective-permute-start.18) | collective-permute-done | bytes 196640 | tf_op jit(solution)/shard_map/gather_papers/ppermute | solution.py:25
  74.8 1.8 %shard_map.119 = (f32[4,64,768]{2,1,0:T(8,128)S(1)}, f32[4,64,768]{2,1,0:T(8,128)S(1)}, f32[4,64,768]{2,1,0:T(8,128)S(1)}, bf16[4,32,768]{2,1,0:T(8,128)(2,1)S(1)}, bf16[4,32,768]{2,1,0:T(8,128)(2,1)S(1)}) custom-call(bf16[2,64,768]{2,1,0:T(8,128)(2,1)S(1)} %get-tuple-element.45.refs_0_, bf16[2,64,768]{2,1,0:T(8,128)(2,1)S(1)} %collective-permute-done.14.refs_1_, ...), custom_call_target="tpu_custom_call" | custom-call | flops 1000000000 | bytes 4194304 | tf_op jit(solution)/shard_map/pallas_call | solution.py:140
  76.6 0.1 collective-permute-start.21
  76.8 3.3 %collective-permute-start.23 = (bf16[4,32,768]{2,1,0:T(8,128)(2,1)S(1)}, bf16[4,32,768]{2,1,0:T(8,128)(2,1)S(1)}, u32[]{:S(2)}, u32[]{:S(2)}) collective-permute-start(bf16[4,32,768]{2,1,0:T(8,128)(2,1)S(1)} %get-tuple-element.51), channel_id=1, source_target_pairs={{0,192},{64,0},{128,64},{192,128},{1,193},{65,1},{129,65},{193,129... | collective-permute-start | bytes 589832 | tf_op jit(solution)/shard_map/sum_authors/ppermute | solution.py:21
  80.1 5.1 %collective-permute-done.21 = bf16[4,32,768]{2,1,0:T(8,128)(2,1)S(1)} collective-permute-done((bf16[4,32,768]{2,1,0:T(8,128)(2,1)S(1)}, bf16[4,32,768]{2,1,0:T(8,128)(2,1)S(1)}, u32[]{:S(2)}, u32[]{:S(2)}) %collective-permute-start.21) | collective-permute-done | bytes 196640 | tf_op jit(solution)/shard_map/sum_authors/ppermute | solution.py:21
  85.2 0.1 collective-permute-start.25
  85.4 3.3 %collective-permute-start.26 = (bf16[64,768]{1,0:T(8,128)(2,1)S(1)}, bf16[64,768]{1,0:T(8,128)(2,1)S(1)}, u32[]{:S(2)}, u32[]{:S(2)}) collective-permute-start(bf16[64,768]{1,0:T(8,128)(2,1)S(1)} %fusion.13), channel_id=1, source_target_pairs={{0,192},{64,0},{128,64},{192,128},{1,193},{65,1},{129,65},{193,129... | collective-permute-start | bytes 294920 | tf_op jit(solution)/shard_map/sum_authors/ppermute | solution.py:21
  88.7 0.6 collective-permute-start.24
  89.3 1.5 %collective-permute-start.22 = (bf16[3,64,768]{2,1,0:T(8,128)(2,1)S(1)}, bf16[3,64,768]{2,1,0:T(8,128)(2,1)S(1)}, u32[]{:S(2)}, u32[]{:S(2)}) collective-permute-start(bf16[3,64,768]{2,1,0:T(8,128)(2,1)S(1)} %fusion.4), channel_id=1, source_target_pairs={{0,64},{64,128},{128,192},{192,0},{1,65},{65,129},{129,193},{193,1... | collective-permute-start | bytes 884744 | tf_op jit(solution)/shard_map/sum_authors/ppermute | solution.py:21
  90.8 0.3 collective-permute-done.25
  91.1 0.8 collective-permute-done.26
  92.0 3.8 %collective-permute-start.27 = (bf16[64,768]{1,0:T(8,128)(2,1)S(1)}, bf16[64,768]{1,0:T(8,128)(2,1)S(1)}, u32[]{:S(2)}, u32[]{:S(2)}) collective-permute-start(bf16[64,768]{1,0:T(8,128)(2,1)S(1)} %fusion.12), channel_id=1, source_target_pairs={{0,32},{16,48},{32,0},{48,16},{1,33},{17,49},{33,1},{49,17},{2,34}... | collective-permute-start | bytes 294920 | tf_op jit(solution)/shard_map/sum_authors/ppermute | solution.py:21
  95.8 1.0 collective-permute-done.24
  96.8 1.3 %collective-permute-done.22 = bf16[3,64,768]{2,1,0:T(8,128)(2,1)S(1)} collective-permute-done((bf16[3,64,768]{2,1,0:T(8,128)(2,1)S(1)}, bf16[3,64,768]{2,1,0:T(8,128)(2,1)S(1)}, u32[]{:S(2)}, u32[]{:S(2)}) %collective-permute-start.22) | collective-permute-done | bytes 294944 | tf_op jit(solution)/shard_map/sum_authors/ppermute | solution.py:21
  98.1 0.1 fusion.16
  98.2 3.5 %collective-permute-start.28 = (bf16[64,768]{1,0:T(8,128)(2,1)S(1)}, bf16[64,768]{1,0:T(8,128)(2,1)S(1)}, u32[]{:S(2)}, u32[]{:S(2)}) collective-permute-start(bf16[64,768]{1,0:T(8,128)(2,1)S(1)} %get-tuple-element.59), channel_id=1, source_target_pairs={{0,16},{16,32},{32,48},{48,0},{1,17},{17,33},{33,49},{49,1},{2,18}... | collective-permute-start | bytes 294920 | tf_op jit(solution)/shard_map/sum_authors/ppermute | solution.py:21
  101.7 4.0 %collective-permute-done.28 = bf16[64,768]{1,0:T(8,128)(2,1)S(1)} collective-permute-done((bf16[64,768]{1,0:T(8,128)(2,1)S(1)}, bf16[64,768]{1,0:T(8,128)(2,1)S(1)}, u32[]{:S(2)}, u32[]{:S(2)}) %collective-permute-start.28) | collective-permute-done | bytes 98336 | tf_op jit(solution)/shard_map/sum_authors/ppermute | solution.py:21
  105.7 3.7 %collective-permute-done.29 = bf16[64,768]{1,0:T(8,128)(2,1)S(1)} collective-permute-done((bf16[64,768]{1,0:T(8,128)(2,1)S(1)}, bf16[64,768]{1,0:T(8,128)(2,1)S(1)}, u32[]{:S(2)}, u32[]{:S(2)}) %collective-permute-start.29) | collective-permute-done | bytes 98336 | tf_op jit(solution)/shard_map/sum_authors/ppermute | solution.py:21
  109.4 0.7 fusion.8
  (42 shorter events, 0.5 us)
Async XLA Ops:
  0.6 21.0 %copy-start = (bf16[768,768]{1,0:T(8,128)(2,1)S(1)}, bf16[768,768]{1,0:T(8,128)(2,1)}, u32[]{:S(2)}) copy-start(bf16[768,768]{1,0:T(8,128)(2,1)} %param.12) | copy-start | bytes 3538948
  0.6 18.8 %collective-permute-start.2 = (bf16[64,768]{1,0:T(8,128)(2,1)}, bf16[64,768]{1,0:T(8,128)(2,1)S(1)}, u32[]{:S(2)}, u32[]{:S(2)}) collective-permute-start(bf16[64,768]{1,0:T(8,128)(2,1)} %refs_2_.1), channel_id=1, source_target_pairs={{0,48},{16,0},{32,16},{48,32},{1,49},{17,1},{33,17},{49,33},{2,50}... | collective-permute-start | bytes 294920 | tf_op jit(solution)/shard_map/gather_authors/ppermute | solution.py:21
  2.1 17.3 %collective-permute-start.1 = (bf16[64,768]{1,0:T(8,128)(2,1)}, bf16[64,768]{1,0:T(8,128)(2,1)S(1)}, u32[]{:S(2)}, u32[]{:S(2)}) collective-permute-start(bf16[64,768]{1,0:T(8,128)(2,1)} %refs_2_.1), channel_id=1, source_target_pairs={{0,32},{16,48},{32,0},{48,16},{1,33},{17,49},{33,1},{49,17},{2,34}... | collective-permute-start | bytes 294920 | tf_op jit(solution)/shard_map/gather_authors/ppermute | solution.py:21
  7.6 11.9 %collective-permute-start = (bf16[64,768]{1,0:T(8,128)(2,1)}, bf16[64,768]{1,0:T(8,128)(2,1)S(1)}, u32[]{:S(2)}, u32[]{:S(2)}) collective-permute-start(bf16[64,768]{1,0:T(8,128)(2,1)} %refs_2_.1), channel_id=1, source_target_pairs={{0,16},{16,32},{32,48},{48,0},{1,17},{17,33},{33,49},{49,1},{2,18}... | collective-permute-start | bytes 294920 | tf_op jit(solution)/shard_map/gather_authors/ppermute | solution.py:21
  10.3 9.2 %collective-permute-start.3 = (bf16[64,768]{1,0:T(8,128)(2,1)}, bf16[64,768]{1,0:T(8,128)(2,1)S(1)}, u32[]{:S(2)}, u32[]{:S(2)}) collective-permute-start(bf16[64,768]{1,0:T(8,128)(2,1)} %refs_2_.1), channel_id=1, source_target_pairs={{0,64},{64,128},{128,192},{192,0},{1,65},{65,129},{129,193},{193,1... | collective-permute-start | bytes 294920 | tf_op jit(solution)/shard_map/gather_authors/ppermute | solution.py:21
  11.8 7.7 %collective-permute-start.4 = (bf16[64,768]{1,0:T(8,128)(2,1)}, bf16[64,768]{1,0:T(8,128)(2,1)S(1)}, u32[]{:S(2)}, u32[]{:S(2)}) collective-permute-start(bf16[64,768]{1,0:T(8,128)(2,1)} %refs_2_.1), channel_id=1, source_target_pairs={{0,192},{64,0},{128,64},{192,128},{1,193},{65,1},{129,65},{193,129... | collective-permute-start | bytes 294920 | tf_op jit(solution)/shard_map/gather_authors/ppermute | solution.py:21
  14.9 1.2 %copy-start.4 = (bf16[1,1,32,128,128]{4,3,2,1,0:T(8,128)(2,1)S(1)}, bf16[1,1,32,128,128]{4,3,2,1,0:T(8,128)(2,1)}, u32[]{:S(2)}) copy-start(bf16[1,1,32,128,128]{4,3,2,1,0:T(8,128)(2,1)} %param.19) | copy-start | bytes 3145732
  16.1 5.5 %copy-start.5 = (bf16[64,768]{1,0:T(8,128)(2,1)S(1)}, bf16[64,768]{1,0:T(8,128)(2,1)}, u32[]{:S(2)}) copy-start(bf16[64,768]{1,0:T(8,128)(2,1)} %param.10) | copy-start | bytes 294916
  16.1 5.8 %copy-start.1 = (bf16[2,768,768]{2,1,0:T(8,128)(2,1)S(1)}, bf16[2,768,768]{2,1,0:T(8,128)(2,1)}, u32[]{:S(2)}) copy-start(bf16[2,768,768]{2,1,0:T(8,128)(2,1)} %refs_1_.5) | copy-start | bytes 7077892
  19.4 2.6 %copy-start.3 = (bf16[64,768]{1,0:T(8,128)(2,1)S(1)}, bf16[64,768]{1,0:T(8,128)(2,1)}, u32[]{:S(2)}) copy-start(bf16[64,768]{1,0:T(8,128)(2,1)} %refs_2_.1) | copy-start | bytes 294916
  19.5 6.9 %collective-permute-start.6 = (bf16[192,768]{1,0:T(8,128)(2,1)S(1)}, bf16[192,768]{1,0:T(8,128)(2,1)S(1)}, u32[]{:S(2)}, u32[]{:S(2)}) collective-permute-start(bf16[192,768]{1,0:T(8,128)(2,1)S(1)} %constant_dynamic-update-slice_fusion), channel_id=1, source_target_pairs={{0,192},{64,0},{128,64},{192,128},{1,193},{65,1},{129,65},{193,129... | collective-permute-start | bytes 884744 | tf_op jit(solution)/shard_map/gather_authors/ppermute | solution.py:21
  20.6 8.7 %collective-permute-start.5 = (bf16[192,768]{1,0:T(8,128)(2,1)S(1)}, bf16[192,768]{1,0:T(8,128)(2,1)S(1)}, u32[]{:S(2)}, u32[]{:S(2)}) collective-permute-start(bf16[192,768]{1,0:T(8,128)(2,1)S(1)} %constant_dynamic-update-slice_fusion), channel_id=1, source_target_pairs={{0,64},{64,128},{128,192},{192,0},{1,65},{65,129},{129,193},{193,1... | collective-permute-start | bytes 884744 | tf_op jit(solution)/shard_map/gather_authors/ppermute | solution.py:21
  29.3 7.0 %collective-permute-start.7 = (bf16[128,768]{1,0:T(8,128)(2,1)S(1)}, bf16[128,768]{1,0:T(8,128)(2,1)S(1)}, u32[]{:S(2)}, u32[]{:S(2)}) collective-permute-start(bf16[128,768]{1,0:T(8,128)(2,1)S(1)} %pad_maximum_fusion.1), channel_id=1, source_target_pairs={{0,64},{64,128},{128,192},{192,0},{1,65},{65,129},{129,193},{193,1... | collective-permute-start | bytes 589832 | tf_op jit(solution)/shard_map/forward_authors/ppermute | solution.py:21
  29.4 6.9 %collective-permute-start.8 = (bf16[128,768]{1,0:T(8,128)(2,1)S(1)}, bf16[128,768]{1,0:T(8,128)(2,1)S(1)}, u32[]{:S(2)}, u32[]{:S(2)}) collective-permute-start(bf16[128,768]{1,0:T(8,128)(2,1)S(1)} %slice.71), channel_id=1, source_target_pairs={{0,192},{64,0},{128,64},{192,128},{1,193},{65,1},{129,65},{193,129... | collective-permute-start | bytes 589832 | tf_op jit(solution)/shard_map/forward_authors/ppermute | solution.py:21
  38.1 2.4 %collective-permute-start.9 = (bf16[4,2,64,768]{3,2,1,0:T(8,128)(2,1)S(1)}, bf16[4,2,64,768]{3,2,1,0:T(8,128)(2,1)S(1)}, u32[]{:S(2)}, u32[]{:S(2)}) collective-permute-start(bf16[4,2,64,768]{3,2,1,0:T(8,128)(2,1)S(1)} %get-tuple-element.42), channel_id=1, source_target_pairs={{0,1},{1,0},{2,3},{3,2},{4,5},{5,4},{6,7},{7,6},{8,9},{9,8},{10,11... | collective-permute-start | bytes 2359304 | tf_op jit(solution)/shard_map/sum_papers/ppermute | solution.py:25
  40.8 8.2 %collective-permute-start.10 = (bf16[2,64,768]{2,1,0:T(8,128)(2,1)S(1)}, bf16[2,64,768]{2,1,0:T(8,128)(2,1)S(1)}, u32[]{:S(2)}, u32[]{:S(2)}) collective-permute-start(bf16[2,64,768]{2,1,0:T(8,128)(2,1)S(1)} %get-tuple-element.56), channel_id=1, source_target_pairs={{0,4},{4,8},{8,12},{12,0},{1,5},{5,9},{9,13},{13,1},{2,6},{6,10},{... | collective-permute-start | bytes 589832 | tf_op jit(solution)/shard_map/sum_papers/ppermute | solution.py:21
  42.7 7.8 %collective-permute-start.12 = (bf16[2,64,768]{2,1,0:T(8,128)(2,1)S(1)}, bf16[2,64,768]{2,1,0:T(8,128)(2,1)S(1)}, u32[]{:S(2)}, u32[]{:S(2)}) collective-permute-start(bf16[2,64,768]{2,1,0:T(8,128)(2,1)S(1)} %get-tuple-element.57), channel_id=1, source_target_pairs={{0,12},{4,0},{8,4},{12,8},{1,13},{5,1},{9,5},{13,9},{2,14},{6,2},{... | collective-permute-start | bytes 589832 | tf_op jit(solution)/shard_map/sum_papers/ppermute | solution.py:21
  44.1 9.9 %collective-permute-start.11 = (bf16[2,64,768]{2,1,0:T(8,128)(2,1)S(1)}, bf16[2,64,768]{2,1,0:T(8,128)(2,1)S(1)}, u32[]{:S(2)}, u32[]{:S(2)}) collective-permute-start(bf16[2,64,768]{2,1,0:T(8,128)(2,1)S(1)} %get-tuple-element.58), channel_id=1, source_target_pairs={{0,8},{4,12},{8,0},{12,4},{1,9},{5,13},{9,1},{13,5},{2,10},{6,14},... | collective-permute-start | bytes 589832 | tf_op jit(solution)/shard_map/sum_papers/ppermute | solution.py:21
  54.0 6.5 %copy-start.2 = (bf16[768,768]{1,0:T(8,128)(2,1)S(1)}, bf16[768,768]{1,0:T(8,128)(2,1)}, u32[]{:S(2)}) copy-start(bf16[768,768]{1,0:T(8,128)(2,1)} %w_ref.1) | copy-start | bytes 3538948
  54.2 6.3 %collective-permute-start.13 = (bf16[2,64,768]{2,1,0:T(8,128)(2,1)S(1)}, bf16[2,64,768]{2,1,0:T(8,128)(2,1)S(1)}, u32[]{:S(2)}, u32[]{:S(2)}) collective-permute-start(bf16[2,64,768]{2,1,0:T(8,128)(2,1)S(1)} %fusion.15), channel_id=1, source_target_pairs={{0,2},{2,0},{1,3},{3,1},{4,6},{6,4},{5,7},{7,5},{8,10},{10,8},{9,1... | collective-permute-start | bytes 589832 | tf_op jit(solution)/shard_map/sum_papers/ppermute | solution.py:25
  61.3 7.4 %collective-permute-start.16 = (bf16[2,64,768]{2,1,0:T(8,128)(2,1)S(1)}, bf16[2,64,768]{2,1,0:T(8,128)(2,1)S(1)}, u32[]{:S(2)}, u32[]{:S(2)}) collective-permute-start(bf16[2,64,768]{2,1,0:T(8,128)(2,1)S(1)} %get-tuple-element.45.refs_0_), channel_id=1, source_target_pairs={{0,12},{4,0},{8,4},{12,8},{1,13},{5,1},{9,5},{13,9},{2,14},{6,2},{... | collective-permute-start | bytes 589832 | tf_op jit(solution)/shard_map/gather_papers/ppermute | solution.py:21
  63.1 8.3 %collective-permute-start.15 = (bf16[2,64,768]{2,1,0:T(8,128)(2,1)S(1)}, bf16[2,64,768]{2,1,0:T(8,128)(2,1)S(1)}, u32[]{:S(2)}, u32[]{:S(2)}) collective-permute-start(bf16[2,64,768]{2,1,0:T(8,128)(2,1)S(1)} %get-tuple-element.45.refs_0_), channel_id=1, source_target_pairs={{0,8},{4,12},{8,0},{12,4},{1,9},{5,13},{9,1},{13,5},{2,10},{6,14},... | collective-permute-start | bytes 589832 | tf_op jit(solution)/shard_map/gather_papers/ppermute | solution.py:21
  64.2 9.2 %collective-permute-start.14 = (bf16[2,64,768]{2,1,0:T(8,128)(2,1)S(1)}, bf16[2,64,768]{2,1,0:T(8,128)(2,1)S(1)}, u32[]{:S(2)}, u32[]{:S(2)}) collective-permute-start(bf16[2,64,768]{2,1,0:T(8,128)(2,1)S(1)} %get-tuple-element.45.refs_0_), channel_id=1, source_target_pairs={{0,4},{4,8},{8,12},{12,0},{1,5},{5,9},{9,13},{13,1},{2,6},{6,10},{... | collective-permute-start | bytes 589832 | tf_op jit(solution)/shard_map/gather_papers/ppermute | solution.py:21
  64.2 9.2 %collective-permute-start.17 = (bf16[2,64,768]{2,1,0:T(8,128)(2,1)S(1)}, bf16[2,64,768]{2,1,0:T(8,128)(2,1)S(1)}, u32[]{:S(2)}, u32[]{:S(2)}) collective-permute-start(bf16[2,64,768]{2,1,0:T(8,128)(2,1)S(1)} %get-tuple-element.45.refs_0_), channel_id=1, source_target_pairs={{0,1},{1,0},{2,3},{3,2},{4,5},{5,4},{6,7},{7,6},{8,9},{9,8},{10,11... | collective-permute-start | bytes 589832 | tf_op jit(solution)/shard_map/gather_papers/ppermute | solution.py:25
  68.7 4.7 %collective-permute-start.20 = (bf16[2,64,768]{2,1,0:T(8,128)(2,1)S(1)}, bf16[2,64,768]{2,1,0:T(8,128)(2,1)S(1)}, u32[]{:S(2)}, u32[]{:S(2)}) collective-permute-start(bf16[2,64,768]{2,1,0:T(8,128)(2,1)S(1)} %collective-permute-done.16.refs_3_), channel_id=1, source_target_pairs={{0,1},{1,0},{2,3},{3,2},{4,5},{5,4},{6,7},{7,6},{8,9},{9,8},{10,11... | collective-permute-start | bytes 589832 | tf_op jit(solution)/shard_map/gather_papers/ppermute | solution.py:25
  71.3 2.1 %collective-permute-start.19 = (bf16[2,64,768]{2,1,0:T(8,128)(2,1)S(1)}, bf16[2,64,768]{2,1,0:T(8,128)(2,1)S(1)}, u32[]{:S(2)}, u32[]{:S(2)}) collective-permute-start(bf16[2,64,768]{2,1,0:T(8,128)(2,1)S(1)} %collective-permute-done.15.refs_2_), channel_id=1, source_target_pairs={{0,1},{1,0},{2,3},{3,2},{4,5},{5,4},{6,7},{7,6},{8,9},{9,8},{10,11... | collective-permute-start | bytes 589832 | tf_op jit(solution)/shard_map/gather_papers/ppermute | solution.py:25
  73.4 1.4 %collective-permute-start.18 = (bf16[2,64,768]{2,1,0:T(8,128)(2,1)S(1)}, bf16[2,64,768]{2,1,0:T(8,128)(2,1)S(1)}, u32[]{:S(2)}, u32[]{:S(2)}) collective-permute-start(bf16[2,64,768]{2,1,0:T(8,128)(2,1)S(1)} %collective-permute-done.14.refs_1_), channel_id=1, source_target_pairs={{0,1},{1,0},{2,3},{3,2},{4,5},{5,4},{6,7},{7,6},{8,9},{9,8},{10,11... | collective-permute-start | bytes 589832 | tf_op jit(solution)/shard_map/gather_papers/ppermute | solution.py:25
  76.6 8.5 %collective-permute-start.21 = (bf16[4,32,768]{2,1,0:T(8,128)(2,1)S(1)}, bf16[4,32,768]{2,1,0:T(8,128)(2,1)S(1)}, u32[]{:S(2)}, u32[]{:S(2)}) collective-permute-start(bf16[4,32,768]{2,1,0:T(8,128)(2,1)S(1)} %get-tuple-element.49), channel_id=1, source_target_pairs={{0,64},{64,128},{128,192},{192,0},{1,65},{65,129},{129,193},{193,1... | collective-permute-start | bytes 589832 | tf_op jit(solution)/shard_map/sum_authors/ppermute | solution.py:21
  76.8 8.5 %collective-permute-start.23 = (bf16[4,32,768]{2,1,0:T(8,128)(2,1)S(1)}, bf16[4,32,768]{2,1,0:T(8,128)(2,1)S(1)}, u32[]{:S(2)}, u32[]{:S(2)}) collective-permute-start(bf16[4,32,768]{2,1,0:T(8,128)(2,1)S(1)} %get-tuple-element.51), channel_id=1, source_target_pairs={{0,192},{64,0},{128,64},{192,128},{1,193},{65,1},{129,65},{193,129... | collective-permute-start | bytes 589832 | tf_op jit(solution)/shard_map/sum_authors/ppermute | solution.py:21
  85.2 5.9 %collective-permute-start.25 = (bf16[64,768]{1,0:T(8,128)(2,1)S(1)}, bf16[64,768]{1,0:T(8,128)(2,1)S(1)}, u32[]{:S(2)}, u32[]{:S(2)}) collective-permute-start(bf16[64,768]{1,0:T(8,128)(2,1)S(1)} %fusion.14), channel_id=1, source_target_pairs={{0,64},{64,128},{128,192},{192,0},{1,65},{65,129},{129,193},{193,1... | collective-permute-start | bytes 294920 | tf_op jit(solution)/shard_map/sum_authors/ppermute | solution.py:21
  85.4 6.5 %collective-permute-start.26 = (bf16[64,768]{1,0:T(8,128)(2,1)S(1)}, bf16[64,768]{1,0:T(8,128)(2,1)S(1)}, u32[]{:S(2)}, u32[]{:S(2)}) collective-permute-start(bf16[64,768]{1,0:T(8,128)(2,1)S(1)} %fusion.13), channel_id=1, source_target_pairs={{0,192},{64,0},{128,64},{192,128},{1,193},{65,1},{129,65},{193,129... | collective-permute-start | bytes 294920 | tf_op jit(solution)/shard_map/sum_authors/ppermute | solution.py:21
  88.7 8.0 %collective-permute-start.24 = (bf16[3,64,768]{2,1,0:T(8,128)(2,1)S(1)}, bf16[3,64,768]{2,1,0:T(8,128)(2,1)S(1)}, u32[]{:S(2)}, u32[]{:S(2)}) collective-permute-start(bf16[3,64,768]{2,1,0:T(8,128)(2,1)S(1)} %fusion.3), channel_id=1, source_target_pairs={{0,192},{64,0},{128,64},{192,128},{1,193},{65,1},{129,65},{193,129... | collective-permute-start | bytes 884744 | tf_op jit(solution)/shard_map/sum_authors/ppermute | solution.py:21
  89.3 8.7 %collective-permute-start.22 = (bf16[3,64,768]{2,1,0:T(8,128)(2,1)S(1)}, bf16[3,64,768]{2,1,0:T(8,128)(2,1)S(1)}, u32[]{:S(2)}, u32[]{:S(2)}) collective-permute-start(bf16[3,64,768]{2,1,0:T(8,128)(2,1)S(1)} %fusion.4), channel_id=1, source_target_pairs={{0,64},{64,128},{128,192},{192,0},{1,65},{65,129},{129,193},{193,1... | collective-permute-start | bytes 884744 | tf_op jit(solution)/shard_map/sum_authors/ppermute | solution.py:21
  92.0 9.7 %collective-permute-start.27 = (bf16[64,768]{1,0:T(8,128)(2,1)S(1)}, bf16[64,768]{1,0:T(8,128)(2,1)S(1)}, u32[]{:S(2)}, u32[]{:S(2)}) collective-permute-start(bf16[64,768]{1,0:T(8,128)(2,1)S(1)} %fusion.12), channel_id=1, source_target_pairs={{0,32},{16,48},{32,0},{48,16},{1,33},{17,49},{33,1},{49,17},{2,34}... | collective-permute-start | bytes 294920 | tf_op jit(solution)/shard_map/sum_authors/ppermute | solution.py:21
  98.2 7.5 %collective-permute-start.28 = (bf16[64,768]{1,0:T(8,128)(2,1)S(1)}, bf16[64,768]{1,0:T(8,128)(2,1)S(1)}, u32[]{:S(2)}, u32[]{:S(2)}) collective-permute-start(bf16[64,768]{1,0:T(8,128)(2,1)S(1)} %get-tuple-element.59), channel_id=1, source_target_pairs={{0,16},{16,32},{32,48},{48,0},{1,17},{17,33},{33,49},{49,1},{2,18}... | collective-permute-start | bytes 294920 | tf_op jit(solution)/shard_map/sum_authors/ppermute | solution.py:21
  101.7 7.8 %collective-permute-start.29 = (bf16[64,768]{1,0:T(8,128)(2,1)S(1)}, bf16[64,768]{1,0:T(8,128)(2,1)S(1)}, u32[]{:S(2)}, u32[]{:S(2)}) collective-permute-start(bf16[64,768]{1,0:T(8,128)(2,1)S(1)} %get-tuple-element.60), channel_id=1, source_target_pairs={{0,48},{16,0},{32,16},{48,32},{1,49},{17,1},{33,17},{49,33},{2,50}... | collective-permute-start | bytes 294920 | tf_op jit(solution)/shard_map/sum_authors/ppermute | solution.py:21

commit v5 on v4

--- a/solution.py
+++ b/solution.py
@@ -29,35 +29,49 @@
     return lax.rem(at + (RING - by), RING)
 
 
-def build_tiles(place, vals, one_ref, two_ref):
-    y, zh, x, zl, core = (place[i] for i in range(PLACE))
+def build_one(place, vals, one_ref):
+    y, _, x, zl, core = (place[i] for i in range(PLACE))
     slots, side = vals.shape[:2]
     half = side // 2
     span = RING * half
-    relations = one_ref.shape[1] // two_ref.shape[1]
+    relations = one_ref.shape[1] // one_ref.shape[0]
     one_ref[...] = jnp.zeros_like(one_ref)
-    two_ref[...] = jnp.zeros_like(two_ref)
 
     def slot(k, carry):
         row, col, kind = (place[PLACE + 1 + i * slots + k] for i in range(3))
-        block = [vals[k, pl.ds(pl.multiple_of(c * half, half), half), :] for c in (core, 1 - core)]
-        turned = jnp.concatenate(block).T
         d = lax.rem(y + RING - lax.div(col, 2), RING)
         group = jnp.where(d == 2, 3, jnp.where(d == 3, 2, d))
         at = (group * relations + kind) * span + lax.rem(col, 2) * side
         lanes = pl.ds(pl.multiple_of(at, side), side)
         d = lax.rem(lax.div(row, 2) + RING - x, RING)
         e = jnp.where(lax.rem(row, 2) == zl, 0, 1)
-        for c in range(2):
-            at = (c * RING + d) * side + e * half
-            one_ref[pl.ds(pl.multiple_of(at, half), half), lanes] = block[c]
+        for i, c in enumerate((core, 1 - core)):
+            at = (i * RING + d) * side + e * half
+            block = vals[k, pl.ds(pl.multiple_of(c * half, half), half), :]
+            one_ref[pl.ds(pl.multiple_of(at, half), half), lanes] = block
+        return carry
+
+    lax.fori_loop(0, place[PLACE], slot, 0)
+
+
+def build_two(place, vals, two_ref):
+    y, zh, x, zl, core = (place[i] for i in range(PLACE))
+    slots, side = vals.shape[:2]
+    half = side // 2
+    two_ref[...] = jnp.zeros_like(two_ref)
+
+    def slot(k, carry):
+        row, col = (place[PLACE + 1 + i * slots + k] for i in range(2))
+        block = [vals[k, pl.ds(pl.multiple_of(c * half, half), half), :] for c in (core, 1 - core)]
+        turned = jnp.concatenate(block).T
         d = lax.rem(x + RING - lax.div(row, 2), RING)
+        e = jnp.where(lax.rem(row, 2) == zl, 0, 1)
         lanes = pl.ds(pl.multiple_of((d * 2 + e) * side, side), side)
         d = lax.rem(lax.div(col, 2) + RING - y, RING)
         for c in range(2):
             e = lax.rem(lax.rem(col, 2) * 2 + c + RING - zh, RING)
             place_of = jnp.where(e == 2, 0, jnp.where(e == 3, 3, e + 1))
-            at = d * span + place_of * half
+            at = (d * RING + place_of) * half
             two_ref[pl.ds(pl.multiple_of(at, half), half), lanes] = turned[c * half : (c + 1) * half]
         return carry
 
@@ -104,25 +118,26 @@
         out_ref[2 * step : 2 * step + 2] = made.reshape(2, *out_ref.shape[1:])
 
 
-def hop_two(*refs):
-    mine, other, refs = refs[:4], refs[4:8], refs[8:]
-    tile_ref, same_ref, up_ref, down_ref, two_up_ref, two_down_ref, table = refs
-    own, width = same_ref.shape[1:]
-    span = RING * own
+def hop_two_first(*refs):
+    mine, other, (tile_ref, two_up_ref, two_down_ref, table_ref) = refs[:RING], refs[RING : 2 * RING], refs[2 * RING :]
+    own = two_up_ref.shape[1] * 2
     for d in range(RING):
         for e in range(2):
             at = (d * 2 + e) * 2 * own
-            table[at : at + own, :] = mine[d][e]
-            table[at + own : at + 2 * own, :] = other[d][e]
-    for d in range(RING):
-        made = jnp.dot(tile_ref[d * span : (d + 1) * span, :], table[...], preferred_element_type=F32)
-        made = made.reshape(RING, own, width)
-        if d == 2:
-            two_up_ref[...] = made[:, : own // 2].astype(BF16)
-            two_down_ref[...] = made[:, own // 2 :].astype(BF16)
-        else:
-            out = (same_ref, up_ref, None, down_ref)[d]
-            out[...] = made
+            table_ref[at : at + own, :] = mine[d][e]
+            table_ref[at + own : at + 2 * own, :] = other[d][e]
+    span = RING * own
+    made = jnp.dot(tile_ref[2 * span : 3 * span, :], table_ref[...], preferred_element_type=F32)
+    made = made.astype(BF16).reshape(RING, own, table_ref.shape[1])
+    two_up_ref[...] = made[:, : own // 2]
+    two_down_ref[...] = made[:, own // 2 :]
+
+
+def hop_two_rest(table_ref, tile_ref, same_ref, up_ref, down_ref):
+    span = same_ref.shape[0] * same_ref.shape[1]
+    for d, out in ((1, up_ref), (3, down_ref), (0, same_ref)):
+        made = jnp.dot(tile_ref[d * span : (d + 1) * span, :], table_ref[...], preferred_element_type=F32)
+        out[...] = made.reshape(out.shape)
 
 
 def hidden_step(base_ref, got_ref, w_ref, hidden_ref, out_ref):
@@ -165,17 +180,8 @@
         return jax.ShapeDtypeStruct((*dims, own, width), dtype)
 
     relations = w_rel.shape[0]
-    tile_one, tile_two = call(
-        build_tiles,
-        10**9,
-        (place,),
-        (vals,),
-        (
-            jax.ShapeDtypeStruct((tile_rows, relations * tile_rows), BF16),
-            jax.ShapeDtypeStruct((tile_rows, tile_rows), BF16),
-        ),
-        [],
-    )
+    tile = jax.ShapeDtypeStruct((tile_rows, relations * tile_rows), BF16)
+    tile_one = call(build_one, 10**9, (place,), (vals,), tile, [])
     self_term = jnp.dot(paper_x, w_self, preferred_element_type=F32)
     span = RING * own
 
@@ -195,7 +201,7 @@
     base_shape = jax.ShapeDtypeStruct((tile_rows, width), F32)
     with jax.named_scope("gather_authors"):
         by_z = [shift(author_x, "zh", e) for e in range(1, RING)]
-        by_z, tile_one, tile_two = lax.optimization_barrier((by_z, tile_one, tile_two))
+        by_z, tile_one = lax.optimization_barrier((by_z, tile_one))
         own_up, own_down = shift(author_x, "y", 1), shift(author_x, "y", RING - 1)
         by_z, own_up, own_down = lax.optimization_barrier((by_z, own_up, own_down))
         relay = jnp.concatenate(by_z)
@@ -221,7 +227,12 @@
         by_x = [shift(pair[d].astype(BF16), "x", d) for d in range(1, RING)]
         both = total_of([pair[0], *by_x])
         both = jnp.stack([both[0] + self_term, both[1]])
+        both, place = lax.optimization_barrier((both, place))
         got = swap(both.astype(BF16), "zl")
+    tile_two = call(
+        build_two, 10**9, (place,), (vals,), jax.ShapeDtypeStruct((tile_rows, tile_rows), BF16), []
+    )
+    got, tile_two = lax.optimization_barrier((got, tile_two))
     paper_hidden, outgoing = call(
         hidden_step, 4 * own * width * width, (), (both, got, w_two), (shaped(), shaped(2)), []
     )
@@ -230,14 +241,15 @@
         other = [swap(m, "core") for m in mine]
     whole = shaped(RING, dtype=F32)
     piece = jax.ShapeDtypeStruct((RING, own // 2, width), BF16)
-    same, up, down, two_up, two_down = call(
-        hop_two,
+    two_up, two_down, table = call(
+        hop_two_first,
         10**9,
         (),
         (*mine, *other, tile_two),
-        (whole, whole, whole, piece, piece),
-        [pltpu.VMEM((tile_rows, width), BF16)],
-    )
+        (piece, piece, jax.ShapeDtypeStruct((tile_rows, width), BF16)),
+        [],
+    )
+    same, up, down = call(hop_two_rest, 10**9, (), (table, tile_two), (whole, whole, whole), [])
     with jax.named_scope("sum_authors"):
         half = own // 2
         from_down = shift(two_up, "y", 1).astype(F32)

time: 110 us -> 110 us (level)
  waiting for transfers between devices: 45.7 us -> 43.3 us
  starting transfers between devices: 44.8 us -> 46.7 us
    ppermute x6, waiting for transfers between devices: 7.46 us -> 5.26 us  [swap(): return lax.ppermute(value, axis, [(0, 1), (1, 0)])]
    pallas_call x7 -> x9, Pallas kernels: 14.1 us -> 14.6 us  [call(): pl.pallas_call(kernel, out_shape=out_shape, in_specs=[spec(pltpu.SMEM)] *...]
  transfers between devices with their start and end apart: 30 -> 30, of which waited for: 18 -> 18; matrix products, arithmetic and copies ran while one was open for 1% -> 1% of each run, Pallas kernels for 9% -> 10%
where the time goes in v5:
time: 110 us
  starting transfers between devices  46.7 us (42%)
  waiting for transfers between devices  43.3 us (39%)
  Pallas kernels  14.6 us (13%)
  local copies, waits for them, and re-layouts  2.2 us (2%)
  between operations  1.66 us (2%)
  other arithmetic  1.37 us (1%)
    ppermute x24, starting transfers between devices, shift(): lax.ppermute(value, axis, [(i, (i + by) % RING) for i in range(RING)])  43.7 us
    ppermute x24, waiting for transfers between devices, shift(): lax.ppermute(value, axis, [(i, (i + by) % RING) for i in range(RING)])  38 us
    pallas_call x9, Pallas kernels, call(): pl.pallas_call(kernel, out_shape=out_shape, in_specs=[spec(pltpu.SMEM)] *...  14.6 us
    ppermute x6, waiting for transfers between devices, swap(): return lax.ppermute(value, axis, [(0, 1), (1, 0)])  5.26 us
    ppermute x6, starting transfers between devices, swap(): return lax.ppermute(value, axis, [(0, 1), (1, 0)])  3.01 us
  transfers between devices with their start and end apart: 30, of which 18 were waited for; matrix products, arithmetic and copies ran while one was open for 1% of the time, Pallas kernels for 10%

profile of v5, /device:TPU:64, one launch (start us, length us, event | category | flops | bytes accessed | tf_op | source)
XLA Modules:
  0.0 110.2 jit_solution(8665062522347866060)
XLA Ops:
  0.6 0.0 copy-start
  0.6 1.5 %collective-permute-start.2 = (bf16[64,768]{1,0:T(8,128)(2,1)}, bf16[64,768]{1,0:T(8,128)(2,1)S(1)}, u32[]{:S(2)}, u32[]{:S(2)}) collective-permute-start(bf16[64,768]{1,0:T(8,128)(2,1)} %refs_2_.1), channel_id=1, source_target_pairs={{0,48},{16,0},{32,16},{48,32},{1,49},{17,1},{33,17},{49,33},{2,50}... | collective-permute-start | bytes 294920 | tf_op jit(solution)/shard_map/gather_authors/ppermute | solution.py:21
  2.1 5.5 %collective-permute-start.1 = (bf16[64,768]{1,0:T(8,128)(2,1)}, bf16[64,768]{1,0:T(8,128)(2,1)S(1)}, u32[]{:S(2)}, u32[]{:S(2)}) collective-permute-start(bf16[64,768]{1,0:T(8,128)(2,1)} %refs_2_.1), channel_id=1, source_target_pairs={{0,32},{16,48},{32,0},{48,16},{1,33},{17,49},{33,1},{49,17},{2,34}... | collective-permute-start | bytes 294920 | tf_op jit(solution)/shard_map/gather_authors/ppermute | solution.py:21
  7.6 2.7 %collective-permute-start = (bf16[64,768]{1,0:T(8,128)(2,1)}, bf16[64,768]{1,0:T(8,128)(2,1)S(1)}, u32[]{:S(2)}, u32[]{:S(2)}) collective-permute-start(bf16[64,768]{1,0:T(8,128)(2,1)} %refs_2_.1), channel_id=1, source_target_pairs={{0,16},{16,32},{32,48},{48,0},{1,17},{17,33},{33,49},{49,1},{2,18}... | collective-permute-start | bytes 294920 | tf_op jit(solution)/shard_map/gather_authors/ppermute | solution.py:21
  10.3 1.6 %collective-permute-start.3 = (bf16[64,768]{1,0:T(8,128)(2,1)}, bf16[64,768]{1,0:T(8,128)(2,1)S(1)}, u32[]{:S(2)}, u32[]{:S(2)}) collective-permute-start(bf16[64,768]{1,0:T(8,128)(2,1)} %refs_2_.1), channel_id=1, source_target_pairs={{0,64},{64,128},{128,192},{192,0},{1,65},{65,129},{129,193},{193,1... | collective-permute-start | bytes 294920 | tf_op jit(solution)/shard_map/gather_authors/ppermute | solution.py:21
  11.8 1.7 %collective-permute-start.4 = (bf16[64,768]{1,0:T(8,128)(2,1)}, bf16[64,768]{1,0:T(8,128)(2,1)S(1)}, u32[]{:S(2)}, u32[]{:S(2)}) collective-permute-start(bf16[64,768]{1,0:T(8,128)(2,1)} %refs_2_.1), channel_id=1, source_target_pairs={{0,192},{64,0},{128,64},{192,128},{1,193},{65,1},{129,65},{193,129... | collective-permute-start | bytes 294920 | tf_op jit(solution)/shard_map/gather_authors/ppermute | solution.py:21
  14.1 0.8 concatenate.17.place
  14.9 1.2 %copy-done.3 = bf16[1,1,32,128,128]{4,3,2,1,0:T(8,128)(2,1)S(1)} copy-done((bf16[1,1,32,128,128]{4,3,2,1,0:T(8,128)(2,1)S(1)}, bf16[1,1,32,128,128]{4,3,2,1,0:T(8,128)(2,1)}, u32[]{:S(2)}) %copy-start.3) | copy-done | bytes 1048600
  16.1 1.4 %shard_map.113.refs_0_.tile_ref = bf16[1024,2048]{1,0:T(8,128)(2,1)S(1)} custom-call(s32[102]{0:T(128)S(1)} %concatenate.17.place, bf16[32,128,128]{2,1,0:T(8,128)(2,1)S(1)} %bitcast.59), custom_call_target="tpu_custom_call" | custom-call | flops 1000000000 | bytes 4194304 | tf_op jit(solution)/shard_map/pallas_call | solution.py:155
  17.5 0.0 copy-start.5
  17.5 0.0 collective-permute-done.2.refs_5_
  17.6 0.0 collective-permute-done.3.refs_3_
  17.7 2.0 %collective-permute-start.6 = (bf16[192,768]{1,0:T(8,128)(2,1)S(1)}, bf16[192,768]{1,0:T(8,128)(2,1)S(1)}, u32[]{:S(2)}, u32[]{:S(2)}) collective-permute-start(bf16[192,768]{1,0:T(8,128)(2,1)S(1)} %constant_dynamic-update-slice_fusion), channel_id=1, source_target_pairs={{0,192},{64,0},{128,64},{192,128},{1,193},{65,1},{129,65},{193,129... | collective-permute-start | bytes 884744 | tf_op jit(solution)/shard_map/gather_authors/ppermute | solution.py:21
  19.6 0.1 collective-permute-start.5
  19.8 0.3 fusion.17
  20.1 0.0 copy-done.1
  20.1 2.2 %shard_map.114.refs_2_ = f32[1024,768]{1,0:T(8,128)S(1)} custom-call(s32[102]{0:T(128)S(1)} %concatenate.17.place, bf16[1024,2048]{1,0:T(8,128)(2,1)S(1)} %shard_map.113.refs_0_.tile_ref, bf16[2,768,768]{2,1,0:T(8,128)(2,1)S(1)} %copy-done.1, bf16[64,768]{1,0:T(8,128)(2,1)S(1)} %copy-done.5, bf16[64,768]{1,0:T(8,128)(2,1)S(1)} %collective-permute-done.refs_3_, ...), custom_call_target="tpu_custom_call" | custom-call | flops 1000000000 | bytes 4194304 | tf_op jit(solution)/shard_map/pallas_call | solution.py:155
  22.3 2.9 %collective-permute-done.6.refs_6_ = bf16[192,768]{1,0:T(8,128)(2,1)S(1)} collective-permute-done((bf16[192,768]{1,0:T(8,128)(2,1)S(1)}, bf16[192,768]{1,0:T(8,128)(2,1)S(1)}, u32[]{:S(2)}, u32[]{:S(2)}) %collective-permute-start.6) | collective-permute-done | bytes 294944 | tf_op jit(solution)/shard_map/gather_authors/ppermute | solution.py:21
  25.3 3.1 %collective-permute-done.5.refs_4_ = bf16[192,768]{1,0:T(8,128)(2,1)S(1)} collective-permute-done((bf16[192,768]{1,0:T(8,128)(2,1)S(1)}, bf16[192,768]{1,0:T(8,128)(2,1)S(1)}, u32[]{:S(2)}, u32[]{:S(2)}) %collective-permute-start.5) | collective-permute-done | bytes 294944 | tf_op jit(solution)/shard_map/gather_authors/ppermute | solution.py:21
  28.4 0.1 collective-permute-start.7
  28.5 3.2 %collective-permute-start.8 = (bf16[128,768]{1,0:T(8,128)(2,1)S(1)}, bf16[128,768]{1,0:T(8,128)(2,1)S(1)}, u32[]{:S(2)}, u32[]{:S(2)}) collective-permute-start(bf16[128,768]{1,0:T(8,128)(2,1)S(1)} %slice.71), channel_id=1, source_target_pairs={{0,192},{64,0},{128,64},{192,128},{1,193},{65,1},{129,65},{193,129... | collective-permute-start | bytes 589832 | tf_op jit(solution)/shard_map/forward_authors/ppermute | solution.py:21
  31.7 3.6 %shard_map.115.refs_2_.base_ref = f32[1024,768]{1,0:T(8,128)S(1)} custom-call(s32[102]{0:T(128)S(1)} %concatenate.17.place, bf16[1024,2048]{1,0:T(8,128)(2,1)S(1)} %shard_map.113.refs_0_.tile_ref, bf16[2,768,768]{2,1,0:T(8,128)(2,1)S(1)} %copy-done.1, f32[1024,768]{1,0:T(8,128)S(1)} %shard_map.114.refs_2_, ...), custom_call_target="tpu_custom_call" | custom-call | flops 1000000000 | bytes 4194304 | tf_op jit(solution)/shard_map/pallas_call | solution.py:155
  35.4 1.8 %shard_map.116 = (bf16[4,2,64,768]{3,2,1,0:T(8,128)(2,1)S(1)}, bf16[512,768]{1,0:T(8,128)(2,1)S(1)}) custom-call(s32[102]{0:T(128)S(1)} %concatenate.17.place, bf16[1024,2048]{1,0:T(8,128)(2,1)S(1)} %shard_map.113.refs_0_.tile_ref, bf16[2,768,768]{2,1,0:T(8,128)(2,1)S(1)} %copy-done.1, f32[1024,768]{1,0:T(8,128)S(1)} %shard_map.115.refs_2_.base_ref, ...), custom_call_target="tpu_custom_call" | custom-call | flops 1000000000 | bytes 4194304 | tf_op jit(solution)/shard_map/pallas_call | solution.py:155
  37.2 0.3 collective-permute-start.9
  37.4 0.6 shard_map.117
  38.0 1.7 %collective-permute-done.9 = bf16[4,2,64,768]{3,2,1,0:T(8,128)(2,1)S(1)} collective-permute-done((bf16[4,2,64,768]{3,2,1,0:T(8,128)(2,1)S(1)}, bf16[4,2,64,768]{3,2,1,0:T(8,128)(2,1)S(1)}, u32[]{:S(2)}, u32[]{:S(2)}) %collective-permute-start.9) | collective-permute-done | bytes 786464 | tf_op jit(solution)/shard_map/sum_papers/ppermute | solution.py:25
  39.7 0.2 fusion.16
  40.0 1.6 %collective-permute-start.10 = (bf16[2,64,768]{2,1,0:T(8,128)(2,1)S(1)}, bf16[2,64,768]{2,1,0:T(8,128)(2,1)S(1)}, u32[]{:S(2)}, u32[]{:S(2)}) collective-permute-start(bf16[2,64,768]{2,1,0:T(8,128)(2,1)S(1)} %get-tuple-element.60), channel_id=1, source_target_pairs={{0,4},{4,8},{8,12},{12,0},{1,5},{5,9},{9,13},{13,1},{2,6},{6,10},{... | collective-permute-start | bytes 589832 | tf_op jit(solution)/shard_map/sum_papers/ppermute | solution.py:21
  41.6 1.8 %collective-permute-start.12 = (bf16[2,64,768]{2,1,0:T(8,128)(2,1)S(1)}, bf16[2,64,768]{2,1,0:T(8,128)(2,1)S(1)}, u32[]{:S(2)}, u32[]{:S(2)}) collective-permute-start(bf16[2,64,768]{2,1,0:T(8,128)(2,1)S(1)} %get-tuple-element.61), channel_id=1, source_target_pairs={{0,12},{4,0},{8,4},{12,8},{1,13},{5,1},{9,5},{13,9},{2,14},{6,2},{... | collective-permute-start | bytes 589832 | tf_op jit(solution)/shard_map/sum_papers/ppermute | solution.py:21
  43.3 1.8 %collective-permute-start.11 = (bf16[2,64,768]{2,1,0:T(8,128)(2,1)S(1)}, bf16[2,64,768]{2,1,0:T(8,128)(2,1)S(1)}, u32[]{:S(2)}, u32[]{:S(2)}) collective-permute-start(bf16[2,64,768]{2,1,0:T(8,128)(2,1)S(1)} %get-tuple-element.62), channel_id=1, source_target_pairs={{0,8},{4,12},{8,0},{12,4},{1,9},{5,13},{9,1},{13,5},{2,10},{6,14},... | collective-permute-start | bytes 589832 | tf_op jit(solution)/shard_map/sum_papers/ppermute | solution.py:21
  45.1 3.1 %collective-permute-done.10 = bf16[2,64,768]{2,1,0:T(8,128)(2,1)S(1)} collective-permute-done((bf16[2,64,768]{2,1,0:T(8,128)(2,1)S(1)}, bf16[2,64,768]{2,1,0:T(8,128)(2,1)S(1)}, u32[]{:S(2)}, u32[]{:S(2)}) %collective-permute-start.10) | collective-permute-done | bytes 196640 | tf_op jit(solution)/shard_map/sum_papers/ppermute | solution.py:21
  48.2 3.5 %collective-permute-done.12 = bf16[2,64,768]{2,1,0:T(8,128)(2,1)S(1)} collective-permute-done((bf16[2,64,768]{2,1,0:T(8,128)(2,1)S(1)}, bf16[2,64,768]{2,1,0:T(8,128)(2,1)S(1)}, u32[]{:S(2)}, u32[]{:S(2)}) %collective-permute-start.12) | collective-permute-done | bytes 196640 | tf_op jit(solution)/shard_map/sum_papers/ppermute | solution.py:21
  51.8 1.7 %collective-permute-done.11 = bf16[2,64,768]{2,1,0:T(8,128)(2,1)S(1)} collective-permute-done((bf16[2,64,768]{2,1,0:T(8,128)(2,1)S(1)}, bf16[2,64,768]{2,1,0:T(8,128)(2,1)S(1)}, u32[]{:S(2)}, u32[]{:S(2)}) %collective-permute-start.11) | collective-permute-done | bytes 196640 | tf_op jit(solution)/shard_map/sum_papers/ppermute | solution.py:21
  53.4 0.1 fusion.2
  53.6 0.0 copy-start.2
  53.6 2.7 %collective-permute-start.13 = (bf16[2,64,768]{2,1,0:T(8,128)(2,1)S(1)}, bf16[2,64,768]{2,1,0:T(8,128)(2,1)S(1)}, u32[]{:S(2)}, u32[]{:S(2)}) collective-permute-start(bf16[2,64,768]{2,1,0:T(8,128)(2,1)S(1)} %convert_element_type.77), channel_id=1, source_target_pairs={{0,2},{2,0},{1,3},{3,1},{4,6},{6,4},{5,7},{7,5},{8,10},{10,8},{9,1... | collective-permute-start | bytes 589832 | tf_op jit(solution)/shard_map/sum_papers/ppermute | solution.py:25
  56.4 2.2 %shard_map.118.refs_8_.tile_ref = bf16[1024,1024]{1,0:T(8,128)(2,1)S(1)} custom-call(s32[102]{0:T(128)S(1)} %concatenate.17.place, bf16[32,128,128]{2,1,0:T(8,128)(2,1)S(1)} %bitcast.60), custom_call_target="tpu_custom_call" | custom-call | flops 1000000000 | bytes 4194304 | tf_op jit(solution)/shard_map/pallas_call | solution.py:155
  58.6 2.1 %collective-permute-done.13.got_ref = bf16[2,64,768]{2,1,0:T(8,128)(2,1)S(1)} collective-permute-done((bf16[2,64,768]{2,1,0:T(8,128)(2,1)S(1)}, bf16[2,64,768]{2,1,0:T(8,128)(2,1)S(1)}, u32[]{:S(2)}, u32[]{:S(2)}) %collective-permute-start.13) | collective-permute-done | bytes 196640 | tf_op jit(solution)/shard_map/sum_papers/ppermute | solution.py:25
  60.8 0.8 shard_map.119
  61.6 1.4 %collective-permute-start.16 = (bf16[2,64,768]{2,1,0:T(8,128)(2,1)S(1)}, bf16[2,64,768]{2,1,0:T(8,128)(2,1)S(1)}, u32[]{:S(2)}, u32[]{:S(2)}) collective-permute-start(bf16[2,64,768]{2,1,0:T(8,128)(2,1)S(1)} %get-tuple-element.48.refs_0_), channel_id=1, source_target_pairs={{0,12},{4,0},{8,4},{12,8},{1,13},{5,1},{9,5},{13,9},{2,14},{6,2},{... | collective-permute-start | bytes 589832 | tf_op jit(solution)/shard_map/gather_papers/ppermute | solution.py:21
  63.0 1.5 %collective-permute-start.15 = (bf16[2,64,768]{2,1,0:T(8,128)(2,1)S(1)}, bf16[2,64,768]{2,1,0:T(8,128)(2,1)S(1)}, u32[]{:S(2)}, u32[]{:S(2)}) collective-permute-start(bf16[2,64,768]{2,1,0:T(8,128)(2,1)S(1)} %get-tuple-element.48.refs_0_), channel_id=1, source_target_pairs={{0,8},{4,12},{8,0},{12,4},{1,9},{5,13},{9,1},{13,5},{2,10},{6,14},... | collective-permute-start | bytes 589832 | tf_op jit(solution)/shard_map/gather_papers/ppermute | solution.py:21
  64.4 4.7 %collective-permute-done.16.refs_3_ = bf16[2,64,768]{2,1,0:T(8,128)(2,1)S(1)} collective-permute-done((bf16[2,64,768]{2,1,0:T(8,128)(2,1)S(1)}, bf16[2,64,768]{2,1,0:T(8,128)(2,1)S(1)}, u32[]{:S(2)}, u32[]{:S(2)}) %collective-permute-start.16) | collective-permute-done | bytes 196640 | tf_op jit(solution)/shard_map/gather_papers/ppermute | solution.py:21
  69.2 2.1 %collective-permute-done.15.refs_2_ = bf16[2,64,768]{2,1,0:T(8,128)(2,1)S(1)} collective-permute-done((bf16[2,64,768]{2,1,0:T(8,128)(2,1)S(1)}, bf16[2,64,768]{2,1,0:T(8,128)(2,1)S(1)}, u32[]{:S(2)}, u32[]{:S(2)}) %collective-permute-start.15) | collective-permute-done | bytes 196640 | tf_op jit(solution)/shard_map/gather_papers/ppermute | solution.py:21
  71.2 2.0 %collective-permute-done.14.refs_1_ = bf16[2,64,768]{2,1,0:T(8,128)(2,1)S(1)} collective-permute-done((bf16[2,64,768]{2,1,0:T(8,128)(2,1)S(1)}, bf16[2,64,768]{2,1,0:T(8,128)(2,1)S(1)}, u32[]{:S(2)}, u32[]{:S(2)}) %collective-permute-start.14) | collective-permute-done | bytes 196640 | tf_op jit(solution)/shard_map/gather_papers/ppermute | solution.py:21
  73.3 1.4 %collective-permute-done.18.refs_5_ = bf16[2,64,768]{2,1,0:T(8,128)(2,1)S(1)} collective-permute-done((bf16[2,64,768]{2,1,0:T(8,128)(2,1)S(1)}, bf16[2,64,768]{2,1,0:T(8,128)(2,1)S(1)}, u32[]{:S(2)}, u32[]{:S(2)}) %collective-permute-start.18) | collective-permute-done | bytes 196640 | tf_op jit(solution)/shard_map/gather_papers/ppermute | solution.py:25
  74.7 0.6 shard_map.120
  75.3 0.1 collective-permute-start.21
  75.4 1.4 %shard_map.121 = (f32[4,64,768]{2,1,0:T(8,128)S(1)}, f32[4,64,768]{2,1,0:T(8,128)S(1)}, f32[4,64,768]{2,1,0:T(8,128)S(1)}) custom-call(bf16[1024,768]{1,0:T(8,128)(2,1)S(1)} %get-tuple-element.50.table_ref, bf16[1024,1024]{1,0:T(8,128)(2,1)S(1)} %shard_map.118.refs_8_.tile_ref), custom_call_target="tpu_custom_call" | custom-call | flops 1000000000 | bytes 4194304 | tf_op jit(solution)/shard_map/pallas_call | solution.py:155
  76.9 3.3 %collective-permute-start.23 = (bf16[4,32,768]{2,1,0:T(8,128)(2,1)S(1)}, bf16[4,32,768]{2,1,0:T(8,128)(2,1)S(1)}, u32[]{:S(2)}, u32[]{:S(2)}) collective-permute-start(bf16[4,32,768]{2,1,0:T(8,128)(2,1)S(1)} %get-tuple-element.55), channel_id=1, source_target_pairs={{0,192},{64,0},{128,64},{192,128},{1,193},{65,1},{129,65},{193,129... | collective-permute-start | bytes 589832 | tf_op jit(solution)/shard_map/sum_authors/ppermute | solution.py:21
  80.2 3.7 %collective-permute-done.21 = bf16[4,32,768]{2,1,0:T(8,128)(2,1)S(1)} collective-permute-done((bf16[4,32,768]{2,1,0:T(8,128)(2,1)S(1)}, bf16[4,32,768]{2,1,0:T(8,128)(2,1)S(1)}, u32[]{:S(2)}, u32[]{:S(2)}) %collective-permute-start.21) | collective-permute-done | bytes 196640 | tf_op jit(solution)/shard_map/sum_authors/ppermute | solution.py:21
  83.9 0.3 collective-permute-start.25
  84.2 0.4 collective-permute-done.23
  84.7 3.8 %collective-permute-start.26 = (bf16[64,768]{1,0:T(8,128)(2,1)S(1)}, bf16[64,768]{1,0:T(8,128)(2,1)S(1)}, u32[]{:S(2)}, u32[]{:S(2)}) collective-permute-start(bf16[64,768]{1,0:T(8,128)(2,1)S(1)} %fusion.13), channel_id=1, source_target_pairs={{0,192},{64,0},{128,64},{192,128},{1,193},{65,1},{129,65},{193,129... | collective-permute-start | bytes 294920 | tf_op jit(solution)/shard_map/sum_authors/ppermute | solution.py:21
  88.5 0.6 collective-permute-start.24
  89.1 1.5 %collective-permute-start.22 = (bf16[3,64,768]{2,1,0:T(8,128)(2,1)S(1)}, bf16[3,64,768]{2,1,0:T(8,128)(2,1)S(1)}, u32[]{:S(2)}, u32[]{:S(2)}) collective-permute-start(bf16[3,64,768]{2,1,0:T(8,128)(2,1)S(1)} %fusion.4), channel_id=1, source_target_pairs={{0,64},{64,128},{128,192},{192,0},{1,65},{65,129},{129,193},{193,1... | collective-permute-start | bytes 884744 | tf_op jit(solution)/shard_map/sum_authors/ppermute | solution.py:21
  90.6 1.1 %collective-permute-done.26 = bf16[64,768]{1,0:T(8,128)(2,1)S(1)} collective-permute-done((bf16[64,768]{1,0:T(8,128)(2,1)S(1)}, bf16[64,768]{1,0:T(8,128)(2,1)S(1)}, u32[]{:S(2)}, u32[]{:S(2)}) %collective-permute-start.26) | collective-permute-done | bytes 98336 | tf_op jit(solution)/shard_map/sum_authors/ppermute | solution.py:21
  91.8 4.1 %collective-permute-start.27 = (bf16[64,768]{1,0:T(8,128)(2,1)S(1)}, bf16[64,768]{1,0:T(8,128)(2,1)S(1)}, u32[]{:S(2)}, u32[]{:S(2)}) collective-permute-start(bf16[64,768]{1,0:T(8,128)(2,1)S(1)} %fusion.12), channel_id=1, source_target_pairs={{0,32},{16,48},{32,0},{48,16},{1,33},{17,49},{33,1},{49,17},{2,34}... | collective-permute-start | bytes 294920 | tf_op jit(solution)/shard_map/sum_authors/ppermute | solution.py:21
  95.9 0.6 collective-permute-done.24
  96.5 1.3 %collective-permute-done.22 = bf16[3,64,768]{2,1,0:T(8,128)(2,1)S(1)} collective-permute-done((bf16[3,64,768]{2,1,0:T(8,128)(2,1)S(1)}, bf16[3,64,768]{2,1,0:T(8,128)(2,1)S(1)}, u32[]{:S(2)}, u32[]{:S(2)}) %collective-permute-start.22) | collective-permute-done | bytes 294944 | tf_op jit(solution)/shard_map/sum_authors/ppermute | solution.py:21
  97.8 0.1 fusion.15
  97.9 3.8 %collective-permute-start.28 = (bf16[64,768]{1,0:T(8,128)(2,1)S(1)}, bf16[64,768]{1,0:T(8,128)(2,1)S(1)}, u32[]{:S(2)}, u32[]{:S(2)}) collective-permute-start(bf16[64,768]{1,0:T(8,128)(2,1)S(1)} %get-tuple-element.63), channel_id=1, source_target_pairs={{0,16},{16,32},{32,48},{48,0},{1,17},{17,33},{33,49},{49,1},{2,18}... | collective-permute-start | bytes 294920 | tf_op jit(solution)/shard_map/sum_authors/ppermute | solution.py:21
  101.7 3.1 %collective-permute-done.28 = bf16[64,768]{1,0:T(8,128)(2,1)S(1)} collective-permute-done((bf16[64,768]{1,0:T(8,128)(2,1)S(1)}, bf16[64,768]{1,0:T(8,128)(2,1)S(1)}, u32[]{:S(2)}, u32[]{:S(2)}) %collective-permute-start.28) | collective-permute-done | bytes 98336 | tf_op jit(solution)/shard_map/sum_authors/ppermute | solution.py:21
  104.8 4.7 %collective-permute-done.29 = bf16[64,768]{1,0:T(8,128)(2,1)S(1)} collective-permute-done((bf16[64,768]{1,0:T(8,128)(2,1)S(1)}, bf16[64,768]{1,0:T(8,128)(2,1)S(1)}, u32[]{:S(2)}, u32[]{:S(2)}) %collective-permute-start.29) | collective-permute-done | bytes 98336 | tf_op jit(solution)/shard_map/sum_authors/ppermute | solution.py:21
  109.5 0.7 fusion.8
  (46 shorter events, 0.5 us)
Async XLA Ops:
  0.6 19.1 %copy-start = (bf16[768,768]{1,0:T(8,128)(2,1)S(1)}, bf16[768,768]{1,0:T(8,128)(2,1)}, u32[]{:S(2)}) copy-start(bf16[768,768]{1,0:T(8,128)(2,1)} %param.12) | copy-start | bytes 3538948
  0.6 16.9 %collective-permute-start.2 = (bf16[64,768]{1,0:T(8,128)(2,1)}, bf16[64,768]{1,0:T(8,128)(2,1)S(1)}, u32[]{:S(2)}, u32[]{:S(2)}) collective-permute-start(bf16[64,768]{1,0:T(8,128)(2,1)} %refs_2_.1), channel_id=1, source_target_pairs={{0,48},{16,0},{32,16},{48,32},{1,49},{17,1},{33,17},{49,33},{2,50}... | collective-permute-start | bytes 294920 | tf_op jit(solution)/shard_map/gather_authors/ppermute | solution.py:21
  2.1 15.4 %collective-permute-start.1 = (bf16[64,768]{1,0:T(8,128)(2,1)}, bf16[64,768]{1,0:T(8,128)(2,1)S(1)}, u32[]{:S(2)}, u32[]{:S(2)}) collective-permute-start(bf16[64,768]{1,0:T(8,128)(2,1)} %refs_2_.1), channel_id=1, source_target_pairs={{0,32},{16,48},{32,0},{48,16},{1,33},{17,49},{33,1},{49,17},{2,34}... | collective-permute-start | bytes 294920 | tf_op jit(solution)/shard_map/gather_authors/ppermute | solution.py:21
  7.6 10.0 %collective-permute-start = (bf16[64,768]{1,0:T(8,128)(2,1)}, bf16[64,768]{1,0:T(8,128)(2,1)S(1)}, u32[]{:S(2)}, u32[]{:S(2)}) collective-permute-start(bf16[64,768]{1,0:T(8,128)(2,1)} %refs_2_.1), channel_id=1, source_target_pairs={{0,16},{16,32},{32,48},{48,0},{1,17},{17,33},{33,49},{49,1},{2,18}... | collective-permute-start | bytes 294920 | tf_op jit(solution)/shard_map/gather_authors/ppermute | solution.py:21
  10.3 7.3 %collective-permute-start.3 = (bf16[64,768]{1,0:T(8,128)(2,1)}, bf16[64,768]{1,0:T(8,128)(2,1)S(1)}, u32[]{:S(2)}, u32[]{:S(2)}) collective-permute-start(bf16[64,768]{1,0:T(8,128)(2,1)} %refs_2_.1), channel_id=1, source_target_pairs={{0,64},{64,128},{128,192},{192,0},{1,65},{65,129},{129,193},{193,1... | collective-permute-start | bytes 294920 | tf_op jit(solution)/shard_map/gather_authors/ppermute | solution.py:21
  11.8 5.8 %collective-permute-start.4 = (bf16[64,768]{1,0:T(8,128)(2,1)}, bf16[64,768]{1,0:T(8,128)(2,1)S(1)}, u32[]{:S(2)}, u32[]{:S(2)}) collective-permute-start(bf16[64,768]{1,0:T(8,128)(2,1)} %refs_2_.1), channel_id=1, source_target_pairs={{0,192},{64,0},{128,64},{192,128},{1,193},{65,1},{129,65},{193,129... | collective-permute-start | bytes 294920 | tf_op jit(solution)/shard_map/gather_authors/ppermute | solution.py:21
  14.9 1.2 %copy-start.3 = (bf16[1,1,32,128,128]{4,3,2,1,0:T(8,128)(2,1)S(1)}, bf16[1,1,32,128,128]{4,3,2,1,0:T(8,128)(2,1)}, u32[]{:S(2)}) copy-start(bf16[1,1,32,128,128]{4,3,2,1,0:T(8,128)(2,1)} %param.19) | copy-start | bytes 3145732
  16.1 3.6 %copy-start.6 = (bf16[64,768]{1,0:T(8,128)(2,1)S(1)}, bf16[64,768]{1,0:T(8,128)(2,1)}, u32[]{:S(2)}) copy-start(bf16[64,768]{1,0:T(8,128)(2,1)} %param.10) | copy-start | bytes 294916
  16.1 4.0 %copy-start.1 = (bf16[2,768,768]{2,1,0:T(8,128)(2,1)S(1)}, bf16[2,768,768]{2,1,0:T(8,128)(2,1)}, u32[]{:S(2)}) copy-start(bf16[2,768,768]{2,1,0:T(8,128)(2,1)} %refs_1_.5) | copy-start | bytes 7077892
  17.5 2.6 %copy-start.5 = (bf16[64,768]{1,0:T(8,128)(2,1)S(1)}, bf16[64,768]{1,0:T(8,128)(2,1)}, u32[]{:S(2)}) copy-start(bf16[64,768]{1,0:T(8,128)(2,1)} %refs_2_.1) | copy-start | bytes 294916
  17.7 7.6 %collective-permute-start.6 = (bf16[192,768]{1,0:T(8,128)(2,1)S(1)}, bf16[192,768]{1,0:T(8,128)(2,1)S(1)}, u32[]{:S(2)}, u32[]{:S(2)}) collective-permute-start(bf16[192,768]{1,0:T(8,128)(2,1)S(1)} %constant_dynamic-update-slice_fusion), channel_id=1, source_target_pairs={{0,192},{64,0},{128,64},{192,128},{1,193},{65,1},{129,65},{193,129... | collective-permute-start | bytes 884744 | tf_op jit(solution)/shard_map/gather_authors/ppermute | solution.py:21
  19.6 8.7 %collective-permute-start.5 = (bf16[192,768]{1,0:T(8,128)(2,1)S(1)}, bf16[192,768]{1,0:T(8,128)(2,1)S(1)}, u32[]{:S(2)}, u32[]{:S(2)}) collective-permute-start(bf16[192,768]{1,0:T(8,128)(2,1)S(1)} %constant_dynamic-update-slice_fusion), channel_id=1, source_target_pairs={{0,64},{64,128},{128,192},{192,0},{1,65},{65,129},{129,193},{193,1... | collective-permute-start | bytes 884744 | tf_op jit(solution)/shard_map/gather_authors/ppermute | solution.py:21
  28.4 7.0 %collective-permute-start.7 = (bf16[128,768]{1,0:T(8,128)(2,1)S(1)}, bf16[128,768]{1,0:T(8,128)(2,1)S(1)}, u32[]{:S(2)}, u32[]{:S(2)}) collective-permute-start(bf16[128,768]{1,0:T(8,128)(2,1)S(1)} %pad_maximum_fusion.1), channel_id=1, source_target_pairs={{0,64},{64,128},{128,192},{192,0},{1,65},{65,129},{129,193},{193,1... | collective-permute-start | bytes 589832 | tf_op jit(solution)/shard_map/forward_authors/ppermute | solution.py:21
  28.5 6.9 %collective-permute-start.8 = (bf16[128,768]{1,0:T(8,128)(2,1)S(1)}, bf16[128,768]{1,0:T(8,128)(2,1)S(1)}, u32[]{:S(2)}, u32[]{:S(2)}) collective-permute-start(bf16[128,768]{1,0:T(8,128)(2,1)S(1)} %slice.71), channel_id=1, source_target_pairs={{0,192},{64,0},{128,64},{192,128},{1,193},{65,1},{129,65},{193,129... | collective-permute-start | bytes 589832 | tf_op jit(solution)/shard_map/forward_authors/ppermute | solution.py:21
  37.2 2.6 %collective-permute-start.9 = (bf16[4,2,64,768]{3,2,1,0:T(8,128)(2,1)S(1)}, bf16[4,2,64,768]{3,2,1,0:T(8,128)(2,1)S(1)}, u32[]{:S(2)}, u32[]{:S(2)}) collective-permute-start(bf16[4,2,64,768]{3,2,1,0:T(8,128)(2,1)S(1)} %get-tuple-element.42), channel_id=1, source_target_pairs={{0,1},{1,0},{2,3},{3,2},{4,5},{5,4},{6,7},{7,6},{8,9},{9,8},{10,11... | collective-permute-start | bytes 2359304 | tf_op jit(solution)/shard_map/sum_papers/ppermute | solution.py:25
  40.0 8.2 %collective-permute-start.10 = (bf16[2,64,768]{2,1,0:T(8,128)(2,1)S(1)}, bf16[2,64,768]{2,1,0:T(8,128)(2,1)S(1)}, u32[]{:S(2)}, u32[]{:S(2)}) collective-permute-start(bf16[2,64,768]{2,1,0:T(8,128)(2,1)S(1)} %get-tuple-element.60), channel_id=1, source_target_pairs={{0,4},{4,8},{8,12},{12,0},{1,5},{5,9},{9,13},{13,1},{2,6},{6,10},{... | collective-permute-start | bytes 589832 | tf_op jit(solution)/shard_map/sum_papers/ppermute | solution.py:21
  41.6 10.2 %collective-permute-start.12 = (bf16[2,64,768]{2,1,0:T(8,128)(2,1)S(1)}, bf16[2,64,768]{2,1,0:T(8,128)(2,1)S(1)}, u32[]{:S(2)}, u32[]{:S(2)}) collective-permute-start(bf16[2,64,768]{2,1,0:T(8,128)(2,1)S(1)} %get-tuple-element.61), channel_id=1, source_target_pairs={{0,12},{4,0},{8,4},{12,8},{1,13},{5,1},{9,5},{13,9},{2,14},{6,2},{... | collective-permute-start | bytes 589832 | tf_op jit(solution)/shard_map/sum_papers/ppermute | solution.py:21
  43.3 10.1 %collective-permute-start.11 = (bf16[2,64,768]{2,1,0:T(8,128)(2,1)S(1)}, bf16[2,64,768]{2,1,0:T(8,128)(2,1)S(1)}, u32[]{:S(2)}, u32[]{:S(2)}) collective-permute-start(bf16[2,64,768]{2,1,0:T(8,128)(2,1)S(1)} %get-tuple-element.62), channel_id=1, source_target_pairs={{0,8},{4,12},{8,0},{12,4},{1,9},{5,13},{9,1},{13,5},{2,10},{6,14},... | collective-permute-start | bytes 589832 | tf_op jit(solution)/shard_map/sum_papers/ppermute | solution.py:21
  53.4 2.9 %copy-start.4 = (bf16[1,1,32,128,128]{4,3,2,1,0:T(8,128)(2,1)S(1)}, bf16[1,1,32,128,128]{4,3,2,1,0:T(8,128)(2,1)}, u32[]{:S(2)}) copy-start(bf16[1,1,32,128,128]{4,3,2,1,0:T(8,128)(2,1)} %param.19) | copy-start | bytes 3145732
  53.6 7.1 %copy-start.2 = (bf16[768,768]{1,0:T(8,128)(2,1)S(1)}, bf16[768,768]{1,0:T(8,128)(2,1)}, u32[]{:S(2)}) copy-start(bf16[768,768]{1,0:T(8,128)(2,1)} %w_ref.1) | copy-start | bytes 3538948
  53.6 7.1 %collective-permute-start.13 = (bf16[2,64,768]{2,1,0:T(8,128)(2,1)S(1)}, bf16[2,64,768]{2,1,0:T(8,128)(2,1)S(1)}, u32[]{:S(2)}, u32[]{:S(2)}) collective-permute-start(bf16[2,64,768]{2,1,0:T(8,128)(2,1)S(1)} %convert_element_type.77), channel_id=1, source_target_pairs={{0,2},{2,0},{1,3},{3,1},{4,6},{6,4},{5,7},{7,5},{8,10},{10,8},{9,1... | collective-permute-start | bytes 589832 | tf_op jit(solution)/shard_map/sum_papers/ppermute | solution.py:25
  61.6 7.6 %collective-permute-start.16 = (bf16[2,64,768]{2,1,0:T(8,128)(2,1)S(1)}, bf16[2,64,768]{2,1,0:T(8,128)(2,1)S(1)}, u32[]{:S(2)}, u32[]{:S(2)}) collective-permute-start(bf16[2,64,768]{2,1,0:T(8,128)(2,1)S(1)} %get-tuple-element.48.refs_0_), channel_id=1, source_target_pairs={{0,12},{4,0},{8,4},{12,8},{1,13},{5,1},{9,5},{13,9},{2,14},{6,2},{... | collective-permute-start | bytes 589832 | tf_op jit(solution)/shard_map/gather_papers/ppermute | solution.py:21
  63.0 8.3 %collective-permute-start.15 = (bf16[2,64,768]{2,1,0:T(8,128)(2,1)S(1)}, bf16[2,64,768]{2,1,0:T(8,128)(2,1)S(1)}, u32[]{:S(2)}, u32[]{:S(2)}) collective-permute-start(bf16[2,64,768]{2,1,0:T(8,128)(2,1)S(1)} %get-tuple-element.48.refs_0_), channel_id=1, source_target_pairs={{0,8},{4,12},{8,0},{12,4},{1,9},{5,13},{9,1},{13,5},{2,10},{6,14},... | collective-permute-start | bytes 589832 | tf_op jit(solution)/shard_map/gather_papers/ppermute | solution.py:21
  64.4 8.9 %collective-permute-start.14 = (bf16[2,64,768]{2,1,0:T(8,128)(2,1)S(1)}, bf16[2,64,768]{2,1,0:T(8,128)(2,1)S(1)}, u32[]{:S(2)}, u32[]{:S(2)}) collective-permute-start(bf16[2,64,768]{2,1,0:T(8,128)(2,1)S(1)} %get-tuple-element.48.refs_0_), channel_id=1, source_target_pairs={{0,4},{4,8},{8,12},{12,0},{1,5},{5,9},{9,13},{13,1},{2,6},{6,10},{... | collective-permute-start | bytes 589832 | tf_op jit(solution)/shard_map/gather_papers/ppermute | solution.py:21
  64.4 8.9 %collective-permute-start.17 = (bf16[2,64,768]{2,1,0:T(8,128)(2,1)S(1)}, bf16[2,64,768]{2,1,0:T(8,128)(2,1)S(1)}, u32[]{:S(2)}, u32[]{:S(2)}) collective-permute-start(bf16[2,64,768]{2,1,0:T(8,128)(2,1)S(1)} %get-tuple-element.48.refs_0_), channel_id=1, source_target_pairs={{0,1},{1,0},{2,3},{3,2},{4,5},{5,4},{6,7},{7,6},{8,9},{9,8},{10,11... | collective-permute-start | bytes 589832 | tf_op jit(solution)/shard_map/gather_papers/ppermute | solution.py:25
  69.2 4.1 %collective-permute-start.20 = (bf16[2,64,768]{2,1,0:T(8,128)(2,1)S(1)}, bf16[2,64,768]{2,1,0:T(8,128)(2,1)S(1)}, u32[]{:S(2)}, u32[]{:S(2)}) collective-permute-start(bf16[2,64,768]{2,1,0:T(8,128)(2,1)S(1)} %collective-permute-done.16.refs_3_), channel_id=1, source_target_pairs={{0,1},{1,0},{2,3},{3,2},{4,5},{5,4},{6,7},{7,6},{8,9},{9,8},{10,11... | collective-permute-start | bytes 589832 | tf_op jit(solution)/shard_map/gather_papers/ppermute | solution.py:25
  71.2 2.1 %collective-permute-start.19 = (bf16[2,64,768]{2,1,0:T(8,128)(2,1)S(1)}, bf16[2,64,768]{2,1,0:T(8,128)(2,1)S(1)}, u32[]{:S(2)}, u32[]{:S(2)}) collective-permute-start(bf16[2,64,768]{2,1,0:T(8,128)(2,1)S(1)} %collective-permute-done.15.refs_2_), channel_id=1, source_target_pairs={{0,1},{1,0},{2,3},{3,2},{4,5},{5,4},{6,7},{7,6},{8,9},{9,8},{10,11... | collective-permute-start | bytes 589832 | tf_op jit(solution)/shard_map/gather_papers/ppermute | solution.py:25
  73.3 1.4 %collective-permute-start.18 = (bf16[2,64,768]{2,1,0:T(8,128)(2,1)S(1)}, bf16[2,64,768]{2,1,0:T(8,128)(2,1)S(1)}, u32[]{:S(2)}, u32[]{:S(2)}) collective-permute-start(bf16[2,64,768]{2,1,0:T(8,128)(2,1)S(1)} %collective-permute-done.14.refs_1_), channel_id=1, source_target_pairs={{0,1},{1,0},{2,3},{3,2},{4,5},{5,4},{6,7},{7,6},{8,9},{9,8},{10,11... | collective-permute-start | bytes 589832 | tf_op jit(solution)/shard_map/gather_papers/ppermute | solution.py:25
  75.3 8.5 %collective-permute-start.21 = (bf16[4,32,768]{2,1,0:T(8,128)(2,1)S(1)}, bf16[4,32,768]{2,1,0:T(8,128)(2,1)S(1)}, u32[]{:S(2)}, u32[]{:S(2)}) collective-permute-start(bf16[4,32,768]{2,1,0:T(8,128)(2,1)S(1)} %get-tuple-element.53), channel_id=1, source_target_pairs={{0,64},{64,128},{128,192},{192,0},{1,65},{65,129},{129,193},{193,1... | collective-permute-start | bytes 589832 | tf_op jit(solution)/shard_map/sum_authors/ppermute | solution.py:21
  76.9 7.8 %collective-permute-start.23 = (bf16[4,32,768]{2,1,0:T(8,128)(2,1)S(1)}, bf16[4,32,768]{2,1,0:T(8,128)(2,1)S(1)}, u32[]{:S(2)}, u32[]{:S(2)}) collective-permute-start(bf16[4,32,768]{2,1,0:T(8,128)(2,1)S(1)} %get-tuple-element.55), channel_id=1, source_target_pairs={{0,192},{64,0},{128,64},{192,128},{1,193},{65,1},{129,65},{193,129... | collective-permute-start | bytes 589832 | tf_op jit(solution)/shard_map/sum_authors/ppermute | solution.py:21
  83.9 6.7 %collective-permute-start.25 = (bf16[64,768]{1,0:T(8,128)(2,1)S(1)}, bf16[64,768]{1,0:T(8,128)(2,1)S(1)}, u32[]{:S(2)}, u32[]{:S(2)}) collective-permute-start(bf16[64,768]{1,0:T(8,128)(2,1)S(1)} %fusion.14), channel_id=1, source_target_pairs={{0,64},{64,128},{128,192},{192,0},{1,65},{65,129},{129,193},{193,1... | collective-permute-start | bytes 294920 | tf_op jit(solution)/shard_map/sum_authors/ppermute | solution.py:21
  84.7 7.0 %collective-permute-start.26 = (bf16[64,768]{1,0:T(8,128)(2,1)S(1)}, bf16[64,768]{1,0:T(8,128)(2,1)S(1)}, u32[]{:S(2)}, u32[]{:S(2)}) collective-permute-start(bf16[64,768]{1,0:T(8,128)(2,1)S(1)} %fusion.13), channel_id=1, source_target_pairs={{0,192},{64,0},{128,64},{192,128},{1,193},{65,1},{129,65},{193,129... | collective-permute-start | bytes 294920 | tf_op jit(solution)/shard_map/sum_authors/ppermute | solution.py:21
  88.5 8.0 %collective-permute-start.24 = (bf16[3,64,768]{2,1,0:T(8,128)(2,1)S(1)}, bf16[3,64,768]{2,1,0:T(8,128)(2,1)S(1)}, u32[]{:S(2)}, u32[]{:S(2)}) collective-permute-start(bf16[3,64,768]{2,1,0:T(8,128)(2,1)S(1)} %fusion.3), channel_id=1, source_target_pairs={{0,192},{64,0},{128,64},{192,128},{1,193},{65,1},{129,65},{193,129... | collective-permute-start | bytes 884744 | tf_op jit(solution)/shard_map/sum_authors/ppermute | solution.py:21
  89.1 8.7 %collective-permute-start.22 = (bf16[3,64,768]{2,1,0:T(8,128)(2,1)S(1)}, bf16[3,64,768]{2,1,0:T(8,128)(2,1)S(1)}, u32[]{:S(2)}, u32[]{:S(2)}) collective-permute-start(bf16[3,64,768]{2,1,0:T(8,128)(2,1)S(1)} %fusion.4), channel_id=1, source_target_pairs={{0,64},{64,128},{128,192},{192,0},{1,65},{65,129},{129,193},{193,1... | collective-permute-start | bytes 884744 | tf_op jit(solution)/shard_map/sum_authors/ppermute | solution.py:21
  91.8 9.9 %collective-permute-start.27 = (bf16[64,768]{1,0:T(8,128)(2,1)S(1)}, bf16[64,768]{1,0:T(8,128)(2,1)S(1)}, u32[]{:S(2)}, u32[]{:S(2)}) collective-permute-start(bf16[64,768]{1,0:T(8,128)(2,1)S(1)} %fusion.12), channel_id=1, source_target_pairs={{0,32},{16,48},{32,0},{48,16},{1,33},{17,49},{33,1},{49,17},{2,34}... | collective-permute-start | bytes 294920 | tf_op jit(solution)/shard_map/sum_authors/ppermute | solution.py:21
  97.9 6.9 %collective-permute-start.28 = (bf16[64,768]{1,0:T(8,128)(2,1)S(1)}, bf16[64,768]{1,0:T(8,128)(2,1)S(1)}, u32[]{:S(2)}, u32[]{:S(2)}) collective-permute-start(bf16[64,768]{1,0:T(8,128)(2,1)S(1)} %get-tuple-element.63), channel_id=1, source_target_pairs={{0,16},{16,32},{32,48},{48,0},{1,17},{17,33},{33,49},{49,1},{2,18}... | collective-permute-start | bytes 294920 | tf_op jit(solution)/shard_map/sum_authors/ppermute | solution.py:21
  101.7 7.8 %collective-permute-start.29 = (bf16[64,768]{1,0:T(8,128)(2,1)S(1)}, bf16[64,768]{1,0:T(8,128)(2,1)S(1)}, u32[]{:S(2)}, u32[]{:S(2)}) collective-permute-start(bf16[64,768]{1,0:T(8,128)(2,1)S(1)} %get-tuple-element.64), channel_id=1, source_target_pairs={{0,48},{16,0},{32,16},{48,32},{1,49},{17,1},{33,17},{49,33},{2,50}... | collective-permute-start | bytes 294920 | tf_op jit(solution)/shard_map/sum_authors/ppermute | solution.py:21

commit v6 on v5

--- a/solution.py
+++ b/solution.py
@@ -207,12 +207,13 @@
         relay = jnp.concatenate(by_z)
         ups, downs = shift(relay, "y", 1), shift(relay, "y", RING - 1)
     base = part(0, 1, [[(0, e)] for e in range(RING)], (author_x, *by_z), None, base_shape)
+    split = [[(0, 0)], [(0, e) for e in range(1, RING)]]
+    base = part(1, 1, split, (own_up, ups), base, base_shape)
     with jax.named_scope("forward_authors"):
         ups, downs, base, self_term = lax.optimization_barrier((ups, downs, base, self_term))
         up_two = shift(jnp.concatenate([own_up, ups[:own]]), "y", 1)
         down_two = shift(downs[own:], "y", RING - 1)
-    split = [es for g in range(2) for es in ([(g, 0)], [(g, e) for e in range(1, RING)])]
-    base = part(1, 2, split, (own_up, ups, own_down, downs), base, base_shape)
+    base = part(2, 1, split, (own_down, downs), base, base_shape)
     send, msgs = part(
         3,
         1,

time: 110 us -> 112 us (1.018)
  waiting for transfers between devices: 43.3 us -> 40.1 us
  starting transfers between devices: 46.7 us -> 49.5 us
  Pallas kernels: 14.6 us -> 16.3 us
    ppermute x24, starting transfers between devices: 43.7 us -> 48.8 us  [shift(): lax.ppermute(value, axis, [(i, (i + by) % RING) for i in range(RING)])]
    ppermute x24, waiting for transfers between devices: 38 us -> 34 us  [shift(): lax.ppermute(value, axis, [(i, (i + by) % RING) for i in range(RING)])]
    ppermute x6, starting transfers between devices: 3.01 us -> 0.7 us  [swap(): return lax.ppermute(value, axis, [(0, 1), (1, 0)])]
    pallas_call x9 -> x10, Pallas kernels: 14.6 us -> 16.3 us  [call(): pl.pallas_call(kernel, out_shape=out_shape, in_specs=[spec(pltpu.SMEM)] *...]
  transfers between devices with their start and end apart: 30 -> 30, of which waited for: 18 -> 16; matrix products, arithmetic and copies ran while one was open for 1% -> 1% of each run, Pallas kernels for 10% -> 12%
where the time goes in v6:
time: 112 us; the launch traced here: 111 us
  starting transfers between devices  49.5 us (44%)
  waiting for transfers between devices  40.1 us (36%)
  Pallas kernels  16.3 us (15%)
  local copies, waits for them, and re-layouts  2.19 us (2%)
  between operations  1.62 us (1%)
  other arithmetic  1.35 us (1%)
    ppermute x24, starting transfers between devices, shift(): lax.ppermute(value, axis, [(i, (i + by) % RING) for i in range(RING)])  48.8 us
    ppermute x24, waiting for transfers between devices, shift(): lax.ppermute(value, axis, [(i, (i + by) % RING) for i in range(RING)])  34 us
    pallas_call x10, Pallas kernels, call(): pl.pallas_call(kernel, out_shape=out_shape, in_specs=[spec(pltpu.SMEM)] *...  16.3 us
    ppermute x6, waiting for transfers between devices, swap(): return lax.ppermute(value, axis, [(0, 1), (1, 0)])  6.13 us
  transfers between devices with their start and end apart: 30, of which 16 were waited for; matrix products, arithmetic and copies ran while one was open for 1% of the time, Pallas kernels for 12%

profile of v6, /device:TPU:64, one launch (start us, length us, event | category | flops | bytes accessed | tf_op | source)
XLA Modules:
  0.0 111.4 jit_solution(17766111488205021718)
XLA Ops:
  0.6 0.0 copy-start
  0.6 4.6 %collective-permute-start = (bf16[64,768]{1,0:T(8,128)(2,1)}, bf16[64,768]{1,0:T(8,128)(2,1)S(1)}, u32[]{:S(2)}, u32[]{:S(2)}) collective-permute-start(bf16[64,768]{1,0:T(8,128)(2,1)} %refs_2_.1), channel_id=1, source_target_pairs={{0,16},{16,32},{32,48},{48,0},{1,17},{17,33},{33,49},{49,1},{2,18}... | collective-permute-start | bytes 294920 | tf_op jit(solution)/shard_map/gather_authors/ppermute | solution.py:21
  5.2 1.0 collective-permute-start.1
  6.2 2.8 %collective-permute-start.2 = (bf16[64,768]{1,0:T(8,128)(2,1)}, bf16[64,768]{1,0:T(8,128)(2,1)S(1)}, u32[]{:S(2)}, u32[]{:S(2)}) collective-permute-start(bf16[64,768]{1,0:T(8,128)(2,1)} %refs_2_.1), channel_id=1, source_target_pairs={{0,48},{16,0},{32,16},{48,32},{1,49},{17,1},{33,17},{49,33},{2,50}... | collective-permute-start | bytes 294920 | tf_op jit(solution)/shard_map/gather_authors/ppermute | solution.py:21
  9.0 1.6 %collective-permute-start.3 = (bf16[64,768]{1,0:T(8,128)(2,1)}, bf16[64,768]{1,0:T(8,128)(2,1)S(1)}, u32[]{:S(2)}, u32[]{:S(2)}) collective-permute-start(bf16[64,768]{1,0:T(8,128)(2,1)} %refs_2_.1), channel_id=1, source_target_pairs={{0,64},{64,128},{128,192},{192,0},{1,65},{65,129},{129,193},{193,1... | collective-permute-start | bytes 294920 | tf_op jit(solution)/shard_map/gather_authors/ppermute | solution.py:21
  10.6 1.7 %collective-permute-start.4 = (bf16[64,768]{1,0:T(8,128)(2,1)}, bf16[64,768]{1,0:T(8,128)(2,1)S(1)}, u32[]{:S(2)}, u32[]{:S(2)}) collective-permute-start(bf16[64,768]{1,0:T(8,128)(2,1)} %refs_2_.1), channel_id=1, source_target_pairs={{0,192},{64,0},{128,64},{192,128},{1,193},{65,1},{129,65},{193,129... | collective-permute-start | bytes 294920 | tf_op jit(solution)/shard_map/gather_authors/ppermute | solution.py:21
  12.9 0.8 concatenate.17.place
  13.7 1.2 %copy-done.3 = bf16[1,1,32,128,128]{4,3,2,1,0:T(8,128)(2,1)S(1)} copy-done((bf16[1,1,32,128,128]{4,3,2,1,0:T(8,128)(2,1)S(1)}, bf16[1,1,32,128,128]{4,3,2,1,0:T(8,128)(2,1)}, u32[]{:S(2)}) %copy-start.3) | copy-done | bytes 1048600
  14.9 1.6 %shard_map.113.refs_0_.tile_ref = bf16[1024,2048]{1,0:T(8,128)(2,1)S(1)} custom-call(s32[102]{0:T(128)S(1)} %concatenate.17.place, bf16[32,128,128]{2,1,0:T(8,128)(2,1)S(1)} %bitcast.59), custom_call_target="tpu_custom_call" | custom-call | flops 1000000000 | bytes 4194304 | tf_op jit(solution)/shard_map/pallas_call | solution.py:155
  16.6 0.0 copy-start.4
  16.6 0.0 collective-permute-done.1.refs_4_
  16.6 0.8 collective-permute-done.2.refs_5_
  17.4 1.7 %collective-permute-start.5 = (bf16[192,768]{1,0:T(8,128)(2,1)S(1)}, bf16[192,768]{1,0:T(8,128)(2,1)S(1)}, u32[]{:S(2)}, u32[]{:S(2)}) collective-permute-start(bf16[192,768]{1,0:T(8,128)(2,1)S(1)} %constant_dynamic-update-slice_fusion), channel_id=1, source_target_pairs={{0,64},{64,128},{128,192},{192,0},{1,65},{65,129},{129,193},{193,1... | collective-permute-start | bytes 884744 | tf_op jit(solution)/shard_map/gather_authors/ppermute | solution.py:21
  19.1 1.7 %collective-permute-start.6 = (bf16[192,768]{1,0:T(8,128)(2,1)S(1)}, bf16[192,768]{1,0:T(8,128)(2,1)S(1)}, u32[]{:S(2)}, u32[]{:S(2)}) collective-permute-start(bf16[192,768]{1,0:T(8,128)(2,1)S(1)} %constant_dynamic-update-slice_fusion), channel_id=1, source_target_pairs={{0,192},{64,0},{128,64},{192,128},{1,193},{65,1},{129,65},{193,129... | collective-permute-start | bytes 884744 | tf_op jit(solution)/shard_map/gather_authors/ppermute | solution.py:21
  20.7 0.3 fusion.17
  21.1 0.0 copy-done.1
  21.1 2.2 %shard_map.114.refs_2_ = f32[1024,768]{1,0:T(8,128)S(1)} custom-call(s32[102]{0:T(128)S(1)} %concatenate.17.place, bf16[1024,2048]{1,0:T(8,128)(2,1)S(1)} %shard_map.113.refs_0_.tile_ref, bf16[2,768,768]{2,1,0:T(8,128)(2,1)S(1)} %copy-done.1, bf16[64,768]{1,0:T(8,128)(2,1)S(1)} %copy-done.4, bf16[64,768]{1,0:T(8,128)(2,1)S(1)} %collective-permute-done.refs_3_, ...), custom_call_target="tpu_custom_call" | custom-call | flops 1000000000 | bytes 4194304 | tf_op jit(solution)/shard_map/pallas_call | solution.py:155
  23.3 3.8 %collective-permute-done.5.refs_4_ = bf16[192,768]{1,0:T(8,128)(2,1)S(1)} collective-permute-done((bf16[192,768]{1,0:T(8,128)(2,1)S(1)}, bf16[192,768]{1,0:T(8,128)(2,1)S(1)}, u32[]{:S(2)}, u32[]{:S(2)}) %collective-permute-start.5) | collective-permute-done | bytes 294944 | tf_op jit(solution)/shard_map/gather_authors/ppermute | solution.py:21
  27.1 2.2 %shard_map.115.refs_2_ = f32[1024,768]{1,0:T(8,128)S(1)} custom-call(s32[102]{0:T(128)S(1)} %concatenate.17.place, bf16[1024,2048]{1,0:T(8,128)(2,1)S(1)} %shard_map.113.refs_0_.tile_ref, bf16[2,768,768]{2,1,0:T(8,128)(2,1)S(1)} %copy-done.1, f32[1024,768]{1,0:T(8,128)S(1)} %shard_map.114.refs_2_, bf16[64,768]{1,0:T(8,128)(2,1)S(1)} %collective-permute-done.3.refs_3_, ...), custom_call_target="tpu_custom_call" | custom-call | flops 1000000000 | bytes 4194304 | tf_op jit(solution)/shard_map/pallas_call | solution.py:155
  29.4 0.4 collective-permute-start.7
  29.8 3.2 %collective-permute-start.8 = (bf16[128,768]{1,0:T(8,128)(2,1)S(1)}, bf16[128,768]{1,0:T(8,128)(2,1)S(1)}, u32[]{:S(2)}, u32[]{:S(2)}) collective-permute-start(bf16[128,768]{1,0:T(8,128)(2,1)S(1)} %slice.71), channel_id=1, source_target_pairs={{0,192},{64,0},{128,64},{192,128},{1,193},{65,1},{129,65},{193,129... | collective-permute-start | bytes 589832 | tf_op jit(solution)/shard_map/forward_authors/ppermute | solution.py:21
  33.0 2.2 %shard_map.116.refs_2_.base_ref = f32[1024,768]{1,0:T(8,128)S(1)} custom-call(s32[102]{0:T(128)S(1)} %concatenate.17.place, bf16[1024,2048]{1,0:T(8,128)(2,1)S(1)} %shard_map.113.refs_0_.tile_ref, bf16[2,768,768]{2,1,0:T(8,128)(2,1)S(1)} %copy-done.1, f32[1024,768]{1,0:T(8,128)S(1)} %shard_map.115.refs_2_, ...), custom_call_target="tpu_custom_call" | custom-call | flops 1000000000 | bytes 4194304 | tf_op jit(solution)/shard_map/pallas_call | solution.py:155
  35.3 1.1 %collective-permute-done.7.refs_3_ = bf16[128,768]{1,0:T(8,128)(2,1)S(1)} collective-permute-done((bf16[128,768]{1,0:T(8,128)(2,1)S(1)}, bf16[128,768]{1,0:T(8,128)(2,1)S(1)}, u32[]{:S(2)}, u32[]{:S(2)}) %collective-permute-start.7) | collective-permute-done | bytes 196640 | tf_op jit(solution)/shard_map/forward_authors/ppermute | solution.py:21
  36.4 1.8 %shard_map.117 = (bf16[4,2,64,768]{3,2,1,0:T(8,128)(2,1)S(1)}, bf16[512,768]{1,0:T(8,128)(2,1)S(1)}) custom-call(s32[102]{0:T(128)S(1)} %concatenate.17.place, bf16[1024,2048]{1,0:T(8,128)(2,1)S(1)} %shard_map.113.refs_0_.tile_ref, bf16[2,768,768]{2,1,0:T(8,128)(2,1)S(1)} %copy-done.1, f32[1024,768]{1,0:T(8,128)S(1)} %shard_map.116.refs_2_.base_ref, ...), custom_call_target="tpu_custom_call" | custom-call | flops 1000000000 | bytes 4194304 | tf_op jit(solution)/shard_map/pallas_call | solution.py:155
  38.2 0.1 collective-permute-start.9
  38.3 0.6 shard_map.118
  38.9 1.7 %collective-permute-done.9 = bf16[4,2,64,768]{3,2,1,0:T(8,128)(2,1)S(1)} collective-permute-done((bf16[4,2,64,768]{3,2,1,0:T(8,128)(2,1)S(1)}, bf16[4,2,64,768]{3,2,1,0:T(8,128)(2,1)S(1)}, u32[]{:S(2)}, u32[]{:S(2)}) %collective-permute-start.9) | collective-permute-done | bytes 786464 | tf_op jit(solution)/shard_map/sum_papers/ppermute | solution.py:25
  40.5 0.2 fusion.16
  40.8 1.6 %collective-permute-start.10 = (bf16[2,64,768]{2,1,0:T(8,128)(2,1)S(1)}, bf16[2,64,768]{2,1,0:T(8,128)(2,1)S(1)}, u32[]{:S(2)}, u32[]{:S(2)}) collective-permute-start(bf16[2,64,768]{2,1,0:T(8,128)(2,1)S(1)} %get-tuple-element.60), channel_id=1, source_target_pairs={{0,4},{4,8},{8,12},{12,0},{1,5},{5,9},{9,13},{13,1},{2,6},{6,10},{... | collective-permute-start | bytes 589832 | tf_op jit(solution)/shard_map/sum_papers/ppermute | solution.py:21
  42.4 2.7 %collective-permute-start.11 = (bf16[2,64,768]{2,1,0:T(8,128)(2,1)S(1)}, bf16[2,64,768]{2,1,0:T(8,128)(2,1)S(1)}, u32[]{:S(2)}, u32[]{:S(2)}) collective-permute-start(bf16[2,64,768]{2,1,0:T(8,128)(2,1)S(1)} %get-tuple-element.62), channel_id=1, source_target_pairs={{0,8},{4,12},{8,0},{12,4},{1,9},{5,13},{9,1},{13,5},{2,10},{6,14},... | collective-permute-start | bytes 589832 | tf_op jit(solution)/shard_map/sum_papers/ppermute | solution.py:21
  45.1 1.4 %collective-permute-start.12 = (bf16[2,64,768]{2,1,0:T(8,128)(2,1)S(1)}, bf16[2,64,768]{2,1,0:T(8,128)(2,1)S(1)}, u32[]{:S(2)}, u32[]{:S(2)}) collective-permute-start(bf16[2,64,768]{2,1,0:T(8,128)(2,1)S(1)} %get-tuple-element.61), channel_id=1, source_target_pairs={{0,12},{4,0},{8,4},{12,8},{1,13},{5,1},{9,5},{13,9},{2,14},{6,2},{... | collective-permute-start | bytes 589832 | tf_op jit(solution)/shard_map/sum_papers/ppermute | solution.py:21
  46.5 2.5 %collective-permute-done.10 = bf16[2,64,768]{2,1,0:T(8,128)(2,1)S(1)} collective-permute-done((bf16[2,64,768]{2,1,0:T(8,128)(2,1)S(1)}, bf16[2,64,768]{2,1,0:T(8,128)(2,1)S(1)}, u32[]{:S(2)}, u32[]{:S(2)}) %collective-permute-start.10) | collective-permute-done | bytes 196640 | tf_op jit(solution)/shard_map/sum_papers/ppermute | solution.py:21
  49.0 5.2 %collective-permute-done.11 = bf16[2,64,768]{2,1,0:T(8,128)(2,1)S(1)} collective-permute-done((bf16[2,64,768]{2,1,0:T(8,128)(2,1)S(1)}, bf16[2,64,768]{2,1,0:T(8,128)(2,1)S(1)}, u32[]{:S(2)}, u32[]{:S(2)}) %collective-permute-start.11) | collective-permute-done | bytes 196640 | tf_op jit(solution)/shard_map/sum_papers/ppermute | solution.py:21
  54.2 0.1 fusion.2
  54.5 0.0 copy-start.2
  54.5 0.1 collective-permute-start.13
  54.6 2.9 %shard_map.119.refs_8_.tile_ref = bf16[1024,1024]{1,0:T(8,128)(2,1)S(1)} custom-call(s32[102]{0:T(128)S(1)} %concatenate.17.place, bf16[32,128,128]{2,1,0:T(8,128)(2,1)S(1)} %bitcast.60), custom_call_target="tpu_custom_call" | custom-call | flops 1000000000 | bytes 4194304 | tf_op jit(solution)/shard_map/pallas_call | solution.py:155
  57.4 3.2 %collective-permute-done.13.got_ref = bf16[2,64,768]{2,1,0:T(8,128)(2,1)S(1)} collective-permute-done((bf16[2,64,768]{2,1,0:T(8,128)(2,1)S(1)}, bf16[2,64,768]{2,1,0:T(8,128)(2,1)S(1)}, u32[]{:S(2)}, u32[]{:S(2)}) %collective-permute-start.13) | collective-permute-done | bytes 196640 | tf_op jit(solution)/shard_map/sum_papers/ppermute | solution.py:25
  60.7 0.8 shard_map.120
  61.5 1.3 %collective-permute-start.14 = (bf16[2,64,768]{2,1,0:T(8,128)(2,1)S(1)}, bf16[2,64,768]{2,1,0:T(8,128)(2,1)S(1)}, u32[]{:S(2)}, u32[]{:S(2)}) collective-permute-start(bf16[2,64,768]{2,1,0:T(8,128)(2,1)S(1)} %get-tuple-element.48.refs_0_), channel_id=1, source_target_pairs={{0,4},{4,8},{8,12},{12,0},{1,5},{5,9},{9,13},{13,1},{2,6},{6,10},{... | collective-permute-start | bytes 589832 | tf_op jit(solution)/shard_map/gather_papers/ppermute | solution.py:21
  62.8 3.1 %collective-permute-start.15 = (bf16[2,64,768]{2,1,0:T(8,128)(2,1)S(1)}, bf16[2,64,768]{2,1,0:T(8,128)(2,1)S(1)}, u32[]{:S(2)}, u32[]{:S(2)}) collective-permute-start(bf16[2,64,768]{2,1,0:T(8,128)(2,1)S(1)} %get-tuple-element.48.refs_0_), channel_id=1, source_target_pairs={{0,8},{4,12},{8,0},{12,4},{1,9},{5,13},{9,1},{13,5},{2,10},{6,14},... | collective-permute-start | bytes 589832 | tf_op jit(solution)/shard_map/gather_papers/ppermute | solution.py:21
  65.9 0.6 collective-permute-start.16
  66.5 2.9 %collective-permute-done.14.refs_1_ = bf16[2,64,768]{2,1,0:T(8,128)(2,1)S(1)} collective-permute-done((bf16[2,64,768]{2,1,0:T(8,128)(2,1)S(1)}, bf16[2,64,768]{2,1,0:T(8,128)(2,1)S(1)}, u32[]{:S(2)}, u32[]{:S(2)}) %collective-permute-start.14) | collective-permute-done | bytes 196640 | tf_op jit(solution)/shard_map/gather_papers/ppermute | solution.py:21
  69.4 4.7 %collective-permute-done.15.refs_2_ = bf16[2,64,768]{2,1,0:T(8,128)(2,1)S(1)} collective-permute-done((bf16[2,64,768]{2,1,0:T(8,128)(2,1)S(1)}, bf16[2,64,768]{2,1,0:T(8,128)(2,1)S(1)}, u32[]{:S(2)}, u32[]{:S(2)}) %collective-permute-start.15) | collective-permute-done | bytes 196640 | tf_op jit(solution)/shard_map/gather_papers/ppermute | solution.py:21
  74.1 0.5 collective-permute-start.20
  74.6 0.9 collective-permute-done.19.refs_6_
  75.5 0.3 collective-permute-done.20.refs_7_
  75.8 0.6 shard_map.121
  76.4 1.2 %collective-permute-start.21 = (bf16[4,32,768]{2,1,0:T(8,128)(2,1)S(1)}, bf16[4,32,768]{2,1,0:T(8,128)(2,1)S(1)}, u32[]{:S(2)}, u32[]{:S(2)}) collective-permute-start(bf16[4,32,768]{2,1,0:T(8,128)(2,1)S(1)} %get-tuple-element.53), channel_id=1, source_target_pairs={{0,64},{64,128},{128,192},{192,0},{1,65},{65,129},{129,193},{193,1... | collective-permute-start | bytes 589832 | tf_op jit(solution)/shard_map/sum_authors/ppermute | solution.py:21
  77.6 1.4 %shard_map.122 = (f32[4,64,768]{2,1,0:T(8,128)S(1)}, f32[4,64,768]{2,1,0:T(8,128)S(1)}, f32[4,64,768]{2,1,0:T(8,128)S(1)}) custom-call(bf16[1024,768]{1,0:T(8,128)(2,1)S(1)} %get-tuple-element.50.table_ref, bf16[1024,1024]{1,0:T(8,128)(2,1)S(1)} %shard_map.119.refs_8_.tile_ref), custom_call_target="tpu_custom_call" | custom-call | flops 1000000000 | bytes 4194304 | tf_op jit(solution)/shard_map/pallas_call | solution.py:155
  79.0 2.7 %collective-permute-start.23 = (bf16[4,32,768]{2,1,0:T(8,128)(2,1)S(1)}, bf16[4,32,768]{2,1,0:T(8,128)(2,1)S(1)}, u32[]{:S(2)}, u32[]{:S(2)}) collective-permute-start(bf16[4,32,768]{2,1,0:T(8,128)(2,1)S(1)} %get-tuple-element.55), channel_id=1, source_target_pairs={{0,192},{64,0},{128,64},{192,128},{1,193},{65,1},{129,65},{193,129... | collective-permute-start | bytes 589832 | tf_op jit(solution)/shard_map/sum_authors/ppermute | solution.py:21
  81.7 3.8 %collective-permute-done.21 = bf16[4,32,768]{2,1,0:T(8,128)(2,1)S(1)} collective-permute-done((bf16[4,32,768]{2,1,0:T(8,128)(2,1)S(1)}, bf16[4,32,768]{2,1,0:T(8,128)(2,1)S(1)}, u32[]{:S(2)}, u32[]{:S(2)}) %collective-permute-start.21) | collective-permute-done | bytes 196640 | tf_op jit(solution)/shard_map/sum_authors/ppermute | solution.py:21
  85.5 0.1 collective-permute-start.25
  85.6 0.6 collective-permute-done.23
  86.3 3.8 %collective-permute-start.26 = (bf16[64,768]{1,0:T(8,128)(2,1)S(1)}, bf16[64,768]{1,0:T(8,128)(2,1)S(1)}, u32[]{:S(2)}, u32[]{:S(2)}) collective-permute-start(bf16[64,768]{1,0:T(8,128)(2,1)S(1)} %fusion.13), channel_id=1, source_target_pairs={{0,192},{64,0},{128,64},{192,128},{1,193},{65,1},{129,65},{193,129... | collective-permute-start | bytes 294920 | tf_op jit(solution)/shard_map/sum_authors/ppermute | solution.py:21
  90.1 0.1 collective-permute-start.22
  90.2 3.2 %collective-permute-start.24 = (bf16[3,64,768]{2,1,0:T(8,128)(2,1)S(1)}, bf16[3,64,768]{2,1,0:T(8,128)(2,1)S(1)}, u32[]{:S(2)}, u32[]{:S(2)}) collective-permute-start(bf16[3,64,768]{2,1,0:T(8,128)(2,1)S(1)} %fusion.3), channel_id=1, source_target_pairs={{0,192},{64,0},{128,64},{192,128},{1,193},{65,1},{129,65},{193,129... | collective-permute-start | bytes 884744 | tf_op jit(solution)/shard_map/sum_authors/ppermute | solution.py:21
  93.5 5.1 %collective-permute-start.27 = (bf16[64,768]{1,0:T(8,128)(2,1)S(1)}, bf16[64,768]{1,0:T(8,128)(2,1)S(1)}, u32[]{:S(2)}, u32[]{:S(2)}) collective-permute-start(bf16[64,768]{1,0:T(8,128)(2,1)S(1)} %fusion.12), channel_id=1, source_target_pairs={{0,32},{16,48},{32,0},{48,16},{1,33},{17,49},{33,1},{49,17},{2,34}... | collective-permute-start | bytes 294920 | tf_op jit(solution)/shard_map/sum_authors/ppermute | solution.py:21
  98.5 0.9 collective-permute-done.22
  99.4 0.1 fusion.15
  99.6 3.4 %collective-permute-start.28 = (bf16[64,768]{1,0:T(8,128)(2,1)S(1)}, bf16[64,768]{1,0:T(8,128)(2,1)S(1)}, u32[]{:S(2)}, u32[]{:S(2)}) collective-permute-start(bf16[64,768]{1,0:T(8,128)(2,1)S(1)} %get-tuple-element.63), channel_id=1, source_target_pairs={{0,16},{16,32},{32,48},{48,0},{1,17},{17,33},{33,49},{49,1},{2,18}... | collective-permute-start | bytes 294920 | tf_op jit(solution)/shard_map/sum_authors/ppermute | solution.py:21
  102.9 4.2 %collective-permute-done.28 = bf16[64,768]{1,0:T(8,128)(2,1)S(1)} collective-permute-done((bf16[64,768]{1,0:T(8,128)(2,1)S(1)}, bf16[64,768]{1,0:T(8,128)(2,1)S(1)}, u32[]{:S(2)}, u32[]{:S(2)}) %collective-permute-start.28) | collective-permute-done | bytes 98336 | tf_op jit(solution)/shard_map/sum_authors/ppermute | solution.py:21
  107.1 3.6 %collective-permute-done.29 = bf16[64,768]{1,0:T(8,128)(2,1)S(1)} collective-permute-done((bf16[64,768]{1,0:T(8,128)(2,1)S(1)}, bf16[64,768]{1,0:T(8,128)(2,1)S(1)}, u32[]{:S(2)}, u32[]{:S(2)}) %collective-permute-start.29) | collective-permute-done | bytes 98336 | tf_op jit(solution)/shard_map/sum_authors/ppermute | solution.py:21
  110.7 0.7 fusion.8
  (45 shorter events, 0.5 us)
Async XLA Ops:
  0.6 20.1 %copy-start = (bf16[768,768]{1,0:T(8,128)(2,1)S(1)}, bf16[768,768]{1,0:T(8,128)(2,1)}, u32[]{:S(2)}) copy-start(bf16[768,768]{1,0:T(8,128)(2,1)} %param.12) | copy-start | bytes 3538948
  0.6 15.9 %collective-permute-start = (bf16[64,768]{1,0:T(8,128)(2,1)}, bf16[64,768]{1,0:T(8,128)(2,1)S(1)}, u32[]{:S(2)}, u32[]{:S(2)}) collective-permute-start(bf16[64,768]{1,0:T(8,128)(2,1)} %refs_2_.1), channel_id=1, source_target_pairs={{0,16},{16,32},{32,48},{48,0},{1,17},{17,33},{33,49},{49,1},{2,18}... | collective-permute-start | bytes 294920 | tf_op jit(solution)/shard_map/gather_authors/ppermute | solution.py:21
  5.2 11.4 %collective-permute-start.1 = (bf16[64,768]{1,0:T(8,128)(2,1)}, bf16[64,768]{1,0:T(8,128)(2,1)S(1)}, u32[]{:S(2)}, u32[]{:S(2)}) collective-permute-start(bf16[64,768]{1,0:T(8,128)(2,1)} %refs_2_.1), channel_id=1, source_target_pairs={{0,32},{16,48},{32,0},{48,16},{1,33},{17,49},{33,1},{49,17},{2,34}... | collective-permute-start | bytes 294920 | tf_op jit(solution)/shard_map/gather_authors/ppermute | solution.py:21
  6.2 11.1 %collective-permute-start.2 = (bf16[64,768]{1,0:T(8,128)(2,1)}, bf16[64,768]{1,0:T(8,128)(2,1)S(1)}, u32[]{:S(2)}, u32[]{:S(2)}) collective-permute-start(bf16[64,768]{1,0:T(8,128)(2,1)} %refs_2_.1), channel_id=1, source_target_pairs={{0,48},{16,0},{32,16},{48,32},{1,49},{17,1},{33,17},{49,33},{2,50}... | collective-permute-start | bytes 294920 | tf_op jit(solution)/shard_map/gather_authors/ppermute | solution.py:21
  9.0 8.3 %collective-permute-start.3 = (bf16[64,768]{1,0:T(8,128)(2,1)}, bf16[64,768]{1,0:T(8,128)(2,1)S(1)}, u32[]{:S(2)}, u32[]{:S(2)}) collective-permute-start(bf16[64,768]{1,0:T(8,128)(2,1)} %refs_2_.1), channel_id=1, source_target_pairs={{0,64},{64,128},{128,192},{192,0},{1,65},{65,129},{129,193},{193,1... | collective-permute-start | bytes 294920 | tf_op jit(solution)/shard_map/gather_authors/ppermute | solution.py:21
  10.6 6.7 %collective-permute-start.4 = (bf16[64,768]{1,0:T(8,128)(2,1)}, bf16[64,768]{1,0:T(8,128)(2,1)S(1)}, u32[]{:S(2)}, u32[]{:S(2)}) collective-permute-start(bf16[64,768]{1,0:T(8,128)(2,1)} %refs_2_.1), channel_id=1, source_target_pairs={{0,192},{64,0},{128,64},{192,128},{1,193},{65,1},{129,65},{193,129... | collective-permute-start | bytes 294920 | tf_op jit(solution)/shard_map/gather_authors/ppermute | solution.py:21
  13.7 1.2 %copy-start.3 = (bf16[1,1,32,128,128]{4,3,2,1,0:T(8,128)(2,1)S(1)}, bf16[1,1,32,128,128]{4,3,2,1,0:T(8,128)(2,1)}, u32[]{:S(2)}) copy-start(bf16[1,1,32,128,128]{4,3,2,1,0:T(8,128)(2,1)} %param.19) | copy-start | bytes 3145732
  14.9 5.8 %copy-start.5 = (bf16[64,768]{1,0:T(8,128)(2,1)S(1)}, bf16[64,768]{1,0:T(8,128)(2,1)}, u32[]{:S(2)}) copy-start(bf16[64,768]{1,0:T(8,128)(2,1)} %param.10) | copy-start | bytes 294916
  14.9 6.1 %copy-start.1 = (bf16[2,768,768]{2,1,0:T(8,128)(2,1)S(1)}, bf16[2,768,768]{2,1,0:T(8,128)(2,1)}, u32[]{:S(2)}) copy-start(bf16[2,768,768]{2,1,0:T(8,128)(2,1)} %refs_1_.7) | copy-start | bytes 7077892
  16.6 4.5 %copy-start.4 = (bf16[64,768]{1,0:T(8,128)(2,1)S(1)}, bf16[64,768]{1,0:T(8,128)(2,1)}, u32[]{:S(2)}) copy-start(bf16[64,768]{1,0:T(8,128)(2,1)} %refs_2_.1) | copy-start | bytes 294916
  17.4 9.7 %collective-permute-start.5 = (bf16[192,768]{1,0:T(8,128)(2,1)S(1)}, bf16[192,768]{1,0:T(8,128)(2,1)S(1)}, u32[]{:S(2)}, u32[]{:S(2)}) collective-permute-start(bf16[192,768]{1,0:T(8,128)(2,1)S(1)} %constant_dynamic-update-slice_fusion), channel_id=1, source_target_pairs={{0,64},{64,128},{128,192},{192,0},{1,65},{65,129},{129,193},{193,1... | collective-permute-start | bytes 884744 | tf_op jit(solution)/shard_map/gather_authors/ppermute | solution.py:21
  19.1 10.3 %collective-permute-start.6 = (bf16[192,768]{1,0:T(8,128)(2,1)S(1)}, bf16[192,768]{1,0:T(8,128)(2,1)S(1)}, u32[]{:S(2)}, u32[]{:S(2)}) collective-permute-start(bf16[192,768]{1,0:T(8,128)(2,1)S(1)} %constant_dynamic-update-slice_fusion), channel_id=1, source_target_pairs={{0,192},{64,0},{128,64},{192,128},{1,193},{65,1},{129,65},{193,129... | collective-permute-start | bytes 884744 | tf_op jit(solution)/shard_map/gather_authors/ppermute | solution.py:21
  29.4 7.0 %collective-permute-start.7 = (bf16[128,768]{1,0:T(8,128)(2,1)S(1)}, bf16[128,768]{1,0:T(8,128)(2,1)S(1)}, u32[]{:S(2)}, u32[]{:S(2)}) collective-permute-start(bf16[128,768]{1,0:T(8,128)(2,1)S(1)} %pad_maximum_fusion.1), channel_id=1, source_target_pairs={{0,64},{64,128},{128,192},{192,0},{1,65},{65,129},{129,193},{193,1... | collective-permute-start | bytes 589832 | tf_op jit(solution)/shard_map/forward_authors/ppermute | solution.py:21
  29.8 6.6 %collective-permute-start.8 = (bf16[128,768]{1,0:T(8,128)(2,1)S(1)}, bf16[128,768]{1,0:T(8,128)(2,1)S(1)}, u32[]{:S(2)}, u32[]{:S(2)}) collective-permute-start(bf16[128,768]{1,0:T(8,128)(2,1)S(1)} %slice.71), channel_id=1, source_target_pairs={{0,192},{64,0},{128,64},{192,128},{1,193},{65,1},{129,65},{193,129... | collective-permute-start | bytes 589832 | tf_op jit(solution)/shard_map/forward_authors/ppermute | solution.py:21
  38.2 2.4 %collective-permute-start.9 = (bf16[4,2,64,768]{3,2,1,0:T(8,128)(2,1)S(1)}, bf16[4,2,64,768]{3,2,1,0:T(8,128)(2,1)S(1)}, u32[]{:S(2)}, u32[]{:S(2)}) collective-permute-start(bf16[4,2,64,768]{3,2,1,0:T(8,128)(2,1)S(1)} %get-tuple-element.42), channel_id=1, source_target_pairs={{0,1},{1,0},{2,3},{3,2},{4,5},{5,4},{6,7},{7,6},{8,9},{9,8},{10,11... | collective-permute-start | bytes 2359304 | tf_op jit(solution)/shard_map/sum_papers/ppermute | solution.py:25
  40.8 8.2 %collective-permute-start.10 = (bf16[2,64,768]{2,1,0:T(8,128)(2,1)S(1)}, bf16[2,64,768]{2,1,0:T(8,128)(2,1)S(1)}, u32[]{:S(2)}, u32[]{:S(2)}) collective-permute-start(bf16[2,64,768]{2,1,0:T(8,128)(2,1)S(1)} %get-tuple-element.60), channel_id=1, source_target_pairs={{0,4},{4,8},{8,12},{12,0},{1,5},{5,9},{9,13},{13,1},{2,6},{6,10},{... | collective-permute-start | bytes 589832 | tf_op jit(solution)/shard_map/sum_papers/ppermute | solution.py:21
  42.4 11.9 %collective-permute-start.11 = (bf16[2,64,768]{2,1,0:T(8,128)(2,1)S(1)}, bf16[2,64,768]{2,1,0:T(8,128)(2,1)S(1)}, u32[]{:S(2)}, u32[]{:S(2)}) collective-permute-start(bf16[2,64,768]{2,1,0:T(8,128)(2,1)S(1)} %get-tuple-element.62), channel_id=1, source_target_pairs={{0,8},{4,12},{8,0},{12,4},{1,9},{5,13},{9,1},{13,5},{2,10},{6,14},... | collective-permute-start | bytes 589832 | tf_op jit(solution)/shard_map/sum_papers/ppermute | solution.py:21
  45.1 9.1 %collective-permute-start.12 = (bf16[2,64,768]{2,1,0:T(8,128)(2,1)S(1)}, bf16[2,64,768]{2,1,0:T(8,128)(2,1)S(1)}, u32[]{:S(2)}, u32[]{:S(2)}) collective-permute-start(bf16[2,64,768]{2,1,0:T(8,128)(2,1)S(1)} %get-tuple-element.61), channel_id=1, source_target_pairs={{0,12},{4,0},{8,4},{12,8},{1,13},{5,1},{9,5},{13,9},{2,14},{6,2},{... | collective-permute-start | bytes 589832 | tf_op jit(solution)/shard_map/sum_papers/ppermute | solution.py:21
  54.5 6.2 %copy-start.2 = (bf16[768,768]{1,0:T(8,128)(2,1)S(1)}, bf16[768,768]{1,0:T(8,128)(2,1)}, u32[]{:S(2)}) copy-start(bf16[768,768]{1,0:T(8,128)(2,1)} %w_ref.1) | copy-start | bytes 3538948
  54.5 6.2 %collective-permute-start.13 = (bf16[2,64,768]{2,1,0:T(8,128)(2,1)S(1)}, bf16[2,64,768]{2,1,0:T(8,128)(2,1)S(1)}, u32[]{:S(2)}, u32[]{:S(2)}) collective-permute-start(bf16[2,64,768]{2,1,0:T(8,128)(2,1)S(1)} %convert_element_type.77), channel_id=1, source_target_pairs={{0,2},{2,0},{1,3},{3,1},{4,6},{6,4},{5,7},{7,5},{8,10},{10,8},{9,1... | collective-permute-start | bytes 589832 | tf_op jit(solution)/shard_map/sum_papers/ppermute | solution.py:25
  61.5 7.9 %collective-permute-start.14 = (bf16[2,64,768]{2,1,0:T(8,128)(2,1)S(1)}, bf16[2,64,768]{2,1,0:T(8,128)(2,1)S(1)}, u32[]{:S(2)}, u32[]{:S(2)}) collective-permute-start(bf16[2,64,768]{2,1,0:T(8,128)(2,1)S(1)} %get-tuple-element.48.refs_0_), channel_id=1, source_target_pairs={{0,4},{4,8},{8,12},{12,0},{1,5},{5,9},{9,13},{13,1},{2,6},{6,10},{... | collective-permute-start | bytes 589832 | tf_op jit(solution)/shard_map/gather_papers/ppermute | solution.py:21
  62.8 11.3 %collective-permute-start.15 = (bf16[2,64,768]{2,1,0:T(8,128)(2,1)S(1)}, bf16[2,64,768]{2,1,0:T(8,128)(2,1)S(1)}, u32[]{:S(2)}, u32[]{:S(2)}) collective-permute-start(bf16[2,64,768]{2,1,0:T(8,128)(2,1)S(1)} %get-tuple-element.48.refs_0_), channel_id=1, source_target_pairs={{0,8},{4,12},{8,0},{12,4},{1,9},{5,13},{9,1},{13,5},{2,10},{6,14},... | collective-permute-start | bytes 589832 | tf_op jit(solution)/shard_map/gather_papers/ppermute | solution.py:21
  65.9 8.2 %collective-permute-start.16 = (bf16[2,64,768]{2,1,0:T(8,128)(2,1)S(1)}, bf16[2,64,768]{2,1,0:T(8,128)(2,1)S(1)}, u32[]{:S(2)}, u32[]{:S(2)}) collective-permute-start(bf16[2,64,768]{2,1,0:T(8,128)(2,1)S(1)} %get-tuple-element.48.refs_0_), channel_id=1, source_target_pairs={{0,12},{4,0},{8,4},{12,8},{1,13},{5,1},{9,5},{13,9},{2,14},{6,2},{... | collective-permute-start | bytes 589832 | tf_op jit(solution)/shard_map/gather_papers/ppermute | solution.py:21
  66.5 8.1 %collective-permute-start.17 = (bf16[2,64,768]{2,1,0:T(8,128)(2,1)S(1)}, bf16[2,64,768]{2,1,0:T(8,128)(2,1)S(1)}, u32[]{:S(2)}, u32[]{:S(2)}) collective-permute-start(bf16[2,64,768]{2,1,0:T(8,128)(2,1)S(1)} %get-tuple-element.48.refs_0_), channel_id=1, source_target_pairs={{0,1},{1,0},{2,3},{3,2},{4,5},{5,4},{6,7},{7,6},{8,9},{9,8},{10,11... | collective-permute-start | bytes 589832 | tf_op jit(solution)/shard_map/gather_papers/ppermute | solution.py:25
  69.4 5.2 %collective-permute-start.18 = (bf16[2,64,768]{2,1,0:T(8,128)(2,1)S(1)}, bf16[2,64,768]{2,1,0:T(8,128)(2,1)S(1)}, u32[]{:S(2)}, u32[]{:S(2)}) collective-permute-start(bf16[2,64,768]{2,1,0:T(8,128)(2,1)S(1)} %collective-permute-done.14.refs_1_), channel_id=1, source_target_pairs={{0,1},{1,0},{2,3},{3,2},{4,5},{5,4},{6,7},{7,6},{8,9},{9,8},{10,11... | collective-permute-start | bytes 589832 | tf_op jit(solution)/shard_map/gather_papers/ppermute | solution.py:25
  74.1 1.4 %collective-permute-start.19 = (bf16[2,64,768]{2,1,0:T(8,128)(2,1)S(1)}, bf16[2,64,768]{2,1,0:T(8,128)(2,1)S(1)}, u32[]{:S(2)}, u32[]{:S(2)}) collective-permute-start(bf16[2,64,768]{2,1,0:T(8,128)(2,1)S(1)} %collective-permute-done.15.refs_2_), channel_id=1, source_target_pairs={{0,1},{1,0},{2,3},{3,2},{4,5},{5,4},{6,7},{7,6},{8,9},{9,8},{10,11... | collective-permute-start | bytes 589832 | tf_op jit(solution)/shard_map/gather_papers/ppermute | solution.py:25
  74.1 1.7 %collective-permute-start.20 = (bf16[2,64,768]{2,1,0:T(8,128)(2,1)S(1)}, bf16[2,64,768]{2,1,0:T(8,128)(2,1)S(1)}, u32[]{:S(2)}, u32[]{:S(2)}) collective-permute-start(bf16[2,64,768]{2,1,0:T(8,128)(2,1)S(1)} %collective-permute-done.16.refs_3_), channel_id=1, source_target_pairs={{0,1},{1,0},{2,3},{3,2},{4,5},{5,4},{6,7},{7,6},{8,9},{9,8},{10,11... | collective-permute-start | bytes 589832 | tf_op jit(solution)/shard_map/gather_papers/ppermute | solution.py:25
  76.4 9.1 %collective-permute-start.21 = (bf16[4,32,768]{2,1,0:T(8,128)(2,1)S(1)}, bf16[4,32,768]{2,1,0:T(8,128)(2,1)S(1)}, u32[]{:S(2)}, u32[]{:S(2)}) collective-permute-start(bf16[4,32,768]{2,1,0:T(8,128)(2,1)S(1)} %get-tuple-element.53), channel_id=1, source_target_pairs={{0,64},{64,128},{128,192},{192,0},{1,65},{65,129},{129,193},{193,1... | collective-permute-start | bytes 589832 | tf_op jit(solution)/shard_map/sum_authors/ppermute | solution.py:21
  79.0 7.2 %collective-permute-start.23 = (bf16[4,32,768]{2,1,0:T(8,128)(2,1)S(1)}, bf16[4,32,768]{2,1,0:T(8,128)(2,1)S(1)}, u32[]{:S(2)}, u32[]{:S(2)}) collective-permute-start(bf16[4,32,768]{2,1,0:T(8,128)(2,1)S(1)} %get-tuple-element.55), channel_id=1, source_target_pairs={{0,192},{64,0},{128,64},{192,128},{1,193},{65,1},{129,65},{193,129... | collective-permute-start | bytes 589832 | tf_op jit(solution)/shard_map/sum_authors/ppermute | solution.py:21
  85.5 7.9 %collective-permute-start.25 = (bf16[64,768]{1,0:T(8,128)(2,1)S(1)}, bf16[64,768]{1,0:T(8,128)(2,1)S(1)}, u32[]{:S(2)}, u32[]{:S(2)}) collective-permute-start(bf16[64,768]{1,0:T(8,128)(2,1)S(1)} %fusion.14), channel_id=1, source_target_pairs={{0,64},{64,128},{128,192},{192,0},{1,65},{65,129},{129,193},{193,1... | collective-permute-start | bytes 294920 | tf_op jit(solution)/shard_map/sum_authors/ppermute | solution.py:21
  86.3 7.1 %collective-permute-start.26 = (bf16[64,768]{1,0:T(8,128)(2,1)S(1)}, bf16[64,768]{1,0:T(8,128)(2,1)S(1)}, u32[]{:S(2)}, u32[]{:S(2)}) collective-permute-start(bf16[64,768]{1,0:T(8,128)(2,1)S(1)} %fusion.13), channel_id=1, source_target_pairs={{0,192},{64,0},{128,64},{192,128},{1,193},{65,1},{129,65},{193,129... | collective-permute-start | bytes 294920 | tf_op jit(solution)/shard_map/sum_authors/ppermute | solution.py:21
  90.1 9.3 %collective-permute-start.22 = (bf16[3,64,768]{2,1,0:T(8,128)(2,1)S(1)}, bf16[3,64,768]{2,1,0:T(8,128)(2,1)S(1)}, u32[]{:S(2)}, u32[]{:S(2)}) collective-permute-start(bf16[3,64,768]{2,1,0:T(8,128)(2,1)S(1)} %fusion.4), channel_id=1, source_target_pairs={{0,64},{64,128},{128,192},{192,0},{1,65},{65,129},{129,193},{193,1... | collective-permute-start | bytes 884744 | tf_op jit(solution)/shard_map/sum_authors/ppermute | solution.py:21
  90.2 9.2 %collective-permute-start.24 = (bf16[3,64,768]{2,1,0:T(8,128)(2,1)S(1)}, bf16[3,64,768]{2,1,0:T(8,128)(2,1)S(1)}, u32[]{:S(2)}, u32[]{:S(2)}) collective-permute-start(bf16[3,64,768]{2,1,0:T(8,128)(2,1)S(1)} %fusion.3), channel_id=1, source_target_pairs={{0,192},{64,0},{128,64},{192,128},{1,193},{65,1},{129,65},{193,129... | collective-permute-start | bytes 884744 | tf_op jit(solution)/shard_map/sum_authors/ppermute | solution.py:21
  93.5 9.5 %collective-permute-start.27 = (bf16[64,768]{1,0:T(8,128)(2,1)S(1)}, bf16[64,768]{1,0:T(8,128)(2,1)S(1)}, u32[]{:S(2)}, u32[]{:S(2)}) collective-permute-start(bf16[64,768]{1,0:T(8,128)(2,1)S(1)} %fusion.12), channel_id=1, source_target_pairs={{0,32},{16,48},{32,0},{48,16},{1,33},{17,49},{33,1},{49,17},{2,34}... | collective-permute-start | bytes 294920 | tf_op jit(solution)/shard_map/sum_authors/ppermute | solution.py:21
  99.6 7.5 %collective-permute-start.28 = (bf16[64,768]{1,0:T(8,128)(2,1)S(1)}, bf16[64,768]{1,0:T(8,128)(2,1)S(1)}, u32[]{:S(2)}, u32[]{:S(2)}) collective-permute-start(bf16[64,768]{1,0:T(8,128)(2,1)S(1)} %get-tuple-element.63), channel_id=1, source_target_pairs={{0,16},{16,32},{32,48},{48,0},{1,17},{17,33},{33,49},{49,1},{2,18}... | collective-permute-start | bytes 294920 | tf_op jit(solution)/shard_map/sum_authors/ppermute | solution.py:21
  102.9 7.8 %collective-permute-start.29 = (bf16[64,768]{1,0:T(8,128)(2,1)S(1)}, bf16[64,768]{1,0:T(8,128)(2,1)S(1)}, u32[]{:S(2)}, u32[]{:S(2)}) collective-permute-start(bf16[64,768]{1,0:T(8,128)(2,1)S(1)} %get-tuple-element.64), channel_id=1, source_target_pairs={{0,48},{16,0},{32,16},{48,32},{1,49},{17,1},{33,17},{49,33},{2,50}... | collective-permute-start | bytes 294920 | tf_op jit(solution)/shard_map/sum_authors/ppermute | solution.py:21
